TPU v7x, 512 devices: a whole 4x4x16 slice. The times are simulated.
512 devices in a mesh: row: 32 (over x, y, core), col: 16 (over z).
Axes of the slice: x: 4, y: 4, z: 16, core: 2. Of those that a mesh axis runs over, the one named last changes fastest.
Arguments:
- src_embed: float32 [32, 32768], P(None, 'row'), may hold values from -20 to 20, as said below
- tgt_embed: float32 [32, 24576], P(None, 'col'), may hold values from -20 to 20, as said below
Outputs:
- src_potential: float32 [32768], P('row')
- tgt_potential: float32 [24576], P('col')
- src_image: float32 [32, 32768], P(None, 'row')
- tgt_image: float32 [32, 24576], P(None, 'col')
Inputs may be any that keep to these rules, and one draw needn't show every extreme that they name: `src_embed`: real-valued coordinates of order one to a few units. `tgt_embed`: real-valued coordinates of order one to a few units.
All inputs are finite; a program needn't handle non-finite values.
Results may differ from a plain program's by a relative error of at most 0.0003.
Values sent between devices are 32-bit elements; how exact they have to be, the bound alone decides.
No kernel may reach another device: no remote copies, remote signals or barrier semaphores. Data moves between devices by JAX's collectives and lax.ppermute only.
A program may use at most 64 MiB of HBM per device.

v0:
```python
import math

import jax
import jax.numpy as jnp
from jax import lax
from jax.sharding import PartitionSpec as P

ITERS = 3


epsilon = 1.0


def cost_block(src_embed, sq_src, tgt_embed, sq_tgt, start, width):
    tblock = lax.dynamic_slice_in_dim(tgt_embed, start, width, 1)
    tsq = lax.dynamic_slice_in_dim(sq_tgt, start, width, 0)
    cross = lax.dot_general(
        src_embed,
        tblock,
        (((0,), (0,)), ((), ())),
        precision=lax.Precision.HIGHEST,
        preferred_element_type=jnp.float32,
    )
    return (sq_src[:, None] + tsq[None, :] - 2.0 * cross, tblock)


def local(src_embed, tgt_embed):
    src_rows = src_embed.shape[1]
    tgt_cols = tgt_embed.shape[1]
    width = 512
    blocks = tgt_cols // width
    n_src = src_rows * lax.axis_size("row")
    n_tgt = tgt_cols * lax.axis_size("col")
    sq_src = jnp.sum(src_embed * src_embed, axis=0)
    sq_tgt = jnp.sum(tgt_embed * tgt_embed, axis=0)
    tgt_potential = jnp.zeros((tgt_cols,), jnp.float32)
    src_potential = jnp.zeros((src_rows,), jnp.float32)
    for step in range(ITERS):

        def row_block(index, carry):
            peak, total = carry
            start = index * width
            cost, unused = cost_block(src_embed, sq_src, tgt_embed, sq_tgt, start, width)
            gblock = lax.dynamic_slice_in_dim(tgt_potential, start, width, 0)
            scores = (gblock[None, :] - cost) / epsilon
            new_peak = jnp.maximum(peak, jnp.max(scores, axis=1))
            total = total * jnp.exp(peak - new_peak) + jnp.sum(
                jnp.exp(scores - new_peak[:, None]), axis=1
            )
            return (new_peak, total)

        start_carry = (
            jnp.full((src_rows,), -jnp.inf, jnp.float32),
            jnp.zeros((src_rows,), jnp.float32),
        )
        peak, total = lax.fori_loop(0, blocks, row_block, start_carry)
        whole_peak = lax.pmax(peak, "col")
        total = lax.psum(total * jnp.exp(peak - whole_peak), "col")
        peak = whole_peak
        src_potential = -epsilon * (peak + jnp.log(total) - math.log(n_tgt))

        def col_block(index, carry):
            peaks, totals = carry
            start = index * width
            cost, unused = cost_block(src_embed, sq_src, tgt_embed, sq_tgt, start, width)
            scores = (src_potential[:, None] - cost) / epsilon
            block_peak = jnp.max(scores, axis=0)
            block_total = jnp.sum(jnp.exp(scores - block_peak[None, :]), axis=0)
            peaks = lax.dynamic_update_slice_in_dim(peaks, block_peak, start, 0)
            totals = lax.dynamic_update_slice_in_dim(totals, block_total, start, 0)
            return (peaks, totals)

        start_carry = (jnp.zeros((tgt_cols,), jnp.float32), jnp.zeros((tgt_cols,), jnp.float32))
        peak, total = lax.fori_loop(0, blocks, col_block, start_carry)
        whole_peak = lax.pmax(peak, "row")
        total = lax.psum(total * jnp.exp(peak - whole_peak), "row")
        peak = whole_peak
        tgt_potential = -epsilon * (peak + jnp.log(total) - math.log(n_src))

    def map_block(index, carry):
        peak, total, moved, col_peaks, col_totals, col_moved = carry
        start = index * width
        cost, tblock = cost_block(src_embed, sq_src, tgt_embed, sq_tgt, start, width)
        gblock = lax.dynamic_slice_in_dim(tgt_potential, start, width, 0)
        scores = (gblock[None, :] - cost) / epsilon
        new_peak = jnp.maximum(peak, jnp.max(scores, axis=1))
        weights = jnp.exp(scores - new_peak[:, None])
        factor = jnp.exp(peak - new_peak)
        total = total * factor + jnp.sum(weights, axis=1)
        moved = moved * factor[None, :] + lax.dot_general(
            tblock,
            weights,
            (((1,), (1,)), ((), ())),
            precision=lax.Precision.HIGHEST,
            preferred_element_type=jnp.float32,
        )
        col_scores = (src_potential[:, None] - cost) / epsilon
        block_peak = jnp.max(col_scores, axis=0)
        col_weights = jnp.exp(col_scores - block_peak[None, :])
        block_total = jnp.sum(col_weights, axis=0)
        block_moved = jnp.dot(
            src_embed,
            col_weights,
            precision=lax.Precision.HIGHEST,
            preferred_element_type=jnp.float32,
        )
        col_peaks = lax.dynamic_update_slice_in_dim(col_peaks, block_peak, start, 0)
        col_totals = lax.dynamic_update_slice_in_dim(col_totals, block_total, start, 0)
        col_moved = lax.dynamic_update_slice_in_dim(col_moved, block_moved, start, 1)
        return (new_peak, total, moved, col_peaks, col_totals, col_moved)

    dims = src_embed.shape[0]
    start_carry = (
        jnp.full((src_rows,), -jnp.inf, jnp.float32),
        jnp.zeros((src_rows,), jnp.float32),
        jnp.zeros((dims, src_rows), jnp.float32),
        jnp.zeros((tgt_cols,), jnp.float32),
        jnp.zeros((tgt_cols,), jnp.float32),
        jnp.zeros((dims, tgt_cols), jnp.float32),
    )
    peak, total, moved, col_peak, col_total, col_moved = lax.fori_loop(
        0, blocks, map_block, start_carry
    )
    whole_peak = lax.pmax(peak, "col")
    factor = jnp.exp(peak - whole_peak)
    total, moved = lax.psum((total * factor, moved * factor[None, :]), "col")
    whole_col = lax.pmax(col_peak, "row")
    col_factor = jnp.exp(col_peak - whole_col)
    col_total, col_moved = lax.psum(
        (col_total * col_factor, col_moved * col_factor[None, :]), "row"
    )
    src_image = moved / total[None, :]
    tgt_image = col_moved / col_total[None, :]
    return (src_potential, tgt_potential, src_image, tgt_image)


def solution(mesh):
    in_specs = (P(None, "row"), P(None, "col"))
    out_specs = (P("row"), P("col"), P(None, "row"), P(None, "col"))
    return jax.shard_map(local, mesh=mesh, in_specs=in_specs, out_specs=out_specs, check_vma=False)
```

profile of v0, /device:TPU:6, one launch (start us, length us, event | category | flops | bytes accessed | tf_op | source)
XLA Modules:
  0.0 999.5 jit_solution(11640935919874107858)
XLA Ops:
  9.2 10.6 %while.120 = (s32[]{:T(128)}, f32[1024]{0:T(1024)S(1)}, f32[1024]{0:T(1024)S(1)}, f32[1024]{0:T(1024)S(1)}, f32[1536]{0:T(1024)S(1)}, /*index=5*/f32[32,1536]{1,...) while((s32[]{:T(128)}, f32[1024]{0:T(1024)S(1)}, ...), condition=%wide.region_5.0_spmd.clone, body=%wide.region_2.0_spmd.clone.sunk | while | flops 205001728 | bytes 4454582 | solution.py:56
  9.3 3.1 fusion.82
  12.8 3.1 fusion.82
  16.4 3.1 fusion.82
  19.8 36.6 %pmax.56 = f32[1024]{0:T(1024)S(1)} all-reduce(f32[1024]{0:T(1024)S(1)} %get-tuple-element.1048), channel_id=1, replica_groups=mesh['row'=32,'col'=16] {'col'}, use_global_device_ids=true, to_apply=%region_6.0 | all-reduce | flops 1024 | bytes 8192 | tf_op jit(solution)/shard_map/pmax | solution.py:57
  56.4 27.0 %psum.70 = f32[1024]{0:T(1024)S(1)} all-reduce(f32[1024]{0:T(1024)S(1)} %exponential_multiply_fusion.5), channel_id=1, replica_groups=mesh['row'=32,'col'=16] {'col'}, use_global_device_ids=true, to_apply=%region_7.0 | all-reduce | flops 1024 | bytes 8192 | tf_op jit(solution)/shard_map/psum | solution.py:58
  83.4 12.8 %while.117 = (s32[]{:T(128)}, f32[1536]{0:T(1024)S(1)}, f32[1536]{0:T(1024)S(1)}, f32[1024]{0:T(1024)S(1)}, f32[1024]{0:T(1024)S(1)}, /*index=5*/f32[1536]{0:T(1...) while((s32[]{:T(128)}, f32[1536]{0:T(1024)S(1)}, ...), condition=%wide.region_11.0_spmd, body=%wide.region_8.0_spmd.sunk | while | flops 204995584 | bytes 4419763 | solution.py:74
  83.5 3.2 fusion.76
  87.8 3.2 fusion.76
  92.1 3.2 fusion.76
  96.3 54.0 %pmax.57 = f32[1536]{0:T(1024)S(1)} all-reduce(f32[1536]{0:T(1024)S(1)} %get-tuple-element.1050), channel_id=1, replica_groups=mesh['row'=32,'col'=16] {'row'}, use_global_device_ids=true, to_apply=%region_12.0 | all-reduce | flops 1536 | bytes 12288 | tf_op jit(solution)/shard_map/pmax | solution.py:75
  150.3 55.2 %psum.71 = f32[1536]{0:T(1024)S(1)} all-reduce(f32[1536]{0:T(1024)S(1)} %exponential_multiply_fusion.2), channel_id=1, replica_groups=mesh['row'=32,'col'=16] {'row'}, use_global_device_ids=true, to_apply=%region_13.0 | all-reduce | flops 1536 | bytes 12288 | tf_op jit(solution)/shard_map/psum | solution.py:76
  205.5 10.9 %while.121 = (s32[]{:T(128)}, f32[1024]{0:T(1024)S(1)}, f32[1024]{0:T(1024)S(1)}, f32[1536]{0:T(1024)S(1)}, f32[1024]{0:T(1024)S(1)}, /*index=5*/f32[1536]{0:T(1...) while((s32[]{:T(128)}, f32[1024]{0:T(1024)S(1)}, ...), condition=%wide.region_17.0_spmd.clone, body=%wide.region_14.0_spmd.clone.sunk | while | flops 205001728 | bytes 4460738 | solution.py:56
  205.7 3.1 fusion.85
  209.3 3.1 fusion.85
  213.0 3.1 fusion.85
  216.4 29.1 %pmax.58 = f32[1024]{0:T(1024)S(1)} all-reduce(f32[1024]{0:T(1024)S(1)} %get-tuple-element.1052), channel_id=1, replica_groups=mesh['row'=32,'col'=16] {'col'}, use_global_device_ids=true, to_apply=%region_18.0 | all-reduce | flops 1024 | bytes 8192 | tf_op jit(solution)/shard_map/pmax | solution.py:57
  245.5 27.0 %psum.72 = f32[1024]{0:T(1024)S(1)} all-reduce(f32[1024]{0:T(1024)S(1)} %exponential_multiply_fusion.4), channel_id=1, replica_groups=mesh['row'=32,'col'=16] {'col'}, use_global_device_ids=true, to_apply=%region_19.0 | all-reduce | flops 1024 | bytes 8192 | tf_op jit(solution)/shard_map/psum | solution.py:58
  272.6 12.8 %while.118 = (s32[]{:T(128)}, f32[1536]{0:T(1024)S(1)}, f32[1536]{0:T(1024)S(1)}, f32[1024]{0:T(1024)S(1)}, f32[1024]{0:T(1024)S(1)}, /*index=5*/f32[1536]{0:T(1...) while((s32[]{:T(128)}, f32[1536]{0:T(1024)S(1)}, ...), condition=%wide.region_23.0_spmd, body=%wide.region_20.0_spmd.sunk | while | flops 204995584 | bytes 4419763 | solution.py:74
  272.7 3.2 fusion.78
  276.9 3.2 fusion.78
  281.2 3.2 fusion.78
  285.4 63.7 %pmax.59 = f32[1536]{0:T(1024)S(1)} all-reduce(f32[1536]{0:T(1024)S(1)} %get-tuple-element.1054), channel_id=1, replica_groups=mesh['row'=32,'col'=16] {'row'}, use_global_device_ids=true, to_apply=%region_24.0 | all-reduce | flops 1536 | bytes 12288 | tf_op jit(solution)/shard_map/pmax | solution.py:75
  349.1 63.9 %psum.73 = f32[1536]{0:T(1024)S(1)} all-reduce(f32[1536]{0:T(1024)S(1)} %exponential_multiply_fusion.1), channel_id=1, replica_groups=mesh['row'=32,'col'=16] {'row'}, use_global_device_ids=true, to_apply=%region_25.0 | all-reduce | flops 1536 | bytes 12288 | tf_op jit(solution)/shard_map/psum | solution.py:76
  413.0 10.9 %while.122 = (s32[]{:T(128)}, f32[1024]{0:T(1024)S(1)}, f32[1024]{0:T(1024)S(1)}, f32[1536]{0:T(1024)S(1)}, f32[1024]{0:T(1024)S(1)}, /*index=5*/f32[1536]{0:T(1...) while((s32[]{:T(128)}, f32[1024]{0:T(1024)S(1)}, ...), condition=%wide.region_29.0_spmd.clone, body=%wide.region_26.0_spmd.clone.sunk | while | flops 205001728 | bytes 4460738 | solution.py:56
  413.2 3.1 fusion.88
  416.8 3.1 fusion.88
  420.4 3.1 fusion.88
  423.9 29.0 %pmax.60 = f32[1024]{0:T(1024)S(1)} all-reduce(f32[1024]{0:T(1024)S(1)} %get-tuple-element.1056), channel_id=1, replica_groups=mesh['row'=32,'col'=16] {'col'}, use_global_device_ids=true, to_apply=%region_30.0 | all-reduce | flops 1024 | bytes 8192 | tf_op jit(solution)/shard_map/pmax | solution.py:57
  452.9 27.1 %psum.74 = f32[1024]{0:T(1024)S(1)} all-reduce(f32[1024]{0:T(1024)S(1)} %exponential_multiply_fusion.3), channel_id=1, replica_groups=mesh['row'=32,'col'=16] {'col'}, use_global_device_ids=true, to_apply=%region_31.0 | all-reduce | flops 1024 | bytes 8192 | tf_op jit(solution)/shard_map/psum | solution.py:58
  480.0 12.8 %while.119 = (s32[]{:T(128)}, f32[1536]{0:T(1024)S(1)}, f32[1536]{0:T(1024)S(1)}, f32[1024]{0:T(1024)S(1)}, f32[1024]{0:T(1024)S(1)}, /*index=5*/f32[1536]{0:T(1...) while((s32[]{:T(128)}, f32[1536]{0:T(1024)S(1)}, ...), condition=%wide.region_35.0_spmd, body=%wide.region_32.0_spmd.sunk | while | flops 204995584 | bytes 4419763 | solution.py:74
  480.1 3.2 fusion.80
  484.4 3.2 fusion.80
  488.7 3.2 fusion.80
  492.8 63.7 %pmax.61 = f32[1536]{0:T(1024)S(1)} all-reduce(f32[1536]{0:T(1024)S(1)} %get-tuple-element.1058), channel_id=1, replica_groups=mesh['row'=32,'col'=16] {'row'}, use_global_device_ids=true, to_apply=%region_36.0 | all-reduce | flops 1536 | bytes 12288 | tf_op jit(solution)/shard_map/pmax | solution.py:75
  556.5 63.7 %psum.75 = f32[1536]{0:T(1024)S(1)} all-reduce(f32[1536]{0:T(1024)S(1)} %exponential_multiply_fusion), channel_id=1, replica_groups=mesh['row'=32,'col'=16] {'row'}, use_global_device_ids=true, to_apply=%region_37.0 | all-reduce | flops 1536 | bytes 12288 | tf_op jit(solution)/shard_map/psum | solution.py:76
  620.3 29.3 %while.123 = (s32[]{:T(128)}, f32[1024]{0:T(1024)S(1)}, f32[1024]{0:T(1024)S(1)}, f32[32,1024]{1,0:T(8,128)S(1)}, f32[1536]{0:T(1024)S(1)}, /*index=5*/f32[1536]...) while((s32[]{:T(128)}, f32[1024]{0:T(1024)S(1)}, ...), condition=%wide.region_43.0_spmd.clone, body=%wide.region_38.0_spmd.clone.sunk | while | flops 612995072 | bytes 9748759 | solution.py:121
  620.5 3.3 subtract_reduce_fusion.3
  625.2 2.5 fusion.95
  630.3 3.3 subtract_reduce_fusion.3
  640.0 3.3 subtract_reduce_fusion.3
  644.7 2.5 fusion.95
  649.6 63.7 %pmax.63 = f32[1536]{0:T(1024)S(1)} all-reduce(f32[1536]{0:T(1024)S(1)} %get-tuple-element.1064), channel_id=1, replica_groups=mesh['row'=32,'col'=16] {'row'}, use_global_device_ids=true, to_apply=%region_47.0 | all-reduce | flops 1536 | bytes 12288 | tf_op jit(solution)/shard_map/pmax | solution.py:127
  714.1 29.1 %pmax.62 = f32[1024]{0:T(1024)S(1)} all-reduce(f32[1024]{0:T(1024)S(1)} %get-tuple-element.1061), channel_id=1, replica_groups=mesh['row'=32,'col'=16] {'col'}, use_global_device_ids=true, to_apply=%region_44.0 | all-reduce | flops 1024 | bytes 8192 | tf_op jit(solution)/shard_map/pmax | solution.py:124
  743.9 27.0 %psum.77 = f32[1024]{0:T(1024)S(1)} all-reduce(f32[1024]{0:T(1024)S(1)} %get-tuple-element.1314), channel_id=1, replica_groups=mesh['row'=32,'col'=16] {'col'}, use_global_device_ids=true, to_apply=%region_46.0 | all-reduce | flops 1024 | bytes 8192 | tf_op jit(solution)/shard_map/psum | solution.py:126
  770.9 63.7 %psum.79 = f32[1536]{0:T(1024)S(1)} all-reduce(f32[1536]{0:T(1024)S(1)} %get-tuple-element.1312), channel_id=1, replica_groups=mesh['row'=32,'col'=16] {'row'}, use_global_device_ids=true, to_apply=%region_49.0 | all-reduce | flops 1536 | bytes 12288 | tf_op jit(solution)/shard_map/psum | solution.py:129
  834.6 19.2 %all-reduce.5.cloned.1.call-done = f32[32,1536]{1,0:T(8,128)} async-done(((f32[32,1536]{1,0:T(8,128)}), f32[32,1536]{1,0:T(8,128)}) %all-reduce.5.cloned.1.call-update) | async-done | bytes 196624 | tf_op jit(solution)/shard_map/psum | solution.py:129
  855.5 135.6 %all-reduce.3.cloned.1.call-done = f32[32,1024]{1,0:T(8,128)} async-done(((f32[32,1024]{1,0:T(8,128)}), f32[32,1024]{1,0:T(8,128)}) %all-reduce.3.cloned.1.call-update) | async-done | bytes 131088 | tf_op jit(solution)/shard_map/psum | solution.py:126
  (167 shorter events, 35.3 us)
Async XLA Ops:
  7.2 846.7 %all-reduce.5.cloned.1.call-start = ((), (), s32[]{:S(2)}) async-start(), calls=%async_computation.1 | async-start | bytes 393216 | tf_op jit(solution)/shard_map/psum | solution.py:129
  623.7 4.0 copy-start
  633.5 4.0 copy-start
  643.3 3.9 copy-start
  649.6 343.0 %copy-start.1 = (f32[1024]{0:T(1024)}, f32[1024]{0:T(1024)S(1)}, u32[]{:S(2)}) copy-start(f32[1024]{0:T(1024)S(1)} %get-tuple-element.2023) | copy-start | bytes 12292
  649.6 343.0 %copy-start.2 = (f32[1536]{0:T(1024)}, f32[1536]{0:T(1024)S(1)}, u32[]{:S(2)}) copy-start(f32[1536]{0:T(1024)S(1)} %get-tuple-element.2026) | copy-start | bytes 18436
  714.1 277.0 %all-reduce.3.cloned.1.call-start = ((), (), s32[]{:S(2)}) async-start(), calls=%async_computation | async-start | bytes 262144 | tf_op jit(solution)/shard_map/psum | solution.py:126
Sparse Core Ops, SparseCore 0:
  714.2 139.6 all-reduce.4
  856.8 134.1 all-reduce.2
where the time goes:
time: 1000 us; the launch traced here: 999 us
  blocking collectives  723 us (72%)
  waiting for transfers between devices  155 us (16%)
  matrix products  80.5 us (8%)
  other arithmetic  17.1 us (2%)
  between operations  14.3 us (1%)
    psum x3, blocking collectives, local(): total = lax.psum(total * jnp.exp(peak - whole_peak), 'row')  183 us
    pmax x3, blocking collectives, local(): whole_peak = lax.pmax(peak, 'row')  181 us
    psum x1, waiting for transfers between devices, local(): total, moved = lax.psum((total * factor, moved * factor[None, :]), 'col')  136 us
    pmax x4, blocking collectives, local(): whole_peak = lax.pmax(peak, 'col')  124 us
    psum x3, blocking collectives, local(): total = lax.psum(total * jnp.exp(peak - whole_peak), 'col')  81.1 us
    dot_general x21, matrix products, cost_block(): lax.dot_general(src_embed, tblock, (((0,), (0,)), ((), ())), precision=la...  65.9 us
    pmax x1, blocking collectives, local(): whole_col = lax.pmax(col_peak, 'row')  63.7 us
    psum x1, blocking collectives, local(): lax.psum((col_total * col_factor, col_moved * col_factor[None, :]), 'row')  63.7 us
  transfers between devices with their start and end apart: 2, of which 2 were waited for; matrix products, arithmetic and copies ran while one was open for 0% of the time, Pallas kernels for 0%

commit v1 on v0

v1 whole, which is shorter than its diff:
```python
import functools
import math

import jax
import jax.numpy as jnp
from jax import lax
from jax.experimental import pallas as pl
from jax.experimental.pallas import tpu as pltpu
from jax.sharding import PartitionSpec as P

ITERS = 3
LOG2E = math.log2(math.e)
LN2 = math.log(2.0)
DEPTH = 256
HALF = 128
TILE = 256
CHUNK = 256
PROBE = 256
LOW, HIGH = 2.0**-90, 2.0**100
BF, F32 = jnp.bfloat16, jnp.float32
VMEM = pl.BlockSpec(memory_space=pltpu.VMEM)


def rounded(v):
    return v.astype(BF).astype(F32)


def split(v):
    a = rounded(v)
    b = rounded(v - a)
    return a, b, rounded(v - a - b)


def as_row(v):
    return jnp.concatenate([v[r : r + 1, :] for r in range(v.shape[0])], axis=1)


def as_dense(v):
    return jnp.concatenate(
        [v[:, HALF * r : HALF * (r + 1)] for r in range(v.shape[1] // HALF)], axis=0
    )


def potential_rows(v, first):
    a, b, c = split(v)
    row = lax.broadcasted_iota(jnp.int32, (8, v.shape[1]), 0)
    ones = jnp.where((row < 6) & ((row < first) | (row >= first + 3)), 1.0, 0.0).astype(F32)
    out = jnp.where(row == first, a, ones)
    out = jnp.where(row == first + 1, b, out)
    return jnp.where(row == first + 2, c, out)


def row_block(v, first):
    rows = potential_rows(v, first)
    return jnp.concatenate([rows, jnp.zeros_like(rows)], axis=0).astype(BF)


def operand(v, order1, order2, first):
    pieces = split(v)
    n = v.shape[1]
    zero = jnp.zeros((32, n), F32)
    rows = potential_rows(jnp.zeros((1, n), F32), first)
    return jnp.concatenate(
        [pieces[k] for k in order1]
        + [zero, rows, zero[:8]]
        + [pieces[k] for k in order2]
        + [zero[:16]],
        axis=0,
    )


SRC = dict(order1=(0, 0, 1), order2=(0, 2, 1), first=0)
TGT = dict(order1=(0, 1, 0), order2=(2, 0, 1), first=3)


def column_half(v, first, static_ref):
    rows = potential_rows(v, first)
    n = v.shape[1]
    keep = lax.broadcasted_iota(jnp.int32, (8, n), 0)
    rows = jnp.where((keep >= first) & (keep < first + 3), rows, 0.0)
    wide = jnp.concatenate([rows, jnp.zeros((HALF - 8, n), F32)], axis=0)
    return static_ref[:, HALF:] + jnp.transpose(wide).astype(BF)


def tile_of(row_ref, block, start):
    cols = pl.ds(start, TILE)
    return jnp.concatenate(
        [row_ref[:HALF, cols], block, row_ref[HALF + 16 :, cols]], axis=0
    )


def scores(col_ref, half_ref, start, rhs):
    rows = pl.ds(start, CHUNK)
    lhs = jnp.concatenate([col_ref[rows, :HALF], half_ref[rows, :]], axis=1)
    return jnp.dot(lhs, rhs, preferred_element_type=F32)


def sums(col_ref, half_ref, row_ref, shift_ref, s_ref, first):
    count, n = col_ref.shape[0], row_ref.shape[1]
    for t in range(n // TILE):
        cols = slice(t * TILE, (t + 1) * TILE)
        rhs = tile_of(row_ref, row_block(shift_ref[:, cols], first), t * TILE)
        acc = jnp.zeros((8, TILE), F32)
        for c in range(count // CHUNK):
            s = scores(col_ref, half_ref, c * CHUNK, rhs)
            acc += jnp.sum(jnp.exp2(s).reshape(CHUNK // 8, 8, TILE), axis=0)
        s_ref[:, cols] = jnp.sum(acc, axis=0, keepdims=True)


def peaks(col_ref, half_ref, row_ref, shift_ref, first, count):
    n = row_ref.shape[1]

    @pl.loop(0, n // TILE)
    def _(t):
        start = pl.multiple_of(t * TILE, TILE)
        rhs = tile_of(row_ref, row_block(jnp.zeros((1, TILE), F32), first), start)

        def step(c, acc):
            s = scores(col_ref, half_ref, pl.multiple_of(c * CHUNK, CHUNK), rhs)
            return jnp.maximum(acc, jnp.max(s.reshape(CHUNK // 8, 8, TILE), axis=0))

        acc = lax.fori_loop(0, count // CHUNK, step, jnp.full((8, TILE), -jnp.inf, F32))
        shift_ref[:, pl.ds(start, TILE)] = -jnp.max(acc, axis=0, keepdims=True)


def outside(s):
    return jnp.any(jnp.logical_not((s > LOW) & (s < HIGH)))


def local_lse(col_ref, half_ref, row_ref, shift_ref, s_ref, first):
    args = (col_ref, half_ref, row_ref, shift_ref)
    sums(*args, s_ref, first)

    @pl.when(outside(s_ref[...]))
    def _():
        peaks(*args, first, col_ref.shape[0])
        sums(*args, s_ref, first)

    return jnp.log2(s_ref[...]) - shift_ref[...]


def joined(parts):
    peak = jnp.max(parts, axis=0)
    return peak + jnp.log2(jnp.sum(jnp.exp2(parts - peak[None]), axis=0))


def send_all(out_ref, v):
    out_ref[...] = jnp.broadcast_to(v[None], out_ref.shape)


def start_kernel(
    x_ref, y_ref,
    xt_ref, yt_ref, xr_ref, yr_ref, xsq_ref, ysq_ref, out_ref,
    half_ref, shift_ref, s_ref,
):
    x, y = x_ref[...], y_ref[...]
    xr = operand(x * (2.0 * LOG2E), **SRC)
    yr = operand(y, **TGT)
    xr_ref[...] = xr.astype(BF)
    yr_ref[...] = yr.astype(BF)
    xt_ref[...] = jnp.transpose(xr).astype(BF)
    yt_ref[...] = jnp.transpose(yr).astype(BF)
    xsq_ref[...] = as_dense(jnp.sum(x * x, axis=0, keepdims=True))
    ysq = jnp.sum(y * y, axis=0, keepdims=True)
    ysq_ref[...] = as_dense(ysq)
    half_ref[...] = column_half(ysq * -LOG2E, 3, yt_ref)
    args = (yt_ref, half_ref, xr_ref, shift_ref)
    peaks(*args, 0, PROBE)
    send_all(out_ref, as_dense(local_lse(*args, s_ref, 0)))


def lse_kernel(
    total, col_first, row_first,
    parts_ref, col_ref, row_ref, old_ref,
    new_ref, out_ref,
    half_ref, shift_ref, s_ref,
):
    new = math.log2(total) - joined(parts_ref[...])
    new_ref[...] = new
    half_ref[...] = column_half(as_row(new), col_first, col_ref)
    args = (col_ref, half_ref, row_ref, shift_ref)
    if old_ref is None:
        peaks(*args, row_first, PROBE)
    else:
        shift_ref[...] = as_row(old_ref[...])
    send_all(out_ref, as_dense(local_lse(*args, s_ref, row_first)))


def maps(col_ref, half_ref, row_ref, block_ref, values_ref, moved_ref, exact):
    n = row_ref.shape[1]

    def chunk(c, unused):
        start = pl.multiple_of(c * CHUNK, CHUNK)
        if exact:
            peak = jnp.full((CHUNK, 1), -jnp.inf, F32)
            for t in range(n // TILE):
                cols = slice(t * TILE, (t + 1) * TILE)
                rhs = tile_of(row_ref, block_ref[:, cols], t * TILE)
                s = scores(col_ref, half_ref, start, rhs)
                peak = jnp.maximum(peak, jnp.max(s, axis=1, keepdims=True))
        total = jnp.zeros((CHUNK, HALF), F32)
        for t in range(n // TILE):
            cols = slice(t * TILE, (t + 1) * TILE)
            rhs = tile_of(row_ref, block_ref[:, cols], t * TILE)
            s = scores(col_ref, half_ref, start, rhs)
            w = jnp.exp2(s - peak) if exact else jnp.exp2(s)
            high = w.astype(BF)
            low = (w - high.astype(F32)).astype(BF)
            values = values_ref[cols, HALF:]
            total += jnp.dot(high, values, preferred_element_type=F32)
            total += jnp.dot(low, values, preferred_element_type=F32)
        if exact:
            lane = lax.broadcasted_iota(jnp.int32, (CHUNK, HALF), 1)
            total = jnp.where(lane == HALF - 1, peak, total)
        moved_ref[pl.ds(start, CHUNK), :] = total
        return unused

    chunks = col_ref.shape[0] // CHUNK
    if exact:
        lax.fori_loop(0, chunks, chunk, 0)
    else:
        for c in range(chunks):
            chunk(c, 0)


def image_kernel(
    total, col_first, row_first, dims, scale,
    parts_ref, col_ref, row_ref, values_ref, old_ref,
    *refs,
):
    new_ref, out_ref = refs[:2]
    half_ref, block_ref, moved_ref, across_ref, shift_ref, image_ref = refs[-6:]
    rows = old_ref.shape[0]
    if len(refs) > 8:
        share_ref = refs[2]
        parts = parts_ref[...]
        logs = parts[:, : new_ref.shape[0]]
        peak = jnp.max(logs, axis=0)
        weights = jnp.exp2(logs - peak[None])
        sum_w = jnp.sum(weights, axis=0)
        new = math.log2(total) - (peak + jnp.log2(sum_w))
        send_all(share_ref, share(parts, weights, sum_w))
    else:
        new = math.log2(total) - joined(parts_ref[...])
    new_ref[...] = new
    block_ref[...] = row_block(as_row(new), row_first)
    shift = as_row(old_ref[...])
    shift_ref[...] = shift
    half_ref[...] = column_half(shift, col_first, col_ref)
    args = (col_ref, half_ref, row_ref, block_ref, values_ref, moved_ref)
    maps(*args, False)
    across_ref[...] = jnp.transpose(moved_ref[...])
    one = 3 - row_first
    one = {0: 3, 3: 0}[row_first]

    @pl.when(outside(across_ref[one : one + 1, :]))
    def _():
        half_ref[...] = col_ref[:, HALF:]
        maps(*args, True)
        across_ref[...] = jnp.transpose(moved_ref[...])
        shift_ref[...] = jnp.zeros_like(shift)

    s = across_ref[one : one + 1, :]
    log = jnp.log2(s) + across_ref[HALF - 1 :, :] - shift_ref[...]
    image = across_ref[16:48, :] + across_ref[48:80, :] + across_ref[80:112, :]
    image = image * (scale / s)
    for r in range(rows):
        image_ref[:, r, :] = image[:, HALF * r : HALF * (r + 1)]
    n = out_ref.shape[0]
    out_ref[:, :rows, :] = jnp.broadcast_to(as_dense(log)[None], (n, rows, HALF))
    for d in range(dims):
        for k in range(n):
            out_ref[k, rows * (d + 1) : rows * (d + 2), :] = image_ref[k * dims + d]


def share(parts, weights, sum_w):
    rows = weights.shape[1]
    out = []
    for d in range(parts.shape[1] // rows - 1):
        part = parts[:, rows * (d + 1) : rows * (d + 2)]
        out.append(jnp.sum(part * weights, axis=0) / sum_w)
    return jnp.concatenate(out, axis=0)


def share_kernel(rows, parts_ref, out_ref):
    parts = parts_ref[...]
    logs = parts[:, :rows]
    weights = jnp.exp2(logs - jnp.max(logs, axis=0)[None])
    send_all(out_ref, share(parts, weights, jnp.sum(weights, axis=0)))


def end_kernel(
    e_ref, h_ref, xsq_ref, ysq_ref, src_ref, tgt_ref, f_ref, g_ref, si_ref, ti_ref
):
    f_ref[...] = LN2 * e_ref[...] + xsq_ref[...]
    g_ref[...] = LN2 * h_ref[...] + ysq_ref[...]
    for parts_ref, out_ref in ((src_ref, si_ref), (tgt_ref, ti_ref)):
        for r in range(parts_ref.shape[1]):
            out_ref[:, HALF * r : HALF * (r + 1)] = parts_ref[:, r, :]


def shape(*dims, dtype=F32):
    return jax.ShapeDtypeStruct(dims, dtype)


def call(kernel, ins, outs, scratch=(), name=None):
    return pl.pallas_call(
        kernel,
        out_shape=outs,
        in_specs=[VMEM] * len(ins),
        out_specs=jax.tree.map(lambda _: VMEM, outs),
        scratch_shapes=list(scratch),
        compiler_params=pltpu.CompilerParams(vmem_limit_bytes=32 * 2**20),
        name=name,
    )(*ins)


def local(x, y):
    ns, nt = x.shape[1], y.shape[1]
    n_row, n_col = lax.axis_size("row"), lax.axis_size("col")
    rs, rt = ns // HALF, nt // HALF
    all_src, all_tgt = ns * n_row, nt * n_col
    dim_src, dim_tgt = x.shape[0] // n_col, x.shape[0] // n_row

    def scratch(m, n):
        return (pltpu.VMEM((m, HALF), BF), pltpu.VMEM((1, n), F32), pltpu.VMEM((1, n), F32))

    def over(axis, v):
        return lax.all_to_all(v, axis, 0, 0)

    xt, yt, xr, yr, xsq, ysq, parts = call(
        start_kernel,
        (x, y),
        (
            shape(ns, DEPTH, dtype=BF),
            shape(nt, DEPTH, dtype=BF),
            shape(DEPTH, ns, dtype=BF),
            shape(DEPTH, nt, dtype=BF),
            shape(rs, HALF),
            shape(rt, HALF),
            shape(n_col, rs, HALF),
        ),
        scratch(nt, ns),
        name="start",
    )
    h = None
    for step in range(ITERS - 1):
        parts = over("col", parts)
        kernel = functools.partial(lse_kernel, all_tgt, 0, 3)
        ins = (parts, xt, yr)
        if h is None:
            base = kernel
            kernel = lambda p, c, r, *refs: base(p, c, r, None, *refs)
        else:
            ins += (h,)
        e, parts = call(
            kernel, ins, (shape(rs, HALF), shape(n_row, rt, HALF)), scratch(ns, nt), name="cols"
        )
        parts = over("row", parts)
        h, parts = call(
            functools.partial(lse_kernel, all_src, 3, 0),
            (parts, yt, xr, e),
            (shape(rt, HALF), shape(n_col, rs, HALF)),
            scratch(nt, ns),
            name="rows",
        )

    def image_scratch(m, n):
        return (
            pltpu.VMEM((m, HALF), BF),
            pltpu.VMEM((16, n), BF),
            pltpu.VMEM((m, HALF), F32),
            pltpu.VMEM((HALF, m), F32),
            pltpu.VMEM((1, m), F32),
            pltpu.VMEM((x.shape[0], m // HALF, HALF), F32),
        )

    parts = over("col", parts)
    e, parts = call(
        functools.partial(image_kernel, all_tgt, 3, 0, dim_tgt, 0.5 * LN2),
        (parts, yt, xr, xt, h),
        (shape(rs, HALF), shape(n_row, rt * (1 + dim_tgt), HALF)),
        image_scratch(nt, ns),
        name="tgt_part",
    )
    parts = over("row", parts)
    h, parts, tgt = call(
        functools.partial(image_kernel, all_src, 0, 3, dim_src, 1.0),
        (parts, xt, yr, yt, e),
        (
            shape(rt, HALF),
            shape(n_col, rs * (1 + dim_src), HALF),
            shape(n_row, rt * dim_tgt, HALF),
        ),
        image_scratch(ns, nt),
        name="src_part",
    )
    parts = over("col", parts)
    src = call(
        functools.partial(share_kernel, rs),
        (parts,),
        shape(n_col, rs * dim_src, HALF),
        name="src_share",
    )
    src = over("col", src).reshape(x.shape[0], rs, HALF)
    tgt = over("row", tgt).reshape(x.shape[0], rt, HALF)
    f, g, si, ti = call(
        end_kernel,
        (e, h, xsq, ysq, src, tgt),
        (shape(rs, HALF), shape(rt, HALF), shape(*x.shape), shape(*y.shape)),
        name="end",
    )
    return f.reshape(ns), g.reshape(nt), si, ti


def solution(mesh):
    in_specs = (P(None, "row"), P(None, "col"))
    out_specs = (P("row"), P("col"), P(None, "row"), P(None, "col"))
    return jax.shard_map(local, mesh=mesh, in_specs=in_specs, out_specs=out_specs, check_vma=False)
```

time: 1000 us -> 217 us (0.22)
  blocking collectives: 723 us -> 155 us
  waiting for transfers between devices: 155 us -> 6.92 us
  matrix products: 80.5 us -> 0 us
  Pallas kernels: 0 us -> 45 us
  other arithmetic: 17.1 us -> 0 us
  between operations: 14.3 us -> 0.71 us
    pmax x8 -> x0, blocking collectives: 369 us -> none  [the longest x3 181 us: local(): whole_peak = lax.pmax(peak, 'row')]
    psum x8 -> x0, blocking collectives: 355 us -> none  [the longest x3 183 us: local(): total = lax.psum(total * jnp.exp(peak - whole_peak), 'row')]
    all_to_all x0 -> x8, blocking collectives: none -> 155 us  [over(): return lax.all_to_all(v, axis, 0, 0)]
    psum x2 -> x0, waiting for transfers between devices: 155 us -> none  [the longest x1 136 us: local(): total, moved = lax.psum((total * factor, moved * factor[None, :]), 'col')]
    dot_general x27 -> x0, matrix products: 80.5 us -> none  [the longest x21 65.9 us: cost_block(): lax.dot_general(src_embed, tblock, (((0,), (0,)), ((), ())), precision=la...]
    pallas_call x0 -> x9, Pallas kernels: none -> 45 us  [call(): pl.pallas_call(kernel, out_shape=outs, in_specs=[VMEM] * len(ins), out_sp...]
    reduce_sum x23 -> x0, other arithmetic: 12.2 us -> none  [the longest x9 4.64 us: col_block(): block_total = jnp.sum(jnp.exp(scores - block_peak[None, :]), axis=0)]
  transfers between devices with their start and end apart: 2 -> 1, of which waited for: 2 -> 1; matrix products, arithmetic and copies ran while one was open for 0% -> 0% of each run, Pallas kernels for 0% -> 0%
where the time goes in v1:
time: 217 us; the launch traced here: 215 us
  blocking collectives  155 us (71%)
  Pallas kernels  45 us (21%)
  waiting for transfers between devices  6.92 us (3%)
  starting transfers between devices  5.88 us (3%)
    all_to_all x8, blocking collectives, over(): return lax.all_to_all(v, axis, 0, 0)  155 us
    pallas_call x9, Pallas kernels, call(): pl.pallas_call(kernel, out_shape=outs, in_specs=[VMEM] * len(ins), out_sp...  45 us
    all_to_all x1, waiting for transfers between devices, over(): return lax.all_to_all(v, axis, 0, 0)  6.92 us
    all_to_all x1, starting transfers between devices, over(): return lax.all_to_all(v, axis, 0, 0)  5.88 us
  transfers between devices with their start and end apart: 1, of which 1 were waited for; matrix products, arithmetic and copies ran while one was open for 0% of the time, Pallas kernels for 0%

profile of v1, /device:TPU:6, one launch (start us, length us, event | category | flops | bytes accessed | tf_op | source)
XLA Modules:
  0.0 215.3 jit_solution(9687197303217343265)
XLA Ops:
  0.6 0.0 copy-start
  0.6 0.9 copy-done
  1.6 0.0 copy-start.1
  1.6 0.9 copy-done.1
  2.5 8.6 %start.1 = (bf16[1024,256]{1,0:T(8,128)(2,1)S(1)}, bf16[1536,256]{1,0:T(8,128)(2,1)S(1)}, bf16[256,1024]{1,0:T(8,128)(2,1)S(1)}, bf16[256,1536]{1,0:T(8,128)(2,1...) custom-call(f32[32,1024]{1,0:T(8,128)S(1)} %copy-done.1, f32[32,1536]{1,0:T(8,128)S(1)} %copy-done), custom_call_target="tpu_custom_call" | custom-call | tf_op jit(solution)/shard_map/start/pallas_call | solution.py:307
  11.0 27.5 %all_to_all.45.p = f32[16,8,128]{2,1,0:T(8,128)S(1)} all-to-all(f32[16,8,128]{2,1,0:T(8,128)S(1)} %get-tuple-element.28), channel_id=1, replica_groups=mesh['row'=32,'col'=16] {'col'}, dimensions={0} | all-to-all | bytes 131072 | tf_op jit(solution)/shard_map/all_to_all | solution.py:329
  38.6 8.7 %cols.2 = (f32[8,128]{1,0:T(8,128)S(1)}, f32[32,12,128]{2,1,0:T(8,128)S(1)}) custom-call(f32[16,8,128]{2,1,0:T(8,128)S(1)} %all_to_all.45.p, bf16[1024,256]{1,0:T(8,128)(2,1)S(1)} %get-tuple-element.29.c.col_ref.values_ref, bf16[256,1536]{1,0:T(8,128)(2,1)S(1)} %get-tuple-element.30.r.row_ref), custom_call_target="tpu_custom_call" | custom-call | tf_op jit(solution)/shard_map/cols/pallas_call | solution.py:307
  47.2 14.4 %all_to_all.46.parts_ref = f32[32,12,128]{2,1,0:T(8,128)S(1)} all-to-all(f32[32,12,128]{2,1,0:T(8,128)S(1)} %get-tuple-element.31), channel_id=1, replica_groups=mesh['row'=32,'col'=16] {'row'}, dimensions={0} | all-to-all | bytes 393216 | tf_op jit(solution)/shard_map/all_to_all | solution.py:329
  61.7 1.3 rows.2
  63.0 22.0 %all_to_all.47.parts_ref = f32[16,8,128]{2,1,0:T(8,128)S(1)} all-to-all(f32[16,8,128]{2,1,0:T(8,128)S(1)} %get-tuple-element.35), channel_id=1, replica_groups=mesh['row'=32,'col'=16] {'col'}, dimensions={0} | all-to-all | bytes 131072 | tf_op jit(solution)/shard_map/all_to_all | solution.py:329
  85.0 7.3 %cols.3 = (f32[8,128]{1,0:T(8,128)S(1)}, f32[32,12,128]{2,1,0:T(8,128)S(1)}) custom-call(f32[16,8,128]{2,1,0:T(8,128)S(1)} %all_to_all.47.parts_ref, bf16[1024,256]{1,0:T(8,128)(2,1)S(1)} %get-tuple-element.29.c.col_ref.values_ref, bf16[256,1536]{1,0:T(8,128)(2,1)S(1)} %get-tuple-element.30.r.row_ref, f32[12,128]{1,0:T(8,128)S(1)} %get-tuple-element.36.old_ref), custom_call_target="tpu_custom_call" | custom-call | tf_op jit(solution)/shard_map/cols/pallas_call | solution.py:307
  92.3 12.1 %all_to_all.48.parts_ref = f32[32,12,128]{2,1,0:T(8,128)S(1)} all-to-all(f32[32,12,128]{2,1,0:T(8,128)S(1)} %get-tuple-element.37), channel_id=1, replica_groups=mesh['row'=32,'col'=16] {'row'}, dimensions={0} | all-to-all | bytes 393216 | tf_op jit(solution)/shard_map/all_to_all | solution.py:329
  104.5 1.3 rows.3
  105.8 22.1 %all_to_all.49.parts_ref = f32[16,8,128]{2,1,0:T(8,128)S(1)} all-to-all(f32[16,8,128]{2,1,0:T(8,128)S(1)} %get-tuple-element.39), channel_id=1, replica_groups=mesh['row'=32,'col'=16] {'col'}, dimensions={0} | all-to-all | bytes 131072 | tf_op jit(solution)/shard_map/all_to_all | solution.py:329
  127.9 10.7 %tgt_part.1 = (f32[8,128]{1,0:T(8,128)S(1)}, f32[32,24,128]{2,1,0:T(8,128)S(1)}) custom-call(f32[16,8,128]{2,1,0:T(8,128)S(1)} %all_to_all.49.parts_ref, bf16[1536,256]{1,0:T(8,128)(2,1)S(1)} %get-tuple-element.32.col_ref.values_ref, bf16[256,1024]{1,0:T(8,128)(2,1)S(1)} %get-tuple-element.33.row_ref, ...), custom_call_target="tpu_custom_call" | custom-call | tf_op jit(solution)/shard_map/tgt_part/pallas_call | solution.py:307
  138.6 13.4 %all_to_all.50.parts_ref = f32[32,24,128]{2,1,0:T(8,128)S(1)} all-to-all(f32[32,24,128]{2,1,0:T(8,128)S(1)} %get-tuple-element.42), channel_id=1, replica_groups=mesh['row'=32,'col'=16] {'row'}, dimensions={0} | all-to-all | bytes 786432 | tf_op jit(solution)/shard_map/all_to_all | solution.py:329
  152.0 6.2 %src_part.1 = (f32[12,128]{1,0:T(8,128)S(1)}, f32[16,24,128]{2,1,0:T(8,128)S(1)}, f32[32,12,128]{2,1,0:T(8,128)}) custom-call(f32[32,24,128]{2,1,0:T(8,128)S(1)} %all_to_all.50.parts_ref, bf16[1024,256]{1,0:T(8,128)(2,1)S(1)} %get-tuple-element.29.c.col_ref.values_ref, bf16[256,1536]{1,0:T(8,128)(2,1)S(1)} %get-tuple-element.30.r.row_ref, ...), custom_call_target="tpu_custom_call" | custom-call | tf_op jit(solution)/shard_map/src_part/pallas_call | solution.py:307
  158.2 22.9 %all_to_all.51.parts_ref = f32[16,24,128]{2,1,0:T(8,128)S(1)} all-to-all(f32[16,24,128]{2,1,0:T(8,128)S(1)} %get-tuple-element.46), channel_id=1, replica_groups=mesh['row'=32,'col'=16] {'col'}, dimensions={0} | all-to-all | bytes 393216 | tf_op jit(solution)/shard_map/all_to_all | solution.py:329
  181.1 5.9 %all-to-all-start.8 = ((f32[32,12,128]{2,1,0:T(8,128)}), f32[32,12,128]{2,1,0:T(8,128)S(1)}, u32[]{:S(2)}, u32[]{:S(2)}) async-start(f32[32,12,128]{2,1,0:T(8,128)} %get-tuple-element.47), calls=%async_computation.8 | async-start | bytes 524288 | tf_op jit(solution)/shard_map/all_to_all | solution.py:329
  187.0 6.9 %all-to-all-done.8.tgt_ref = f32[32,12,128]{2,1,0:T(8,128)S(1)} async-done(((f32[32,12,128]{2,1,0:T(8,128)}), f32[32,12,128]{2,1,0:T(8,128)S(1)}, u32[]{:S(2)}, u32[]{:S(2)}) %all-to-all-start.8) | async-done | bytes 196640 | tf_op jit(solution)/shard_map/all_to_all | solution.py:329
  193.9 20.4 %all_to_all.52 = f32[16,16,128]{2,1,0:T(8,128)S(1)} all-to-all(f32[16,16,128]{2,1,0:T(8,128)S(1)} %src_share.1), channel_id=1, replica_groups=mesh['row'=32,'col'=16] {'col'}, dimensions={0} | all-to-all | bytes 262144 | tf_op jit(solution)/shard_map/all_to_all | solution.py:329
  214.4 0.9 end.1
  (1 shorter events, 0.0 us)
Async XLA Ops:
  0.6 0.9 copy-start
  1.6 0.9 copy-start.1
  181.1 12.9 %all-to-all-start.8 = ((f32[32,12,128]{2,1,0:T(8,128)}), f32[32,12,128]{2,1,0:T(8,128)S(1)}, u32[]{:S(2)}, u32[]{:S(2)}) async-start(f32[32,12,128]{2,1,0:T(8,128)} %get-tuple-element.47), calls=%async_computation.8 | async-start | bytes 524288 | tf_op jit(solution)/shard_map/all_to_all | solution.py:329

commit v2 on v1

--- a/solution.py
+++ b/solution.py
@@ -15,7 +15,7 @@
 HALF = 128
 TILE = 256
 CHUNK = 256
-PROBE = 256
+PROBE = 64
 LOW, HIGH = 2.0**-90, 2.0**100
 BF, F32 = jnp.bfloat16, jnp.float32
 VMEM = pl.BlockSpec(memory_space=pltpu.VMEM)
@@ -89,8 +89,8 @@
     )
 
 
-def scores(col_ref, half_ref, start, rhs):
-    rows = pl.ds(start, CHUNK)
+def scores(col_ref, half_ref, start, rhs, count=CHUNK):
+    rows = pl.ds(start, count)
     lhs = jnp.concatenate([col_ref[rows, :HALF], half_ref[rows, :]], axis=1)
     return jnp.dot(lhs, rhs, preferred_element_type=F32)
 
@@ -121,6 +121,14 @@
 
         acc = lax.fori_loop(0, count // CHUNK, step, jnp.full((8, TILE), -jnp.inf, F32))
         shift_ref[:, pl.ds(start, TILE)] = -jnp.max(acc, axis=0, keepdims=True)
+
+
+def probe(col_ref, half_ref, row_ref, shift_ref, first):
+    for t in range(row_ref.shape[1] // TILE):
+        cols = slice(t * TILE, (t + 1) * TILE)
+        rhs = tile_of(row_ref, row_block(jnp.zeros((1, TILE), F32), first), t * TILE)
+        s = scores(col_ref, half_ref, 0, rhs, PROBE)
+        shift_ref[:, cols] = -jnp.max(s, axis=0, keepdims=True)
 
 
 def outside(s):
@@ -165,7 +173,7 @@
     ysq_ref[...] = as_dense(ysq)
     half_ref[...] = column_half(ysq * -LOG2E, 3, yt_ref)
     args = (yt_ref, half_ref, xr_ref, shift_ref)
-    peaks(*args, 0, PROBE)
+    probe(*args, 0)
     send_all(out_ref, as_dense(local_lse(*args, s_ref, 0)))
 
 
@@ -180,89 +188,63 @@
     half_ref[...] = column_half(as_row(new), col_first, col_ref)
     args = (col_ref, half_ref, row_ref, shift_ref)
     if old_ref is None:
-        peaks(*args, row_first, PROBE)
+        probe(*args, row_first)
     else:
         shift_ref[...] = as_row(old_ref[...])
     send_all(out_ref, as_dense(local_lse(*args, s_ref, row_first)))
 
 
-def maps(col_ref, half_ref, row_ref, block_ref, values_ref, moved_ref, exact):
-    n = row_ref.shape[1]
-
-    def chunk(c, unused):
-        start = pl.multiple_of(c * CHUNK, CHUNK)
-        if exact:
-            peak = jnp.full((CHUNK, 1), -jnp.inf, F32)
-            for t in range(n // TILE):
-                cols = slice(t * TILE, (t + 1) * TILE)
-                rhs = tile_of(row_ref, block_ref[:, cols], t * TILE)
-                s = scores(col_ref, half_ref, start, rhs)
-                peak = jnp.maximum(peak, jnp.max(s, axis=1, keepdims=True))
-        total = jnp.zeros((CHUNK, HALF), F32)
-        for t in range(n // TILE):
-            cols = slice(t * TILE, (t + 1) * TILE)
-            rhs = tile_of(row_ref, block_ref[:, cols], t * TILE)
-            s = scores(col_ref, half_ref, start, rhs)
-            w = jnp.exp2(s - peak) if exact else jnp.exp2(s)
+def maps(col_ref, half_ref, row_ref, values_ref, shift_ref, moved_ref, first):
+    count, n = col_ref.shape[0], row_ref.shape[1]
+    for t in range(n // TILE):
+        cols = slice(t * TILE, (t + 1) * TILE)
+        rhs = tile_of(row_ref, row_block(shift_ref[:, cols], first), t * TILE)
+        total = jnp.zeros((HALF, TILE), F32)
+        for c in range(count // CHUNK):
+            w = jnp.exp2(scores(col_ref, half_ref, c * CHUNK, rhs))
             high = w.astype(BF)
             low = (w - high.astype(F32)).astype(BF)
-            values = values_ref[cols, HALF:]
-            total += jnp.dot(high, values, preferred_element_type=F32)
-            total += jnp.dot(low, values, preferred_element_type=F32)
-        if exact:
-            lane = lax.broadcasted_iota(jnp.int32, (CHUNK, HALF), 1)
-            total = jnp.where(lane == HALF - 1, peak, total)
-        moved_ref[pl.ds(start, CHUNK), :] = total
-        return unused
-
-    chunks = col_ref.shape[0] // CHUNK
-    if exact:
-        lax.fori_loop(0, chunks, chunk, 0)
-    else:
-        for c in range(chunks):
-            chunk(c, 0)
+            values = values_ref[HALF:, c * CHUNK : (c + 1) * CHUNK]
+            total += jnp.dot(values, high, preferred_element_type=F32)
+            total += jnp.dot(values, low, preferred_element_type=F32)
+        moved_ref[:, cols] = total
+
+
+def potential_kernel(total, parts_ref, new_ref):
+    new_ref[...] = math.log2(total) - joined(parts_ref[...])
+
+
+def join_kernel(total, parts_ref, new_ref, share_ref):
+    parts = parts_ref[...]
+    logs = parts[:, : new_ref.shape[0]]
+    peak = jnp.max(logs, axis=0)
+    weights = jnp.exp2(logs - peak[None])
+    sum_w = jnp.sum(weights, axis=0)
+    new_ref[...] = math.log2(total) - (peak + jnp.log2(sum_w))
+    send_all(share_ref, share(parts, weights, sum_w))
 
 
 def image_kernel(
-    total, col_first, row_first, dims, scale,
-    parts_ref, col_ref, row_ref, values_ref, old_ref,
-    *refs,
+    dims, scale, col_first, row_first,
+    new_ref, col_ref, row_ref, values_ref, old_ref,
+    out_ref,
+    half_ref, shift_ref, moved_ref, image_ref,
 ):
-    new_ref, out_ref = refs[:2]
-    half_ref, block_ref, moved_ref, across_ref, shift_ref, image_ref = refs[-6:]
     rows = old_ref.shape[0]
-    if len(refs) > 8:
-        share_ref = refs[2]
-        parts = parts_ref[...]
-        logs = parts[:, : new_ref.shape[0]]
-        peak = jnp.max(logs, axis=0)
-        weights = jnp.exp2(logs - peak[None])
-        sum_w = jnp.sum(weights, axis=0)
-        new = math.log2(total) - (peak + jnp.log2(sum_w))
-        send_all(share_ref, share(parts, weights, sum_w))
-    else:
-        new = math.log2(total) - joined(parts_ref[...])
-    new_ref[...] = new
-    block_ref[...] = row_block(as_row(new), row_first)
-    shift = as_row(old_ref[...])
-    shift_ref[...] = shift
-    half_ref[...] = column_half(shift, col_first, col_ref)
-    args = (col_ref, half_ref, row_ref, block_ref, values_ref, moved_ref)
-    maps(*args, False)
-    across_ref[...] = jnp.transpose(moved_ref[...])
-    one = 3 - row_first
-    one = {0: 3, 3: 0}[row_first]
-
-    @pl.when(outside(across_ref[one : one + 1, :]))
+    half_ref[...] = column_half(as_row(new_ref[...]), col_first, col_ref)
+    shift_ref[...] = as_row(old_ref[...])
+    args = (col_ref, half_ref, row_ref)
+    maps(*args, values_ref, shift_ref, moved_ref, row_first)
+    one = 3 - col_first
+
+    @pl.when(outside(moved_ref[one : one + 1, :]))
     def _():
-        half_ref[...] = col_ref[:, HALF:]
-        maps(*args, True)
-        across_ref[...] = jnp.transpose(moved_ref[...])
-        shift_ref[...] = jnp.zeros_like(shift)
-
-    s = across_ref[one : one + 1, :]
-    log = jnp.log2(s) + across_ref[HALF - 1 :, :] - shift_ref[...]
-    image = across_ref[16:48, :] + across_ref[48:80, :] + across_ref[80:112, :]
+        peaks(*args, shift_ref, row_first, col_ref.shape[0])
+        maps(*args, values_ref, shift_ref, moved_ref, row_first)
+
+    s = moved_ref[one : one + 1, :]
+    log = jnp.log2(s) - shift_ref[...]
+    image = moved_ref[16:48, :] + moved_ref[48:80, :] + moved_ref[80:112, :]
     image = image * (scale / s)
     for r in range(rows):
         image_ref[:, r, :] = image[:, HALF * r : HALF * (r + 1)]
@@ -366,33 +348,33 @@
         )
 
     def image_scratch(m, n):
-        return (
-            pltpu.VMEM((m, HALF), BF),
-            pltpu.VMEM((16, n), BF),
-            pltpu.VMEM((m, HALF), F32),
-            pltpu.VMEM((HALF, m), F32),
-            pltpu.VMEM((1, m), F32),
-            pltpu.VMEM((x.shape[0], m // HALF, HALF), F32),
+        return scratch(m, n)[:2] + (
+            pltpu.VMEM((HALF, n), F32),
+            pltpu.VMEM((x.shape[0], n // HALF, HALF), F32),
         )
 
     parts = over("col", parts)
-    e, parts = call(
-        functools.partial(image_kernel, all_tgt, 3, 0, dim_tgt, 0.5 * LN2),
-        (parts, yt, xr, xt, h),
-        (shape(rs, HALF), shape(n_row, rt * (1 + dim_tgt), HALF)),
+    e = call(functools.partial(potential_kernel, all_tgt), (parts,), shape(rs, HALF), name="src_join")
+    parts = call(
+        functools.partial(image_kernel, dim_tgt, 0.5 * LN2, 0, 3),
+        (e, xt, yr, xr, h),
+        shape(n_row, rt * (1 + dim_tgt), HALF),
+        image_scratch(ns, nt),
+        name="tgt_part",
+    )
+    parts = over("row", parts)
+    h, tgt = call(
+        functools.partial(join_kernel, all_src),
+        (parts,),
+        (shape(rt, HALF), shape(n_row, rt * dim_tgt, HALF)),
+        name="tgt_join",
+    )
+    tgt = over("row", tgt).reshape(x.shape[0], rt, HALF)
+    parts = call(
+        functools.partial(image_kernel, dim_src, 1.0, 3, 0),
+        (h, yt, xr, yr, e),
+        shape(n_col, rs * (1 + dim_src), HALF),
         image_scratch(nt, ns),
-        name="tgt_part",
-    )
-    parts = over("row", parts)
-    h, parts, tgt = call(
-        functools.partial(image_kernel, all_src, 0, 3, dim_src, 1.0),
-        (parts, xt, yr, yt, e),
-        (
-            shape(rt, HALF),
-            shape(n_col, rs * (1 + dim_src), HALF),
-            shape(n_row, rt * dim_tgt, HALF),
-        ),
-        image_scratch(ns, nt),
         name="src_part",
     )
     parts = over("col", parts)
@@ -403,7 +385,6 @@
         name="src_share",
     )
     src = over("col", src).reshape(x.shape[0], rs, HALF)
-    tgt = over("row", tgt).reshape(x.shape[0], rt, HALF)
     f, g, si, ti = call(
         end_kernel,
         (e, h, xsq, ysq, src, tgt),

time: 217 us -> 213 us (0.982)
  blocking collectives: 155 us -> 139 us
  Pallas kernels: 45 us -> 57.6 us
    all_to_all x8, blocking collectives: 155 us -> 139 us  [over(): return lax.all_to_all(v, axis, 0, 0)]
    pallas_call x9 -> x11, Pallas kernels: 45 us -> 57.6 us  [call(): pl.pallas_call(kernel, out_shape=outs, in_specs=[VMEM] * len(ins), out_sp...]
where the time goes in v2:
time: 213 us; the launch traced here: 212 us
  blocking collectives  139 us (65%)
  Pallas kernels  57.6 us (27%)
  waiting for transfers between devices  6.95 us (3%)
  starting transfers between devices  6.19 us (3%)
    all_to_all x8, blocking collectives, over(): return lax.all_to_all(v, axis, 0, 0)  139 us
    pallas_call x11, Pallas kernels, call(): pl.pallas_call(kernel, out_shape=outs, in_specs=[VMEM] * len(ins), out_sp...  57.6 us
    all_to_all x1, waiting for transfers between devices, over(): return lax.all_to_all(v, axis, 0, 0)  6.95 us
    all_to_all x1, starting transfers between devices, over(): return lax.all_to_all(v, axis, 0, 0)  6.19 us
  transfers between devices with their start and end apart: 1, of which 1 were waited for; matrix products, arithmetic and copies ran while one was open for 0% of the time, Pallas kernels for 0%

profile of v2, /device:TPU:6, one launch (start us, length us, event | category | flops | bytes accessed | tf_op | source)
XLA Modules:
  0.0 211.9 jit_solution(11623826229265955823)
XLA Ops:
  0.6 0.0 copy-start
  0.6 0.9 copy-done
  1.6 0.0 copy-start.1
  1.6 0.9 copy-done.1
  2.5 7.6 %start.1 = (bf16[1024,256]{1,0:T(8,128)(2,1)S(1)}, bf16[1536,256]{1,0:T(8,128)(2,1)S(1)}, bf16[256,1024]{1,0:T(8,128)(2,1)S(1)}, bf16[256,1536]{1,0:T(8,128)(2,1...) custom-call(f32[32,1024]{1,0:T(8,128)S(1)} %copy-done.1, f32[32,1536]{1,0:T(8,128)S(1)} %copy-done), custom_call_target="tpu_custom_call" | custom-call | tf_op jit(solution)/shard_map/start/pallas_call | solution.py:289
  10.1 27.7 %all_to_all.45.p = f32[16,8,128]{2,1,0:T(8,128)S(1)} all-to-all(f32[16,8,128]{2,1,0:T(8,128)S(1)} %get-tuple-element.25), channel_id=1, replica_groups=mesh['row'=32,'col'=16] {'col'}, dimensions={0} | all-to-all | bytes 131072 | tf_op jit(solution)/shard_map/all_to_all | solution.py:311
  37.8 7.4 %cols.2 = (f32[8,128]{1,0:T(8,128)S(1)}, f32[32,12,128]{2,1,0:T(8,128)S(1)}) custom-call(f32[16,8,128]{2,1,0:T(8,128)S(1)} %all_to_all.45.p, bf16[1024,256]{1,0:T(8,128)(2,1)S(1)} %get-tuple-element.26.c.col_ref, bf16[256,1536]{1,0:T(8,128)(2,1)S(1)} %get-tuple-element.27.r.row_ref.values_ref), custom_call_target="tpu_custom_call" | custom-call | tf_op jit(solution)/shard_map/cols/pallas_call | solution.py:289
  45.2 14.4 %all_to_all.46.parts_ref = f32[32,12,128]{2,1,0:T(8,128)S(1)} all-to-all(f32[32,12,128]{2,1,0:T(8,128)S(1)} %get-tuple-element.28), channel_id=1, replica_groups=mesh['row'=32,'col'=16] {'row'}, dimensions={0} | all-to-all | bytes 393216 | tf_op jit(solution)/shard_map/all_to_all | solution.py:311
  59.6 7.3 %rows.2 = (f32[12,128]{1,0:T(8,128)S(1)}, f32[16,8,128]{2,1,0:T(8,128)S(1)}) custom-call(f32[32,12,128]{2,1,0:T(8,128)S(1)} %all_to_all.46.parts_ref, bf16[1536,256]{1,0:T(8,128)(2,1)S(1)} %get-tuple-element.29.col_ref, bf16[256,1024]{1,0:T(8,128)(2,1)S(1)} %get-tuple-element.30.row_ref.values_ref, f32[8,128]{1,0:T(8,128)S(1)} %get-tuple-element.31.old_ref), custom_call_target="tpu_custom_call" | custom-call | tf_op jit(solution)/shard_map/rows/pallas_call | solution.py:289
  66.9 16.0 %all_to_all.47.parts_ref = f32[16,8,128]{2,1,0:T(8,128)S(1)} all-to-all(f32[16,8,128]{2,1,0:T(8,128)S(1)} %get-tuple-element.32), channel_id=1, replica_groups=mesh['row'=32,'col'=16] {'col'}, dimensions={0} | all-to-all | bytes 131072 | tf_op jit(solution)/shard_map/all_to_all | solution.py:311
  83.0 7.2 %cols.3 = (f32[8,128]{1,0:T(8,128)S(1)}, f32[32,12,128]{2,1,0:T(8,128)S(1)}) custom-call(f32[16,8,128]{2,1,0:T(8,128)S(1)} %all_to_all.47.parts_ref, bf16[1024,256]{1,0:T(8,128)(2,1)S(1)} %get-tuple-element.26.c.col_ref, bf16[256,1536]{1,0:T(8,128)(2,1)S(1)} %get-tuple-element.27.r.row_ref.values_ref, f32[12,128]{1,0:T(8,128)S(1)} %get-tuple-element.33.old_ref), custom_call_target="tpu_custom_call" | custom-call | tf_op jit(solution)/shard_map/cols/pallas_call | solution.py:289
  90.2 12.2 %all_to_all.48.parts_ref = f32[32,12,128]{2,1,0:T(8,128)S(1)} all-to-all(f32[32,12,128]{2,1,0:T(8,128)S(1)} %get-tuple-element.34), channel_id=1, replica_groups=mesh['row'=32,'col'=16] {'row'}, dimensions={0} | all-to-all | bytes 393216 | tf_op jit(solution)/shard_map/all_to_all | solution.py:311
  102.5 7.5 %rows.3 = (f32[12,128]{1,0:T(8,128)S(1)}, f32[16,8,128]{2,1,0:T(8,128)S(1)}) custom-call(f32[32,12,128]{2,1,0:T(8,128)S(1)} %all_to_all.48.parts_ref, bf16[1536,256]{1,0:T(8,128)(2,1)S(1)} %get-tuple-element.29.col_ref, bf16[256,1024]{1,0:T(8,128)(2,1)S(1)} %get-tuple-element.30.row_ref.values_ref, f32[8,128]{1,0:T(8,128)S(1)} %get-tuple-element.35.old_ref), custom_call_target="tpu_custom_call" | custom-call | tf_op jit(solution)/shard_map/rows/pallas_call | solution.py:289
  109.9 16.0 %all_to_all.49.parts_ref = f32[16,8,128]{2,1,0:T(8,128)S(1)} all-to-all(f32[16,8,128]{2,1,0:T(8,128)S(1)} %get-tuple-element.36), channel_id=1, replica_groups=mesh['row'=32,'col'=16] {'col'}, dimensions={0} | all-to-all | bytes 131072 | tf_op jit(solution)/shard_map/all_to_all | solution.py:311
  126.0 9.4 %tgt_part.1 = f32[32,24,128]{2,1,0:T(8,128)S(1)} custom-call(f32[8,128]{1,0:T(8,128)S(1)} %src_join.1.new_ref.old_ref.e_ref, bf16[1024,256]{1,0:T(8,128)(2,1)S(1)} %get-tuple-element.26.c.col_ref, bf16[256,1536]{1,0:T(8,128)(2,1)S(1)} %get-tuple-element.27.r.row_ref.values_ref, bf16[256,1024]{1,0:T(8,128)(2,1)S(1)} %get-tuple-element.30.row_ref.values_ref, ...), custom_call_target="tpu_custom_call" | custom-call | tf_op jit(solution)/shard_map/tgt_part/pallas_call | solution.py:289
  135.4 13.3 %all_to_all.50.parts_ref = f32[32,24,128]{2,1,0:T(8,128)S(1)} all-to-all(f32[32,24,128]{2,1,0:T(8,128)S(1)} %tgt_part.1), channel_id=1, replica_groups=mesh['row'=32,'col'=16] {'row'}, dimensions={0} | all-to-all | bytes 786432 | tf_op jit(solution)/shard_map/all_to_all | solution.py:311
  148.7 0.8 tgt_join.1
  149.5 9.4 %src_part.1 = f32[16,24,128]{2,1,0:T(8,128)S(1)} custom-call(f32[12,128]{1,0:T(8,128)S(1)} %get-tuple-element.38.new_ref.h_ref, bf16[1536,256]{1,0:T(8,128)(2,1)S(1)} %get-tuple-element.29.col_ref, bf16[256,1024]{1,0:T(8,128)(2,1)S(1)} %get-tuple-element.30.row_ref.values_ref, bf16[256,1536]{1,0:T(8,128)(2,1)S(1)} %get-tuple-element.27.r.row_ref.values_ref, ...), custom_call_target="tpu_custom_call" | custom-call | tf_op jit(solution)/shard_map/src_part/pallas_call | solution.py:289
  158.9 18.7 %all_to_all.51.parts_ref = f32[16,24,128]{2,1,0:T(8,128)S(1)} all-to-all(f32[16,24,128]{2,1,0:T(8,128)S(1)} %src_part.1), channel_id=1, replica_groups=mesh['row'=32,'col'=16] {'col'}, dimensions={0} | all-to-all | bytes 393216 | tf_op jit(solution)/shard_map/all_to_all | solution.py:311
  177.7 6.2 %all-to-all-start.8 = ((f32[32,12,128]{2,1,0:T(8,128)}), f32[32,12,128]{2,1,0:T(8,128)S(1)}, u32[]{:S(2)}, u32[]{:S(2)}) async-start(f32[32,12,128]{2,1,0:T(8,128)} %get-tuple-element.41), calls=%async_computation.8 | async-start | bytes 524288 | tf_op jit(solution)/shard_map/all_to_all | solution.py:311
  183.9 6.9 %all-to-all-done.8.tgt_ref = f32[32,12,128]{2,1,0:T(8,128)S(1)} async-done(((f32[32,12,128]{2,1,0:T(8,128)}), f32[32,12,128]{2,1,0:T(8,128)S(1)}, u32[]{:S(2)}, u32[]{:S(2)}) %all-to-all-start.8) | async-done | bytes 196640 | tf_op jit(solution)/shard_map/all_to_all | solution.py:311
  190.8 20.2 %all_to_all.52 = f32[16,16,128]{2,1,0:T(8,128)S(1)} all-to-all(f32[16,16,128]{2,1,0:T(8,128)S(1)} %src_share.1), channel_id=1, replica_groups=mesh['row'=32,'col'=16] {'col'}, dimensions={0} | all-to-all | bytes 262144 | tf_op jit(solution)/shard_map/all_to_all | solution.py:311
  211.0 0.9 end.1
  (2 shorter events, 0.1 us)
Async XLA Ops:
  0.6 0.9 copy-start
  1.6 0.9 copy-start.1
  177.7 13.2 %all-to-all-start.8 = ((f32[32,12,128]{2,1,0:T(8,128)}), f32[32,12,128]{2,1,0:T(8,128)S(1)}, u32[]{:S(2)}, u32[]{:S(2)}) async-start(f32[32,12,128]{2,1,0:T(8,128)} %get-tuple-element.41), calls=%async_computation.8 | async-start | bytes 524288 | tf_op jit(solution)/shard_map/all_to_all | solution.py:311

commit v3 on v2

--- a/solution.py
+++ b/solution.py
@@ -13,6 +13,7 @@
 LN2 = math.log(2.0)
 DEPTH = 256
 HALF = 128
+DIM = 32
 TILE = 256
 CHUNK = 256
 PROBE = 64
@@ -79,7 +80,7 @@
     keep = lax.broadcasted_iota(jnp.int32, (8, n), 0)
     rows = jnp.where((keep >= first) & (keep < first + 3), rows, 0.0)
     wide = jnp.concatenate([rows, jnp.zeros((HALF - 8, n), F32)], axis=0)
-    return static_ref[:, HALF:] + jnp.transpose(wide).astype(BF)
+    return static_ref[:, HALF:] + jnp.transpose(wide.astype(BF))
 
 
 def tile_of(row_ref, block, start):
@@ -107,8 +108,8 @@
         s_ref[:, cols] = jnp.sum(acc, axis=0, keepdims=True)
 
 
-def peaks(col_ref, half_ref, row_ref, shift_ref, first, count):
-    n = row_ref.shape[1]
+def peaks(col_ref, half_ref, row_ref, shift_ref, first):
+    count, n = col_ref.shape[0], row_ref.shape[1]
 
     @pl.loop(0, n // TILE)
     def _(t):
@@ -135,16 +136,16 @@
     return jnp.any(jnp.logical_not((s > LOW) & (s < HIGH)))
 
 
-def local_lse(col_ref, half_ref, row_ref, shift_ref, s_ref, first):
-    args = (col_ref, half_ref, row_ref, shift_ref)
-    sums(*args, s_ref, first)
-
-    @pl.when(outside(s_ref[...]))
+def guarded(compute, finish, sum_ref, col_ref, half_ref, row_ref, shift_ref, first):
+    compute()
+    s = as_dense(sum_ref[...])
+    finish(s)
+
+    @pl.when(outside(s))
     def _():
-        peaks(*args, first, col_ref.shape[0])
-        sums(*args, s_ref, first)
-
-    return jnp.log2(s_ref[...]) - shift_ref[...]
+        peaks(col_ref, half_ref, row_ref, shift_ref, first)
+        compute()
+        finish(as_dense(sum_ref[...]))
 
 
 def joined(parts):
@@ -152,29 +153,51 @@
     return peak + jnp.log2(jnp.sum(jnp.exp2(parts - peak[None]), axis=0))
 
 
-def send_all(out_ref, v):
-    out_ref[...] = jnp.broadcast_to(v[None], out_ref.shape)
+def joined_rows(total, parts_ref, new_ref):
+    new = math.log2(total) - joined(parts_ref[...])
+    step = new.shape[1]
+    for k in range(new.shape[0]):
+        new_ref[step * k : step * (k + 1), :] = new[k]
+
+
+def send_logs(out_ref, log):
+    n, step = out_ref.shape[0], out_ref.shape[2]
+    for k in range(log.shape[0] // step):
+        rows = log[step * k : step * (k + 1)]
+        out_ref[:, k] = jnp.broadcast_to(rows[None], (n, step, HALF))
 
 
 def start_kernel(
-    x_ref, y_ref,
+    xy_ref,
     xt_ref, yt_ref, xr_ref, yr_ref, xsq_ref, ysq_ref, out_ref,
     half_ref, shift_ref, s_ref,
 ):
-    x, y = x_ref[...], y_ref[...]
+    x = xy_ref[:, : xr_ref.shape[1]]
     xr = operand(x * (2.0 * LOG2E), **SRC)
+    xr_ref[...] = xr.astype(BF)
+    xt_ref[...] = jnp.transpose(xr.astype(BF))
+    xsq_ref[...] = as_dense(jnp.sum(x * x, axis=0, keepdims=True))
+    y = xy_ref[:, xr_ref.shape[1] :]
     yr = operand(y, **TGT)
-    xr_ref[...] = xr.astype(BF)
     yr_ref[...] = yr.astype(BF)
-    xt_ref[...] = jnp.transpose(xr).astype(BF)
-    yt_ref[...] = jnp.transpose(yr).astype(BF)
-    xsq_ref[...] = as_dense(jnp.sum(x * x, axis=0, keepdims=True))
+    yt_ref[...] = jnp.transpose(yr.astype(BF))
     ysq = jnp.sum(y * y, axis=0, keepdims=True)
     ysq_ref[...] = as_dense(ysq)
     half_ref[...] = column_half(ysq * -LOG2E, 3, yt_ref)
     args = (yt_ref, half_ref, xr_ref, shift_ref)
     probe(*args, 0)
-    send_all(out_ref, as_dense(local_lse(*args, s_ref, 0)))
+    lse(out_ref, *args, s_ref, 0)
+
+
+def lse(out_ref, col_ref, half_ref, row_ref, shift_ref, s_ref, first):
+    args = (col_ref, half_ref, row_ref, shift_ref)
+    guarded(
+        lambda: sums(*args, s_ref, first),
+        lambda s: send_logs(out_ref, jnp.log2(s) - as_dense(shift_ref[...])),
+        s_ref,
+        *args,
+        first,
+    )
 
 
 def lse_kernel(
@@ -183,15 +206,14 @@
     new_ref, out_ref,
     half_ref, shift_ref, s_ref,
 ):
-    new = math.log2(total) - joined(parts_ref[...])
-    new_ref[...] = new
-    half_ref[...] = column_half(as_row(new), col_first, col_ref)
+    joined_rows(total, parts_ref, new_ref)
+    half_ref[...] = column_half(as_row(new_ref[...]), col_first, col_ref)
     args = (col_ref, half_ref, row_ref, shift_ref)
     if old_ref is None:
         probe(*args, row_first)
     else:
         shift_ref[...] = as_row(old_ref[...])
-    send_all(out_ref, as_dense(local_lse(*args, s_ref, row_first)))
+    lse(out_ref, *args, s_ref, row_first)
 
 
 def maps(col_ref, half_ref, row_ref, values_ref, shift_ref, moved_ref, first):
@@ -210,75 +232,129 @@
         moved_ref[:, cols] = total
 
 
-def potential_kernel(total, parts_ref, new_ref):
-    new_ref[...] = math.log2(total) - joined(parts_ref[...])
-
-
-def join_kernel(total, parts_ref, new_ref, share_ref):
-    parts = parts_ref[...]
-    logs = parts[:, : new_ref.shape[0]]
-    peak = jnp.max(logs, axis=0)
-    weights = jnp.exp2(logs - peak[None])
-    sum_w = jnp.sum(weights, axis=0)
-    new_ref[...] = math.log2(total) - (peak + jnp.log2(sum_w))
-    send_all(share_ref, share(parts, weights, sum_w))
-
-
-def image_kernel(
-    dims, scale, col_first, row_first,
+def image(dims, scale, send, out_ref, col_ref, half_ref, row_ref, values_ref, shift_ref, moved_ref, first):
+    one = first
+    n, cells = out_ref.shape[0], row_ref.shape[1] // HALF
+    groups = n * dims // DIM
+    args = (col_ref, half_ref, row_ref, shift_ref)
+
+    def finish(s):
+        log = jnp.log2(s) - as_dense(shift_ref[...])
+        base = send(out_ref, log, groups)
+        part = moved_ref[16:48, :] + moved_ref[48:80, :] + moved_ref[80:112, :]
+        part = part * (scale / as_row(s))
+        for k in range(n):
+            top, group = dims * (k // groups), k % groups
+            at = base
+            for cell in range(group, cells, groups):
+                for d in range(top, top + dims, 4):
+                    out_ref[k, at] = part[d : d + 4, HALF * cell : HALF * (cell + 1)]
+                    at += 1
+
+    guarded(
+        lambda: maps(col_ref, half_ref, row_ref, values_ref, shift_ref, moved_ref, first),
+        finish,
+        moved_ref.at[one : one + 1, :],
+        *args,
+        first,
+    )
+
+
+def send_all_logs(out_ref, log, groups):
+    send_logs(out_ref, log)
+    return log.shape[0] // 4
+
+
+def send_own_logs(out_ref, log, groups):
+    n, each = out_ref.shape[0], log.shape[0] // groups
+    blocks = -(-each // 4)
+    for group in range(groups):
+        rows = [log[c : c + 1] for c in range(group, log.shape[0], groups)]
+        rows = rows + [jnp.zeros_like(rows[0])] * (4 * blocks - each)
+        for b in range(blocks):
+            block = jnp.concatenate(rows[4 * b : 4 * b + 4], axis=0)
+            for k in range(group, n, groups):
+                out_ref[k, b] = block
+    return blocks
+
+
+def tgt_part_kernel(
+    total, dims,
+    parts_ref, col_ref, row_ref, values_ref, old_ref,
+    new_ref, out_ref,
+    half_ref, shift_ref, moved_ref,
+):
+    joined_rows(total, parts_ref, new_ref)
+    half_ref[...] = column_half(as_row(new_ref[...]), 0, col_ref)
+    shift_ref[...] = as_row(old_ref[...])
+    image(
+        dims, 0.5 * LN2, send_all_logs, out_ref,
+        col_ref, half_ref, row_ref, values_ref, shift_ref, moved_ref, 3,
+    )
+
+
+def src_part_kernel(
+    dims,
     new_ref, col_ref, row_ref, values_ref, old_ref,
     out_ref,
-    half_ref, shift_ref, moved_ref, image_ref,
+    half_ref, shift_ref, moved_ref,
 ):
-    rows = old_ref.shape[0]
-    half_ref[...] = column_half(as_row(new_ref[...]), col_first, col_ref)
+    half_ref[...] = column_half(as_row(new_ref[...]), 3, col_ref)
     shift_ref[...] = as_row(old_ref[...])
-    args = (col_ref, half_ref, row_ref)
-    maps(*args, values_ref, shift_ref, moved_ref, row_first)
-    one = 3 - col_first
-
-    @pl.when(outside(moved_ref[one : one + 1, :]))
-    def _():
-        peaks(*args, shift_ref, row_first, col_ref.shape[0])
-        maps(*args, values_ref, shift_ref, moved_ref, row_first)
-
-    s = moved_ref[one : one + 1, :]
-    log = jnp.log2(s) - shift_ref[...]
-    image = moved_ref[16:48, :] + moved_ref[48:80, :] + moved_ref[80:112, :]
-    image = image * (scale / s)
-    for r in range(rows):
-        image_ref[:, r, :] = image[:, HALF * r : HALF * (r + 1)]
-    n = out_ref.shape[0]
-    out_ref[:, :rows, :] = jnp.broadcast_to(as_dense(log)[None], (n, rows, HALF))
-    for d in range(dims):
-        for k in range(n):
-            out_ref[k, rows * (d + 1) : rows * (d + 2), :] = image_ref[k * dims + d]
-
-
-def share(parts, weights, sum_w):
-    rows = weights.shape[1]
-    out = []
-    for d in range(parts.shape[1] // rows - 1):
-        part = parts[:, rows * (d + 1) : rows * (d + 2)]
-        out.append(jnp.sum(part * weights, axis=0) / sum_w)
-    return jnp.concatenate(out, axis=0)
-
-
-def share_kernel(rows, parts_ref, out_ref):
-    parts = parts_ref[...]
-    logs = parts[:, :rows]
-    weights = jnp.exp2(logs - jnp.max(logs, axis=0)[None])
-    send_all(out_ref, share(parts, weights, jnp.sum(weights, axis=0)))
+    image(
+        dims, 1.0, send_own_logs, out_ref,
+        col_ref, half_ref, row_ref, values_ref, shift_ref, moved_ref, 0,
+    )
+
+
+def share(parts_ref, out_ref, base, dims, logs_of):
+    n, blocks = out_ref.shape[:2]
+    each = dims // 4
+    for c in range(blocks // each):
+        logs = logs_of(c)
+        weights = jnp.exp2(logs - jnp.max(logs, axis=0)[None])
+        weights = weights / jnp.sum(weights, axis=0)[None]
+        for u in range(each):
+            at = c * each + u
+            part = jnp.sum(parts_ref[:, base + at] * weights, axis=0)
+            out_ref[:, at] = jnp.broadcast_to(part[None], (n, 4, HALF))
+
+
+def tgt_join_kernel(total, dims, groups, parts_ref, new_ref, out_ref):
+    logs_ref = parts_ref.at[:, : new_ref.shape[0] // 4]
+    joined_rows(total, logs_ref, new_ref)
+    group = lax.rem(lax.axis_index("row"), groups)
+
+    def logs_of(c):
+        cell = groups * c + group
+        return logs_ref[:, cell // 4, pl.ds(lax.rem(cell, 4), 1), :]
+
+    share(parts_ref, out_ref, new_ref.shape[0] // 4, dims, logs_of)
+
+
+def src_share_kernel(dims, parts_ref, out_ref):
+    base = parts_ref.shape[1] - out_ref.shape[1]
+    share(
+        parts_ref, out_ref, base, dims, lambda c: parts_ref[:, c // 4, c % 4 : c % 4 + 1, :]
+    )
 
 
 def end_kernel(
-    e_ref, h_ref, xsq_ref, ysq_ref, src_ref, tgt_ref, f_ref, g_ref, si_ref, ti_ref
+    dims_of, e_ref, h_ref, xsq_ref, ysq_ref, src_ref, tgt_ref, f_ref, g_ref, si_ref, ti_ref
 ):
     f_ref[...] = LN2 * e_ref[...] + xsq_ref[...]
     g_ref[...] = LN2 * h_ref[...] + ysq_ref[...]
     for parts_ref, out_ref in ((src_ref, si_ref), (tgt_ref, ti_ref)):
-        for r in range(parts_ref.shape[1]):
-            out_ref[:, HALF * r : HALF * (r + 1)] = parts_ref[:, r, :]
+        n, blocks = parts_ref.shape[:2]
+        cells = out_ref.shape[1] // HALF
+        dims = dims_of[0] if out_ref is si_ref else dims_of[1]
+        groups = n * dims // DIM
+        for k in range(n):
+            top, at = dims * (k // groups), 0
+            for cell in range(k % groups, cells, groups):
+                for d in range(top, top + dims, 4):
+                    out_ref[d : d + 4, HALF * cell : HALF * (cell + 1)] = parts_ref[k, at]
+                    at += 1
 
 
 def shape(*dims, dtype=F32):
@@ -302,17 +378,20 @@
     n_row, n_col = lax.axis_size("row"), lax.axis_size("col")
     rs, rt = ns // HALF, nt // HALF
     all_src, all_tgt = ns * n_row, nt * n_col
-    dim_src, dim_tgt = x.shape[0] // n_col, x.shape[0] // n_row
-
-    def scratch(m, n):
-        return (pltpu.VMEM((m, HALF), BF), pltpu.VMEM((1, n), F32), pltpu.VMEM((1, n), F32))
+    dim_src, dim_tgt = DIM // min(n_col, 4), DIM // min(n_row, 8)
+    grp_src, grp_tgt = n_col * dim_src // DIM, n_row * dim_tgt // DIM
+    blk_src, blk_tgt = ns * DIM // n_col // 512, nt * DIM // n_row // 512
+    log_src = -(-rs // grp_src // 4)
+
+    def scratch(m, n, rows=1):
+        return (pltpu.VMEM((m, HALF), BF), pltpu.VMEM((1, n), F32), pltpu.VMEM((rows, n), F32))
 
     def over(axis, v):
         return lax.all_to_all(v, axis, 0, 0)
 
     xt, yt, xr, yr, xsq, ysq, parts = call(
         start_kernel,
-        (x, y),
+        (jnp.concatenate([x, y], axis=1),),
         (
             shape(ns, DEPTH, dtype=BF),
             shape(nt, DEPTH, dtype=BF),
@@ -320,7 +399,7 @@
             shape(DEPTH, nt, dtype=BF),
             shape(rs, HALF),
             shape(rt, HALF),
-            shape(n_col, rs, HALF),
+            shape(n_col, rs // 8, 8, HALF),
         ),
         scratch(nt, ns),
         name="start",
@@ -336,57 +415,54 @@
         else:
             ins += (h,)
         e, parts = call(
-            kernel, ins, (shape(rs, HALF), shape(n_row, rt, HALF)), scratch(ns, nt), name="cols"
+            kernel,
+            ins,
+            (shape(rs, HALF), shape(n_row, rt // 4, 4, HALF)),
+            scratch(ns, nt),
+            name="cols",
         )
         parts = over("row", parts)
         h, parts = call(
             functools.partial(lse_kernel, all_src, 3, 0),
             (parts, yt, xr, e),
-            (shape(rt, HALF), shape(n_col, rs, HALF)),
+            (shape(rt, HALF), shape(n_col, rs // 8, 8, HALF)),
             scratch(nt, ns),
             name="rows",
         )
-
-    def image_scratch(m, n):
-        return scratch(m, n)[:2] + (
-            pltpu.VMEM((HALF, n), F32),
-            pltpu.VMEM((x.shape[0], n // HALF, HALF), F32),
-        )
-
     parts = over("col", parts)
-    e = call(functools.partial(potential_kernel, all_tgt), (parts,), shape(rs, HALF), name="src_join")
-    parts = call(
-        functools.partial(image_kernel, dim_tgt, 0.5 * LN2, 0, 3),
-        (e, xt, yr, xr, h),
-        shape(n_row, rt * (1 + dim_tgt), HALF),
-        image_scratch(ns, nt),
+    e, parts = call(
+        functools.partial(tgt_part_kernel, all_tgt, dim_tgt),
+        (parts, xt, yr, xr, h),
+        (shape(rs, HALF), shape(n_row, rt // 4 + blk_tgt, 4, HALF)),
+        scratch(ns, nt, HALF),
         name="tgt_part",
     )
     parts = over("row", parts)
     h, tgt = call(
-        functools.partial(join_kernel, all_src),
+        functools.partial(tgt_join_kernel, all_src, dim_tgt, grp_tgt),
         (parts,),
-        (shape(rt, HALF), shape(n_row, rt * dim_tgt, HALF)),
+        (shape(rt, HALF), shape(n_row, blk_tgt, 4, HALF)),
         name="tgt_join",
     )
-    tgt = over("row", tgt).reshape(x.shape[0], rt, HALF)
+    tgt = over("row", tgt)
     parts = call(
-        functools.partial(image_kernel, dim_src, 1.0, 3, 0),
+        functools.partial(src_part_kernel, dim_src),
         (h, yt, xr, yr, e),
-        shape(n_col, rs * (1 + dim_src), HALF),
-        image_scratch(nt, ns),
+        shape(n_col, log_src + blk_src, 4, HALF),
+        scratch(nt, ns, HALF),
         name="src_part",
     )
+    parts, tgt = lax.optimization_barrier((parts, tgt))
     parts = over("col", parts)
     src = call(
-        functools.partial(share_kernel, rs),
+        functools.partial(src_share_kernel, dim_src),
         (parts,),
-        shape(n_col, rs * dim_src, HALF),
+        shape(n_col, blk_src, 4, HALF),
         name="src_share",
     )
-    src = over("col", src).reshape(x.shape[0], rs, HALF)
+    src = over("col", src)
     f, g, si, ti = call(
-        end_kernel,
+        functools.partial(end_kernel, (dim_src, dim_tgt)),
         (e, h, xsq, ysq, src, tgt),
         (shape(rs, HALF), shape(rt, HALF), shape(*x.shape), shape(*y.shape)),
         name="end",

time: 213 us -> 201 us (0.944)
  the two profiles are of different devices: /device:TPU:6 before, /device:TPU:4 now
where the time goes in v3:
time: 201 us
  blocking collectives  136 us (68%)
  Pallas kernels  57.3 us (29%)
  starting transfers between devices  5.58 us (3%)
    all_to_all x8, blocking collectives, over(): return lax.all_to_all(v, axis, 0, 0)  136 us
    pallas_call x10, Pallas kernels, call(): pl.pallas_call(kernel, out_shape=outs, in_specs=[VMEM] * len(ins), out_sp...  57.3 us
    all_to_all x1, starting transfers between devices, over(): return lax.all_to_all(v, axis, 0, 0)  5.58 us
  transfers between devices with their start and end apart: 1, of which 0 were waited for; matrix products, arithmetic and copies ran while one was open for 0% of the time, Pallas kernels for 5%

profile of v3, /device:TPU:4, one launch (start us, length us, event | category | flops | bytes accessed | tf_op | source)
XLA Modules:
  0.0 200.8 jit_solution(18439182053804171684)
XLA Ops:
  0.6 1.0 pad_maximum_fusion.xy_ref
  1.7 7.5 %start.1 = (bf16[1024,256]{1,0:T(8,128)(2,1)S(1)}, bf16[1536,256]{1,0:T(8,128)(2,1)S(1)}, bf16[256,1024]{1,0:T(8,128)(2,1)S(1)}, bf16[256,1536]{1,0:T(8,128)(2,1...) custom-call(f32[32,2560]{1,0:T(8,128)S(1)} %pad_maximum_fusion.xy_ref), custom_call_target="tpu_custom_call" | custom-call | tf_op jit(solution)/shard_map/start/pallas_call | solution.py:365
  9.1 27.7 %all_to_all.45.p = f32[16,1,8,128]{3,2,1,0:T(8,128)S(1)} all-to-all(f32[16,1,8,128]{3,2,1,0:T(8,128)S(1)} %get-tuple-element.29), channel_id=1, replica_groups=mesh['row'=32,'col'=16] {'col'}, dimensions={0} | all-to-all | bytes 131072 | tf_op jit(solution)/shard_map/all_to_all | solution.py:390
  36.8 7.4 %cols.2 = (f32[8,128]{1,0:T(8,128)S(1)}, f32[32,3,4,128]{3,2,1,0:T(4,128)S(1)}) custom-call(f32[16,1,8,128]{3,2,1,0:T(8,128)S(1)} %all_to_all.45.p, bf16[1024,256]{1,0:T(8,128)(2,1)S(1)} %get-tuple-element.30.c.col_ref, bf16[256,1536]{1,0:T(8,128)(2,1)S(1)} %get-tuple-element.31.r.row_ref.values_ref), custom_call_target="tpu_custom_call" | custom-call | tf_op jit(solution)/shard_map/cols/pallas_call | solution.py:365
  44.3 13.8 %all_to_all.46.parts_ref = f32[32,3,4,128]{3,2,1,0:T(4,128)S(1)} all-to-all(f32[32,3,4,128]{3,2,1,0:T(4,128)S(1)} %get-tuple-element.32), channel_id=1, replica_groups=mesh['row'=32,'col'=16] {'row'}, dimensions={0} | all-to-all | bytes 393216 | tf_op jit(solution)/shard_map/all_to_all | solution.py:390
  58.0 7.3 %rows.2 = (f32[12,128]{1,0:T(8,128)S(1)}, f32[16,1,8,128]{3,2,1,0:T(8,128)S(1)}) custom-call(f32[32,3,4,128]{3,2,1,0:T(4,128)S(1)} %all_to_all.46.parts_ref, bf16[1536,256]{1,0:T(8,128)(2,1)S(1)} %get-tuple-element.33.col_ref, bf16[256,1024]{1,0:T(8,128)(2,1)S(1)} %get-tuple-element.34.row_ref.values_ref, f32[8,128]{1,0:T(8,128)S(1)} %get-tuple-element.35.old_ref), custom_call_target="tpu_custom_call" | custom-call | tf_op jit(solution)/shard_map/rows/pallas_call | solution.py:365
  65.3 15.9 %all_to_all.47.parts_ref = f32[16,1,8,128]{3,2,1,0:T(8,128)S(1)} all-to-all(f32[16,1,8,128]{3,2,1,0:T(8,128)S(1)} %get-tuple-element.36), channel_id=1, replica_groups=mesh['row'=32,'col'=16] {'col'}, dimensions={0} | all-to-all | bytes 131072 | tf_op jit(solution)/shard_map/all_to_all | solution.py:390
  81.3 7.3 %cols.3 = (f32[8,128]{1,0:T(8,128)S(1)}, f32[32,3,4,128]{3,2,1,0:T(4,128)S(1)}) custom-call(f32[16,1,8,128]{3,2,1,0:T(8,128)S(1)} %all_to_all.47.parts_ref, bf16[1024,256]{1,0:T(8,128)(2,1)S(1)} %get-tuple-element.30.c.col_ref, bf16[256,1536]{1,0:T(8,128)(2,1)S(1)} %get-tuple-element.31.r.row_ref.values_ref, f32[12,128]{1,0:T(8,128)S(1)} %get-tuple-element.37.old_ref), custom_call_target="tpu_custom_call" | custom-call | tf_op jit(solution)/shard_map/cols/pallas_call | solution.py:365
  88.6 11.7 %all_to_all.48.parts_ref = f32[32,3,4,128]{3,2,1,0:T(4,128)S(1)} all-to-all(f32[32,3,4,128]{3,2,1,0:T(4,128)S(1)} %get-tuple-element.38), channel_id=1, replica_groups=mesh['row'=32,'col'=16] {'row'}, dimensions={0} | all-to-all | bytes 393216 | tf_op jit(solution)/shard_map/all_to_all | solution.py:390
  100.3 7.5 %rows.3 = (f32[12,128]{1,0:T(8,128)S(1)}, f32[16,1,8,128]{3,2,1,0:T(8,128)S(1)}) custom-call(f32[32,3,4,128]{3,2,1,0:T(4,128)S(1)} %all_to_all.48.parts_ref, bf16[1536,256]{1,0:T(8,128)(2,1)S(1)} %get-tuple-element.33.col_ref, bf16[256,1024]{1,0:T(8,128)(2,1)S(1)} %get-tuple-element.34.row_ref.values_ref, f32[8,128]{1,0:T(8,128)S(1)} %get-tuple-element.39.old_ref), custom_call_target="tpu_custom_call" | custom-call | tf_op jit(solution)/shard_map/rows/pallas_call | solution.py:365
  107.8 15.9 %all_to_all.49.parts_ref = f32[16,1,8,128]{3,2,1,0:T(8,128)S(1)} all-to-all(f32[16,1,8,128]{3,2,1,0:T(8,128)S(1)} %get-tuple-element.40), channel_id=1, replica_groups=mesh['row'=32,'col'=16] {'col'}, dimensions={0} | all-to-all | bytes 131072 | tf_op jit(solution)/shard_map/all_to_all | solution.py:390
  123.7 9.3 %tgt_part.1 = (f32[8,128]{1,0:T(8,128)S(1)}, f32[32,6,4,128]{3,2,1,0:T(4,128)S(1)}) custom-call(f32[16,1,8,128]{3,2,1,0:T(8,128)S(1)} %all_to_all.49.parts_ref, bf16[1024,256]{1,0:T(8,128)(2,1)S(1)} %get-tuple-element.30.c.col_ref, bf16[256,1536]{1,0:T(8,128)(2,1)S(1)} %get-tuple-element.31.r.row_ref.values_ref, ...), custom_call_target="tpu_custom_call" | custom-call | tf_op jit(solution)/shard_map/tgt_part/pallas_call | solution.py:365
  133.0 13.5 %all_to_all.50.parts_ref = f32[32,6,4,128]{3,2,1,0:T(4,128)S(1)} all-to-all(f32[32,6,4,128]{3,2,1,0:T(4,128)S(1)} %get-tuple-element.43), channel_id=1, replica_groups=mesh['row'=32,'col'=16] {'row'}, dimensions={0} | all-to-all | bytes 786432 | tf_op jit(solution)/shard_map/all_to_all | solution.py:390
  146.5 0.9 tgt_join.1
  147.4 5.6 %all-to-all-start.6 = ((f32[32,3,4,128]{3,2,1,0:T(4,128)}), f32[32,3,4,128]{3,2,1,0:T(4,128)S(1)}, u32[]{:S(2)}, u32[]{:S(2)}) async-start(f32[32,3,4,128]{3,2,1,0:T(4,128)} %get-tuple-element.47), calls=%async_computation.6 | async-start | bytes 393216 | tf_op jit(solution)/shard_map/all_to_all | solution.py:390
  153.0 9.2 %src_part.1 = f32[16,5,4,128]{3,2,1,0:T(4,128)S(1)} custom-call(f32[12,128]{1,0:T(8,128)S(1)} %get-tuple-element.44.new_ref.h_ref, bf16[1536,256]{1,0:T(8,128)(2,1)S(1)} %get-tuple-element.33.col_ref, bf16[256,1024]{1,0:T(8,128)(2,1)S(1)} %get-tuple-element.34.row_ref.values_ref, bf16[256,1536]{1,0:T(8,128)(2,1)S(1)} %get-tuple-element.31.r.row_ref.values_ref, ...), custom_call_target="tpu_custom_call" | custom-call | tf_op jit(solution)/shard_map/src_part/pallas_call | solution.py:365
  162.2 0.0 all-to-all-done.6.tgt_ref
  162.2 18.1 %all_to_all.51.parts_ref = f32[16,5,4,128]{3,2,1,0:T(4,128)S(1)} all-to-all(f32[16,5,4,128]{3,2,1,0:T(4,128)S(1)} %src_part.1), channel_id=1, replica_groups=mesh['row'=32,'col'=16] {'col'}, dimensions={0} | all-to-all | bytes 327680 | tf_op jit(solution)/shard_map/all_to_all | solution.py:390
  180.3 0.1 src_share.1
  180.4 19.5 %all_to_all.52.src_ref = f32[16,4,4,128]{3,2,1,0:T(4,128)S(1)} all-to-all(f32[16,4,4,128]{3,2,1,0:T(4,128)S(1)} %src_share.1), channel_id=1, replica_groups=mesh['row'=32,'col'=16] {'col'}, dimensions={0} | all-to-all | bytes 262144 | tf_op jit(solution)/shard_map/all_to_all | solution.py:390
  200.0 0.8 end.1
Async XLA Ops:
  147.4 14.8 %all-to-all-start.6 = ((f32[32,3,4,128]{3,2,1,0:T(4,128)}), f32[32,3,4,128]{3,2,1,0:T(4,128)S(1)}, u32[]{:S(2)}, u32[]{:S(2)}) async-start(f32[32,3,4,128]{3,2,1,0:T(4,128)} %get-tuple-element.47), calls=%async_computation.6 | async-start | bytes 393216 | tf_op jit(solution)/shard_map/all_to_all | solution.py:390

commit v4 on v3

--- a/solution.py
+++ b/solution.py
@@ -16,10 +16,12 @@
 DIM = 32
 TILE = 256
 CHUNK = 256
+UNROLL = 8
 PROBE = 64
 LOW, HIGH = 2.0**-90, 2.0**100
 BF, F32 = jnp.bfloat16, jnp.float32
 VMEM = pl.BlockSpec(memory_space=pltpu.VMEM)
+HBM = pl.BlockSpec(memory_space=pltpu.HBM)
 
 
 def rounded(v):
@@ -74,13 +76,17 @@
 TGT = dict(order1=(0, 1, 0), order2=(2, 0, 1), first=3)
 
 
-def column_half(v, first, static_ref):
+def column_part(v, first):
     rows = potential_rows(v, first)
     n = v.shape[1]
     keep = lax.broadcasted_iota(jnp.int32, (8, n), 0)
     rows = jnp.where((keep >= first) & (keep < first + 3), rows, 0.0)
     wide = jnp.concatenate([rows, jnp.zeros((HALF - 8, n), F32)], axis=0)
-    return static_ref[:, HALF:] + jnp.transpose(wide.astype(BF))
+    return jnp.transpose(wide.astype(BF))
+
+
+def column_half(v, first, static_ref):
+    return static_ref[:, HALF:] + column_part(v, first)
 
 
 def tile_of(row_ref, block, start):
@@ -108,20 +114,37 @@
         s_ref[:, cols] = jnp.sum(acc, axis=0, keepdims=True)
 
 
+def fold(col_ref, half_ref, row_ref, shift_ref, out_ref, first, shifted, start, step, end):
+    @pl.loop(0, row_ref.shape[1] // TILE)
+    def _(t):
+        at = pl.multiple_of(t * TILE, TILE)
+        cols = pl.ds(at, TILE)
+        shift = shift_ref[:, cols] if shifted else jnp.zeros((1, TILE), F32)
+        rhs = tile_of(row_ref, row_block(shift, first), at)
+
+        def chunk(c, acc):
+            c = pl.multiple_of(c * CHUNK, CHUNK)
+            return step(c, acc, scores(col_ref, half_ref, c, rhs))
+
+        out_ref[:, cols] = end(lax.fori_loop(0, col_ref.shape[0] // CHUNK, chunk, start))
+
+
 def peaks(col_ref, half_ref, row_ref, shift_ref, first):
-    count, n = col_ref.shape[0], row_ref.shape[1]
-
-    @pl.loop(0, n // TILE)
-    def _(t):
-        start = pl.multiple_of(t * TILE, TILE)
-        rhs = tile_of(row_ref, row_block(jnp.zeros((1, TILE), F32), first), start)
-
-        def step(c, acc):
-            s = scores(col_ref, half_ref, pl.multiple_of(c * CHUNK, CHUNK), rhs)
-            return jnp.maximum(acc, jnp.max(s.reshape(CHUNK // 8, 8, TILE), axis=0))
-
-        acc = lax.fori_loop(0, count // CHUNK, step, jnp.full((8, TILE), -jnp.inf, F32))
-        shift_ref[:, pl.ds(start, TILE)] = -jnp.max(acc, axis=0, keepdims=True)
+    fold(
+        col_ref, half_ref, row_ref, shift_ref, shift_ref, first, False,
+        jnp.full((8, TILE), -jnp.inf, F32),
+        lambda c, acc, s: jnp.maximum(acc, jnp.max(s.reshape(CHUNK // 8, 8, TILE), axis=0)),
+        lambda acc: -jnp.max(acc, axis=0, keepdims=True),
+    )
+
+
+def slow_sums(col_ref, half_ref, row_ref, shift_ref, s_ref, first):
+    fold(
+        col_ref, half_ref, row_ref, shift_ref, s_ref, first, True,
+        jnp.zeros((8, TILE), F32),
+        lambda c, acc, s: acc + jnp.sum(jnp.exp2(s).reshape(CHUNK // 8, 8, TILE), axis=0),
+        lambda acc: jnp.sum(acc, axis=0, keepdims=True),
+    )
 
 
 def probe(col_ref, half_ref, row_ref, shift_ref, first):
@@ -136,7 +159,7 @@
     return jnp.any(jnp.logical_not((s > LOW) & (s < HIGH)))
 
 
-def guarded(compute, finish, sum_ref, col_ref, half_ref, row_ref, shift_ref, first):
+def guarded(compute, redo, finish, sum_ref, col_ref, half_ref, row_ref, shift_ref, first):
     compute()
     s = as_dense(sum_ref[...])
     finish(s)
@@ -144,7 +167,7 @@
     @pl.when(outside(s))
     def _():
         peaks(col_ref, half_ref, row_ref, shift_ref, first)
-        compute()
+        redo()
         finish(as_dense(sum_ref[...]))
 
 
@@ -193,6 +216,7 @@
     args = (col_ref, half_ref, row_ref, shift_ref)
     guarded(
         lambda: sums(*args, s_ref, first),
+        lambda: slow_sums(*args, s_ref, first),
         lambda s: send_logs(out_ref, jnp.log2(s) - as_dense(shift_ref[...])),
         s_ref,
         *args,
@@ -216,20 +240,34 @@
     lse(out_ref, *args, s_ref, row_first)
 
 
-def maps(col_ref, half_ref, row_ref, values_ref, shift_ref, moved_ref, first):
+def weighted(score, values):
+    w = jnp.exp2(score)
+    high = w.astype(BF)
+    low = (w - high.astype(F32)).astype(BF)
+    return jnp.dot(values, high, preferred_element_type=F32) + jnp.dot(
+        values, low, preferred_element_type=F32
+    )
+
+
+def maps(col_ref, half_ref, row_ref, shift_ref, values_ref, moved_ref, first):
     count, n = col_ref.shape[0], row_ref.shape[1]
     for t in range(n // TILE):
         cols = slice(t * TILE, (t + 1) * TILE)
         rhs = tile_of(row_ref, row_block(shift_ref[:, cols], first), t * TILE)
         total = jnp.zeros((HALF, TILE), F32)
         for c in range(count // CHUNK):
-            w = jnp.exp2(scores(col_ref, half_ref, c * CHUNK, rhs))
-            high = w.astype(BF)
-            low = (w - high.astype(F32)).astype(BF)
             values = values_ref[HALF:, c * CHUNK : (c + 1) * CHUNK]
-            total += jnp.dot(values, high, preferred_element_type=F32)
-            total += jnp.dot(values, low, preferred_element_type=F32)
+            total += weighted(scores(col_ref, half_ref, c * CHUNK, rhs), values)
         moved_ref[:, cols] = total
+
+
+def slow_maps(col_ref, half_ref, row_ref, shift_ref, values_ref, moved_ref, first):
+    fold(
+        col_ref, half_ref, row_ref, shift_ref, moved_ref, first, True,
+        jnp.zeros((HALF, TILE), F32),
+        lambda c, acc, s: acc + weighted(s, values_ref[HALF:, pl.ds(c, CHUNK)]),
+        lambda acc: acc,
+    )
 
 
 def image(dims, scale, send, out_ref, col_ref, half_ref, row_ref, values_ref, shift_ref, moved_ref, first):
@@ -252,7 +290,8 @@
                     at += 1
 
     guarded(
-        lambda: maps(col_ref, half_ref, row_ref, values_ref, shift_ref, moved_ref, first),
+        lambda: maps(*args, values_ref, moved_ref, first),
+        lambda: slow_maps(*args, values_ref, moved_ref, first),
         finish,
         moved_ref.at[one : one + 1, :],
         *args,
@@ -263,19 +302,6 @@
 def send_all_logs(out_ref, log, groups):
     send_logs(out_ref, log)
     return log.shape[0] // 4
-
-
-def send_own_logs(out_ref, log, groups):
-    n, each = out_ref.shape[0], log.shape[0] // groups
-    blocks = -(-each // 4)
-    for group in range(groups):
-        rows = [log[c : c + 1] for c in range(group, log.shape[0], groups)]
-        rows = rows + [jnp.zeros_like(rows[0])] * (4 * blocks - each)
-        for b in range(blocks):
-            block = jnp.concatenate(rows[4 * b : 4 * b + 4], axis=0)
-            for k in range(group, n, groups):
-                out_ref[k, b] = block
-    return blocks
 
 
 def tgt_part_kernel(
@@ -293,25 +319,19 @@
     )
 
 
-def src_part_kernel(
-    dims,
-    new_ref, col_ref, row_ref, values_ref, old_ref,
-    out_ref,
-    half_ref, shift_ref, moved_ref,
-):
-    half_ref[...] = column_half(as_row(new_ref[...]), 3, col_ref)
-    shift_ref[...] = as_row(old_ref[...])
-    image(
-        dims, 1.0, send_own_logs, out_ref,
-        col_ref, half_ref, row_ref, values_ref, shift_ref, moved_ref, 0,
-    )
-
-
-def share(parts_ref, out_ref, base, dims, logs_of):
+def tgt_join_kernel(total, parts_ref, new_ref, out_ref):
+    joined_rows(total, parts_ref.at[:, : new_ref.shape[0] // 4], new_ref)
+    send_logs(out_ref, new_ref[...])
+
+
+def tgt_share_kernel(dims, groups, parts_ref, out_ref):
     n, blocks = out_ref.shape[:2]
     each = dims // 4
+    base = parts_ref.shape[1] - blocks
+    group = lax.rem(lax.axis_index("row"), groups)
     for c in range(blocks // each):
-        logs = logs_of(c)
+        cell = groups * c + group
+        logs = parts_ref[:, cell // 4, pl.ds(lax.rem(cell, 4), 1), :]
         weights = jnp.exp2(logs - jnp.max(logs, axis=0)[None])
         weights = weights / jnp.sum(weights, axis=0)[None]
         for u in range(each):
@@ -320,52 +340,131 @@
             out_ref[:, at] = jnp.broadcast_to(part[None], (n, 4, HALF))
 
 
-def tgt_join_kernel(total, dims, groups, parts_ref, new_ref, out_ref):
-    logs_ref = parts_ref.at[:, : new_ref.shape[0] // 4]
-    joined_rows(total, logs_ref, new_ref)
-    group = lax.rem(lax.axis_index("row"), groups)
-
-    def logs_of(c):
-        cell = groups * c + group
-        return logs_ref[:, cell // 4, pl.ds(lax.rem(cell, 4), 1), :]
-
-    share(parts_ref, out_ref, new_ref.shape[0] // 4, dims, logs_of)
-
-
-def src_share_kernel(dims, parts_ref, out_ref):
-    base = parts_ref.shape[1] - out_ref.shape[1]
-    share(
-        parts_ref, out_ref, base, dims, lambda c: parts_ref[:, c // 4, c % 4 : c % 4 + 1, :]
-    )
+def src_scratch(count, n_blocks, width):
+    return (
+        pltpu.VMEM((DEPTH, count), BF),
+        pltpu.VMEM((count // HALF, HALF), F32),
+        pltpu.VMEM((HALF, count), F32),
+    )
+
+
+def src_map_kernel(
+    h_ref, y_hbm, xr_ref, e_ref,
+    out_ref,
+    row_ref, shift_ref, moved_ref, y_ref, sems,
+):
+    n_blocks, _, width = y_ref.shape
+    each = math.gcd(n_blocks, UNROLL)
+    copies = [
+        pltpu.make_async_copy(
+            y_hbm.at[pl.ds(k, each)], y_ref.at[pl.ds(k, each)], sems.at[k // each]
+        )
+        for k in range(0, n_blocks, each)
+    ]
+    for copy in copies:
+        copy.start()
+    count = row_ref.shape[1]
+    pieces = count // HALF
+    group = lax.rem(lax.axis_index("col"), out_ref.shape[0])
+    cols = pl.ds(pl.multiple_of(group * count, count), count)
+    one, two, three = xr_ref[0:32, cols], xr_ref[64:96, cols], xr_ref[176:208, cols]
+    zero = jnp.zeros((16, count), BF)
+    row_ref[...] = jnp.concatenate(
+        [one, one, one, zero, zero, two, two, three, zero, zero], axis=0
+    )
+    row_ref[96:112, :] = xr_ref[128:144, cols]
+
+    def chunk_of(block, t):
+        y = y_ref[block, :, TILE * t : TILE * (t + 1)]
+        first = TILE // HALF * t
+        h = jnp.concatenate(
+            [h_ref[block, c // 4, c % 4 : c % 4 + 1, :] for c in range(first, first + TILE // HALF)],
+            axis=1,
+        )
+        values = jnp.concatenate(
+            [v.astype(BF) for v in split(y)] + [row_block(h, 3), jnp.zeros((16, TILE), BF)], axis=0
+        )
+        again = jnp.concatenate([values[:64], values[:64]], axis=0)
+        return values, jnp.concatenate([jnp.transpose(values), jnp.transpose(again)], axis=1)
+
+    def step(block, total):
+        rhs = row_ref[...]
+        for t in range(width // TILE):
+            values, lhs = chunk_of(block, t)
+            total += weighted(jnp.dot(lhs, rhs, preferred_element_type=F32), values)
+        return total
+
+    def maps(arrived):
+        shift = as_row(shift_ref[...])
+        row_ref[96:112, :] = row_block(shift, 0)
+        moved_ref[...] = jnp.zeros((HALF, count), F32)
+
+        @pl.loop(0, n_blocks, step=each)
+        def _(block):
+            if not arrived:
+                pltpu.make_async_copy(
+                    y_hbm.at[pl.ds(block, each)], y_ref.at[pl.ds(block, each)], sems.at[block // each]
+                ).wait()
+            total = moved_ref[...]
+            for k in range(each):
+                total = step(block + k, total)
+            moved_ref[...] = total
+
+        s = moved_ref[96:97, :]
+        part = moved_ref[0:32, :] + moved_ref[32:64, :] + moved_ref[64:96, :]
+        part = part / s
+        for k in range(pieces):
+            for d in range(4):
+                block = part[8 * d : 8 * d + 8, HALF * k : HALF * (k + 1)]
+                out_ref[:, 4 * k + d] = jnp.broadcast_to(block[None], (out_ref.shape[0], 8, HALF))
+        return as_dense(s)
+
+    def peaks(block, top):
+        for t in range(width // TILE):
+            s = jnp.dot(chunk_of(block, t)[1], row_ref[...], preferred_element_type=F32)
+            top = jnp.maximum(top, jnp.max(s.reshape(TILE // 8, 8, count), axis=0))
+        return top
+
+    shift_ref[...] = e_ref[pl.ds(group * pieces, pieces), :]
+    s = maps(False)
+
+    @pl.when(outside(s))
+    def _():
+        row_ref[96:112, :] = xr_ref[128:144, cols]
+        top = lax.fori_loop(0, n_blocks, peaks, jnp.full((8, count), -jnp.inf, F32))
+        shift_ref[...] = as_dense(-jnp.max(top, axis=0, keepdims=True))
+        maps(True)
 
 
 def end_kernel(
-    dims_of, e_ref, h_ref, xsq_ref, ysq_ref, src_ref, tgt_ref, f_ref, g_ref, si_ref, ti_ref
+    dims, e_ref, h_ref, xsq_ref, ysq_ref, src_ref, tgt_ref, f_ref, g_ref, si_ref, ti_ref
 ):
     f_ref[...] = LN2 * e_ref[...] + xsq_ref[...]
     g_ref[...] = LN2 * h_ref[...] + ysq_ref[...]
-    for parts_ref, out_ref in ((src_ref, si_ref), (tgt_ref, ti_ref)):
-        n, blocks = parts_ref.shape[:2]
-        cells = out_ref.shape[1] // HALF
-        dims = dims_of[0] if out_ref is si_ref else dims_of[1]
-        groups = n * dims // DIM
-        for k in range(n):
-            top, at = dims * (k // groups), 0
-            for cell in range(k % groups, cells, groups):
-                for d in range(top, top + dims, 4):
-                    out_ref[d : d + 4, HALF * cell : HALF * (cell + 1)] = parts_ref[k, at]
-                    at += 1
+    n, blocks = src_ref.shape[:2]
+    for p in range(n):
+        for at in range(blocks):
+            d, cell = 8 * (at % 4), HALF * (p * blocks // 4 + at // 4)
+            si_ref[d : d + 8, cell : cell + HALF] = src_ref[p, at]
+    n, cells = tgt_ref.shape[0], ti_ref.shape[1] // HALF
+    groups = n * dims // DIM
+    for p in range(n):
+        top, at = dims * (p // groups), 0
+        for cell in range(p % groups, cells, groups):
+            for d in range(top, top + dims, 4):
+                ti_ref[d : d + 4, HALF * cell : HALF * (cell + 1)] = tgt_ref[p, at]
+                at += 1
 
 
 def shape(*dims, dtype=F32):
     return jax.ShapeDtypeStruct(dims, dtype)
 
 
-def call(kernel, ins, outs, scratch=(), name=None):
+def call(kernel, ins, outs, scratch=(), name=None, hbm=()):
     return pl.pallas_call(
         kernel,
         out_shape=outs,
-        in_specs=[VMEM] * len(ins),
+        in_specs=[HBM if k in hbm else VMEM for k in range(len(ins))],
         out_specs=jax.tree.map(lambda _: VMEM, outs),
         scratch_shapes=list(scratch),
         compiler_params=pltpu.CompilerParams(vmem_limit_bytes=32 * 2**20),
@@ -378,16 +477,19 @@
     n_row, n_col = lax.axis_size("row"), lax.axis_size("col")
     rs, rt = ns // HALF, nt // HALF
     all_src, all_tgt = ns * n_row, nt * n_col
-    dim_src, dim_tgt = DIM // min(n_col, 4), DIM // min(n_row, 8)
-    grp_src, grp_tgt = n_col * dim_src // DIM, n_row * dim_tgt // DIM
-    blk_src, blk_tgt = ns * DIM // n_col // 512, nt * DIM // n_row // 512
-    log_src = -(-rs // grp_src // 4)
+    dims = DIM // min(n_row, 8)
+    groups = n_row * dims // DIM
+    blocks = nt * DIM // n_row // 512
+    near = min(n_col, 4)
+    quarter = ns // near
 
     def scratch(m, n, rows=1):
         return (pltpu.VMEM((m, HALF), BF), pltpu.VMEM((1, n), F32), pltpu.VMEM((rows, n), F32))
 
-    def over(axis, v):
-        return lax.all_to_all(v, axis, 0, 0)
+    def over(axis, v, groups=None):
+        return lax.all_to_all(v, axis, 0, 0, axis_index_groups=groups)
+
+    every_y = lax.all_gather(y, "col")
 
     xt, yt, xr, yr, xsq, ysq, parts = call(
         start_kernel,
@@ -431,38 +533,42 @@
         )
     parts = over("col", parts)
     e, parts = call(
-        functools.partial(tgt_part_kernel, all_tgt, dim_tgt),
+        functools.partial(tgt_part_kernel, all_tgt, dims),
         (parts, xt, yr, xr, h),
-        (shape(rs, HALF), shape(n_row, rt // 4 + blk_tgt, 4, HALF)),
+        (shape(rs, HALF), shape(n_row, rt // 4 + blocks, 4, HALF)),
         scratch(ns, nt, HALF),
         name="tgt_part",
     )
     parts = over("row", parts)
-    h, tgt = call(
-        functools.partial(tgt_join_kernel, all_src, dim_tgt, grp_tgt),
+    h, every_h = call(
+        functools.partial(tgt_join_kernel, all_src),
         (parts,),
-        (shape(rt, HALF), shape(n_row, blk_tgt, 4, HALF)),
+        (shape(rt, HALF), shape(n_col, rt // 4, 4, HALF)),
         name="tgt_join",
     )
+    every_h, every_y = lax.optimization_barrier((every_h, every_y))
+    every_h = over("col", every_h)
+    parts, every_h = lax.optimization_barrier((parts, every_h))
+    tgt = call(
+        functools.partial(tgt_share_kernel, dims, groups),
+        (parts,),
+        shape(n_row, blocks, 4, HALF),
+        name="tgt_share",
+    )
     tgt = over("row", tgt)
-    parts = call(
-        functools.partial(src_part_kernel, dim_src),
-        (h, yt, xr, yr, e),
-        shape(n_col, log_src + blk_src, 4, HALF),
-        scratch(nt, ns, HALF),
-        name="src_part",
-    )
-    parts, tgt = lax.optimization_barrier((parts, tgt))
-    parts = over("col", parts)
     src = call(
-        functools.partial(src_share_kernel, dim_src),
-        (parts,),
-        shape(n_col, blk_src, 4, HALF),
-        name="src_share",
-    )
-    src = over("col", src)
+        src_map_kernel,
+        (every_h, pltpu.with_memory_space_constraint(every_y, pltpu.HBM), xr, e),
+        shape(near, 4 * quarter // HALF, 8, HALF),
+        src_scratch(quarter, n_col, nt)
+        + (pltpu.VMEM((n_col, DIM, nt), F32), pltpu.SemaphoreType.DMA((n_col,))),
+        name="src_map",
+        hbm=(1,),
+    )
+    src, tgt = lax.optimization_barrier((src, tgt))
+    src = over("col", src, [[near * k + j for j in range(near)] for k in range(n_col // near)])
     f, g, si, ti = call(
-        functools.partial(end_kernel, (dim_src, dim_tgt)),
+        functools.partial(end_kernel, dims),
         (e, h, xsq, ysq, src, tgt),
         (shape(rs, HALF), shape(rt, HALF), shape(*x.shape), shape(*y.shape)),
         name="end",

time: 201 us -> 234 us (1.16)
  the two profiles are of different devices: /device:TPU:4 before, /device:TPU:6 now
where the time goes in v4:
time: 234 us
  blocking collectives  125 us (53%)
  Pallas kernels  86.6 us (37%)
  between operations  14.1 us (6%)
  starting transfers between devices  6.07 us (3%)
    all_to_all x8, blocking collectives, over(): return lax.all_to_all(v, axis, 0, 0, axis_index_groups=groups)  125 us
    pallas_call x10, Pallas kernels, call(): pl.pallas_call(kernel, out_shape=outs, in_specs=[HBM if k in hbm else VME...  86.6 us
    all_to_all x1, starting transfers between devices, over(): return lax.all_to_all(v, axis, 0, 0, axis_index_groups=groups)  6.03 us
  transfers between devices with their start and end apart: 2, of which 0 were waited for; matrix products, arithmetic and copies ran while one was open for 0% of the time, Pallas kernels for 36%

profile of v4, /device:TPU:6, one launch (start us, length us, event | category | flops | bytes accessed | tf_op | source)
XLA Modules:
  0.0 233.8 jit_solution(12585671568871668228)
XLA Ops:
  7.2 0.0 all-gather.3.cloned.1.call-start
  7.2 0.7 all-gather.3.cloned.1.call-update
  7.9 1.0 pad_maximum_fusion.xy_ref
  8.9 11.8 %start.1 = (bf16[1024,256]{1,0:T(8,128)(2,1)S(1)}, bf16[1536,256]{1,0:T(8,128)(2,1)S(1)}, bf16[256,1024]{1,0:T(8,128)(2,1)S(1)}, bf16[256,1536]{1,0:T(8,128)(2,1...) custom-call(f32[32,2560]{1,0:T(8,128)S(1)} %pad_maximum_fusion.xy_ref), custom_call_target="tpu_custom_call" | custom-call | tf_op jit(solution)/shard_map/start/pallas_call | solution.py:464
  20.7 28.5 %all_to_all.45.p = f32[16,1,8,128]{3,2,1,0:T(8,128)S(1)} all-to-all(f32[16,1,8,128]{3,2,1,0:T(8,128)S(1)} %get-tuple-element.33), channel_id=1, replica_groups=mesh['row'=32,'col'=16] {'col'}, dimensions={0} | all-to-all | bytes 131072 | tf_op jit(solution)/shard_map/all_to_all | solution.py:490
  49.2 11.8 %cols.2 = (f32[8,128]{1,0:T(8,128)S(1)}, f32[32,3,4,128]{3,2,1,0:T(4,128)S(1)}) custom-call(f32[16,1,8,128]{3,2,1,0:T(8,128)S(1)} %all_to_all.45.p, bf16[1024,256]{1,0:T(8,128)(2,1)S(1)} %get-tuple-element.34.c.col_ref, bf16[256,1536]{1,0:T(8,128)(2,1)S(1)} %get-tuple-element.35.r.row_ref), custom_call_target="tpu_custom_call" | custom-call | tf_op jit(solution)/shard_map/cols/pallas_call | solution.py:464
  61.0 14.0 %all_to_all.46.parts_ref = f32[32,3,4,128]{3,2,1,0:T(4,128)S(1)} all-to-all(f32[32,3,4,128]{3,2,1,0:T(4,128)S(1)} %get-tuple-element.36), channel_id=1, replica_groups=mesh['row'=32,'col'=16] {'row'}, dimensions={0} | all-to-all | bytes 393216 | tf_op jit(solution)/shard_map/all_to_all | solution.py:490
  74.9 11.6 %rows.2 = (f32[12,128]{1,0:T(8,128)S(1)}, f32[16,1,8,128]{3,2,1,0:T(8,128)S(1)}) custom-call(f32[32,3,4,128]{3,2,1,0:T(4,128)S(1)} %all_to_all.46.parts_ref, bf16[1536,256]{1,0:T(8,128)(2,1)S(1)} %get-tuple-element.37.col_ref, bf16[256,1024]{1,0:T(8,128)(2,1)S(1)} %get-tuple-element.38.row_ref.values_ref.xr_ref, f32[8,128]{1,0:T(8,128)S(1)} %get-tuple-element.39.old_ref), custom_call_target="tpu_custom_call" | custom-call | tf_op jit(solution)/shard_map/rows/pallas_call | solution.py:464
  86.6 15.9 %all_to_all.47.parts_ref = f32[16,1,8,128]{3,2,1,0:T(8,128)S(1)} all-to-all(f32[16,1,8,128]{3,2,1,0:T(8,128)S(1)} %get-tuple-element.40), channel_id=1, replica_groups=mesh['row'=32,'col'=16] {'col'}, dimensions={0} | all-to-all | bytes 131072 | tf_op jit(solution)/shard_map/all_to_all | solution.py:490
  102.5 11.7 %cols.3 = (f32[8,128]{1,0:T(8,128)S(1)}, f32[32,3,4,128]{3,2,1,0:T(4,128)S(1)}) custom-call(f32[16,1,8,128]{3,2,1,0:T(8,128)S(1)} %all_to_all.47.parts_ref, bf16[1024,256]{1,0:T(8,128)(2,1)S(1)} %get-tuple-element.34.c.col_ref, bf16[256,1536]{1,0:T(8,128)(2,1)S(1)} %get-tuple-element.35.r.row_ref, f32[12,128]{1,0:T(8,128)S(1)} %get-tuple-element.41.old_ref), custom_call_target="tpu_custom_call" | custom-call | tf_op jit(solution)/shard_map/cols/pallas_call | solution.py:464
  114.2 11.8 %all_to_all.48.parts_ref = f32[32,3,4,128]{3,2,1,0:T(4,128)S(1)} all-to-all(f32[32,3,4,128]{3,2,1,0:T(4,128)S(1)} %get-tuple-element.42), channel_id=1, replica_groups=mesh['row'=32,'col'=16] {'row'}, dimensions={0} | all-to-all | bytes 393216 | tf_op jit(solution)/shard_map/all_to_all | solution.py:490
  126.0 11.6 %rows.3 = (f32[12,128]{1,0:T(8,128)S(1)}, f32[16,1,8,128]{3,2,1,0:T(8,128)S(1)}) custom-call(f32[32,3,4,128]{3,2,1,0:T(4,128)S(1)} %all_to_all.48.parts_ref, bf16[1536,256]{1,0:T(8,128)(2,1)S(1)} %get-tuple-element.37.col_ref, bf16[256,1024]{1,0:T(8,128)(2,1)S(1)} %get-tuple-element.38.row_ref.values_ref.xr_ref, f32[8,128]{1,0:T(8,128)S(1)} %get-tuple-element.43.old_ref), custom_call_target="tpu_custom_call" | custom-call | tf_op jit(solution)/shard_map/rows/pallas_call | solution.py:464
  137.7 16.0 %all_to_all.49.parts_ref = f32[16,1,8,128]{3,2,1,0:T(8,128)S(1)} all-to-all(f32[16,1,8,128]{3,2,1,0:T(8,128)S(1)} %get-tuple-element.44), channel_id=1, replica_groups=mesh['row'=32,'col'=16] {'col'}, dimensions={0} | all-to-all | bytes 131072 | tf_op jit(solution)/shard_map/all_to_all | solution.py:490
  153.7 17.3 %tgt_part.1 = (f32[8,128]{1,0:T(8,128)S(1)}, f32[32,6,4,128]{3,2,1,0:T(4,128)S(1)}) custom-call(f32[16,1,8,128]{3,2,1,0:T(8,128)S(1)} %all_to_all.49.parts_ref, bf16[1024,256]{1,0:T(8,128)(2,1)S(1)} %get-tuple-element.34.c.col_ref, bf16[256,1536]{1,0:T(8,128)(2,1)S(1)} %get-tuple-element.35.r.row_ref, ...), custom_call_target="tpu_custom_call" | custom-call | tf_op jit(solution)/shard_map/tgt_part/pallas_call | solution.py:464
  171.0 13.0 %all_to_all.50.parts_ref = f32[32,6,4,128]{3,2,1,0:T(4,128)S(1)} all-to-all(f32[32,6,4,128]{3,2,1,0:T(4,128)S(1)} %get-tuple-element.47), channel_id=1, replica_groups=mesh['row'=32,'col'=16] {'row'}, dimensions={0} | all-to-all | bytes 786432 | tf_op jit(solution)/shard_map/all_to_all | solution.py:490
  184.0 0.1 tgt_join.1
  184.2 0.0 all-gather.3.cloned.1.call-done
  184.2 16.5 %all_to_all.51.h_ref = f32[16,3,4,128]{3,2,1,0:T(4,128)S(1)} all-to-all(f32[16,3,4,128]{3,2,1,0:T(4,128)S(1)} %get-tuple-element.52), channel_id=1, replica_groups=mesh['row'=32,'col'=16] {'col'}, dimensions={0} | all-to-all | bytes 196608 | tf_op jit(solution)/shard_map/all_to_all | solution.py:490
  200.7 0.9 tgt_share.1
  201.6 6.0 %all-to-all-start.7 = ((f32[32,3,4,128]{3,2,1,0:T(4,128)}), f32[32,3,4,128]{3,2,1,0:T(4,128)S(1)}, u32[]{:S(2)}, u32[]{:S(2)}) async-start(f32[32,3,4,128]{3,2,1,0:T(4,128)} %tgt_share.1), calls=%async_computation.7 | async-start | bytes 393216 | tf_op jit(solution)/shard_map/all_to_all | solution.py:490
  207.6 9.0 %src_map.1 = f32[4,8,8,128]{3,2,1,0:T(8,128)S(1)} custom-call(f32[16,3,4,128]{3,2,1,0:T(4,128)S(1)} %all_to_all.51.h_ref, f32[16,32,1536]{2,1,0:T(8,128)} %bitcast.3, bf16[256,1024]{1,0:T(8,128)(2,1)S(1)} %get-tuple-element.38.row_ref.values_ref.xr_ref, f32[8,128]{1,0:T(8,128)S(1)} %get-tuple-element.46.e_ref), custom_call_target="tpu_custom_call" | custom-call | tf_op jit(solution)/shard_map/src_map/pallas_call | solution.py:464
  216.6 0.0 all-to-all-done.7.tgt_ref
  216.6 9.5 %all_to_all.52.src_ref = f32[4,8,8,128]{3,2,1,0:T(8,128)S(1)} all-to-all(f32[4,8,8,128]{3,2,1,0:T(8,128)S(1)} %src_map.1), channel_id=1, replica_groups={{0,1,2,3},{4,5,6,7},{8,9,10,11},{12,13,14,15},{16,17,18,19},{20,21,22,2..., dimensions={0} | all-to-all | bytes 262144 | tf_op jit(solution)/shard_map/all_to_all | solution.py:490
  226.1 0.8 end.1
Async XLA Ops:
  7.2 177.0 %all-gather.3.cloned.1.call-start = ((), (), s32[]{:S(2)}) async-start(), calls=%async_computation.9 | async-start | bytes 3342336 | tf_op jit(solution)/shard_map/all_gather | solution.py:492
  201.6 15.1 %all-to-all-start.7 = ((f32[32,3,4,128]{3,2,1,0:T(4,128)}), f32[32,3,4,128]{3,2,1,0:T(4,128)S(1)}, u32[]{:S(2)}, u32[]{:S(2)}) async-start(f32[32,3,4,128]{3,2,1,0:T(4,128)} %tgt_share.1), calls=%async_computation.7 | async-start | bytes 393216 | tf_op jit(solution)/shard_map/all_to_all | solution.py:490
Sparse Core Ops, SparseCore 0:
  10.1 82.6 all-gather.2

commit v5 on v3

--- a/solution.py
+++ b/solution.py
@@ -108,20 +108,37 @@
         s_ref[:, cols] = jnp.sum(acc, axis=0, keepdims=True)
 
 
+def fold(col_ref, half_ref, row_ref, shift_ref, out_ref, first, shifted, start, step, end):
+    @pl.loop(0, row_ref.shape[1] // TILE)
+    def _(t):
+        at = pl.multiple_of(t * TILE, TILE)
+        cols = pl.ds(at, TILE)
+        shift = shift_ref[:, cols] if shifted else jnp.zeros((1, TILE), F32)
+        rhs = tile_of(row_ref, row_block(shift, first), at)
+
+        def chunk(c, acc):
+            c = pl.multiple_of(c * CHUNK, CHUNK)
+            return step(c, acc, scores(col_ref, half_ref, c, rhs))
+
+        out_ref[:, cols] = end(lax.fori_loop(0, col_ref.shape[0] // CHUNK, chunk, start))
+
+
 def peaks(col_ref, half_ref, row_ref, shift_ref, first):
-    count, n = col_ref.shape[0], row_ref.shape[1]
-
-    @pl.loop(0, n // TILE)
-    def _(t):
-        start = pl.multiple_of(t * TILE, TILE)
-        rhs = tile_of(row_ref, row_block(jnp.zeros((1, TILE), F32), first), start)
-
-        def step(c, acc):
-            s = scores(col_ref, half_ref, pl.multiple_of(c * CHUNK, CHUNK), rhs)
-            return jnp.maximum(acc, jnp.max(s.reshape(CHUNK // 8, 8, TILE), axis=0))
-
-        acc = lax.fori_loop(0, count // CHUNK, step, jnp.full((8, TILE), -jnp.inf, F32))
-        shift_ref[:, pl.ds(start, TILE)] = -jnp.max(acc, axis=0, keepdims=True)
+    fold(
+        col_ref, half_ref, row_ref, shift_ref, shift_ref, first, False,
+        jnp.full((8, TILE), -jnp.inf, F32),
+        lambda c, acc, s: jnp.maximum(acc, jnp.max(s.reshape(CHUNK // 8, 8, TILE), axis=0)),
+        lambda acc: -jnp.max(acc, axis=0, keepdims=True),
+    )
+
+
+def slow_sums(col_ref, half_ref, row_ref, shift_ref, s_ref, first):
+    fold(
+        col_ref, half_ref, row_ref, shift_ref, s_ref, first, True,
+        jnp.zeros((8, TILE), F32),
+        lambda c, acc, s: acc + jnp.sum(jnp.exp2(s).reshape(CHUNK // 8, 8, TILE), axis=0),
+        lambda acc: jnp.sum(acc, axis=0, keepdims=True),
+    )
 
 
 def probe(col_ref, half_ref, row_ref, shift_ref, first):
@@ -136,7 +153,7 @@
     return jnp.any(jnp.logical_not((s > LOW) & (s < HIGH)))
 
 
-def guarded(compute, finish, sum_ref, col_ref, half_ref, row_ref, shift_ref, first):
+def guarded(compute, redo, finish, sum_ref, col_ref, half_ref, row_ref, shift_ref, first):
     compute()
     s = as_dense(sum_ref[...])
     finish(s)
@@ -144,7 +161,7 @@
     @pl.when(outside(s))
     def _():
         peaks(col_ref, half_ref, row_ref, shift_ref, first)
-        compute()
+        redo()
         finish(as_dense(sum_ref[...]))
 
 
@@ -193,6 +210,7 @@
     args = (col_ref, half_ref, row_ref, shift_ref)
     guarded(
         lambda: sums(*args, s_ref, first),
+        lambda: slow_sums(*args, s_ref, first),
         lambda s: send_logs(out_ref, jnp.log2(s) - as_dense(shift_ref[...])),
         s_ref,
         *args,
@@ -216,20 +234,34 @@
     lse(out_ref, *args, s_ref, row_first)
 
 
-def maps(col_ref, half_ref, row_ref, values_ref, shift_ref, moved_ref, first):
+def weighted(score, values):
+    w = jnp.exp2(score)
+    high = w.astype(BF)
+    low = (w - high.astype(F32)).astype(BF)
+    return jnp.dot(values, high, preferred_element_type=F32) + jnp.dot(
+        values, low, preferred_element_type=F32
+    )
+
+
+def maps(col_ref, half_ref, row_ref, shift_ref, values_ref, moved_ref, first):
     count, n = col_ref.shape[0], row_ref.shape[1]
     for t in range(n // TILE):
         cols = slice(t * TILE, (t + 1) * TILE)
         rhs = tile_of(row_ref, row_block(shift_ref[:, cols], first), t * TILE)
         total = jnp.zeros((HALF, TILE), F32)
         for c in range(count // CHUNK):
-            w = jnp.exp2(scores(col_ref, half_ref, c * CHUNK, rhs))
-            high = w.astype(BF)
-            low = (w - high.astype(F32)).astype(BF)
             values = values_ref[HALF:, c * CHUNK : (c + 1) * CHUNK]
-            total += jnp.dot(values, high, preferred_element_type=F32)
-            total += jnp.dot(values, low, preferred_element_type=F32)
+            total += weighted(scores(col_ref, half_ref, c * CHUNK, rhs), values)
         moved_ref[:, cols] = total
+
+
+def slow_maps(col_ref, half_ref, row_ref, shift_ref, values_ref, moved_ref, first):
+    fold(
+        col_ref, half_ref, row_ref, shift_ref, moved_ref, first, True,
+        jnp.zeros((HALF, TILE), F32),
+        lambda c, acc, s: acc + weighted(s, values_ref[HALF:, pl.ds(c, CHUNK)]),
+        lambda acc: acc,
+    )
 
 
 def image(dims, scale, send, out_ref, col_ref, half_ref, row_ref, values_ref, shift_ref, moved_ref, first):
@@ -252,7 +284,8 @@
                     at += 1
 
     guarded(
-        lambda: maps(col_ref, half_ref, row_ref, values_ref, shift_ref, moved_ref, first),
+        lambda: maps(*args, values_ref, moved_ref, first),
+        lambda: slow_maps(*args, values_ref, moved_ref, first),
         finish,
         moved_ref.at[one : one + 1, :],
         *args,
@@ -330,6 +363,15 @@
         return logs_ref[:, cell // 4, pl.ds(lax.rem(cell, 4), 1), :]
 
     share(parts_ref, out_ref, new_ref.shape[0] // 4, dims, logs_of)
+
+
+def src_join_kernel(dims, base, parts_ref, out_ref):
+    out_ref[:, :base] = jnp.zeros((out_ref.shape[0], base, 4, HALF), F32)
+    for c in range((parts_ref.shape[1] - base) * 4 // dims):
+        rows = slice(c % 4, c % 4 + 1)
+        log = joined(parts_ref[:, c // 4, rows, :])
+        out_ref[:, c // 4, rows, :] = jnp.broadcast_to(log[None], (out_ref.shape[0], 1, HALF))
+    src_share_kernel(dims, parts_ref, out_ref.at[:, base:])
 
 
 def src_share_kernel(dims, parts_ref, out_ref):
@@ -378,16 +420,19 @@
     n_row, n_col = lax.axis_size("row"), lax.axis_size("col")
     rs, rt = ns // HALF, nt // HALF
     all_src, all_tgt = ns * n_row, nt * n_col
-    dim_src, dim_tgt = DIM // min(n_col, 4), DIM // min(n_row, 8)
-    grp_src, grp_tgt = n_col * dim_src // DIM, n_row * dim_tgt // DIM
-    blk_src, blk_tgt = ns * DIM // n_col // 512, nt * DIM // n_row // 512
-    log_src = -(-rs // grp_src // 4)
+    dim_tgt = DIM // min(n_row, 8)
+    grp_tgt = n_row * dim_tgt // DIM
+    blk_tgt = nt * DIM // n_row // 512
+    near = min(n_col, 4)
+    neighbours = [[near * k + j for j in range(near)] for k in range(n_col // near)]
+    apart = [[near * k + j for k in range(n_col // near)] for j in range(near)]
+    blk_src, log_src = ns * DIM // near // 512, -(-rs // near // 4)
 
     def scratch(m, n, rows=1):
         return (pltpu.VMEM((m, HALF), BF), pltpu.VMEM((1, n), F32), pltpu.VMEM((rows, n), F32))
 
-    def over(axis, v):
-        return lax.all_to_all(v, axis, 0, 0)
+    def over(axis, v, groups=None):
+        return lax.all_to_all(v, axis, 0, 0, axis_index_groups=groups)
 
     xt, yt, xr, yr, xsq, ysq, parts = call(
         start_kernel,
@@ -446,23 +491,30 @@
     )
     tgt = over("row", tgt)
     parts = call(
-        functools.partial(src_part_kernel, dim_src),
+        functools.partial(src_part_kernel, DIM),
         (h, yt, xr, yr, e),
-        shape(n_col, log_src + blk_src, 4, HALF),
+        shape(near, log_src + blk_src, 4, HALF),
         scratch(nt, ns, HALF),
         name="src_part",
     )
     parts, tgt = lax.optimization_barrier((parts, tgt))
-    parts = over("col", parts)
+    parts = over("col", parts, neighbours)
+    parts = call(
+        functools.partial(src_join_kernel, DIM, log_src),
+        (parts,),
+        shape(n_col // near, log_src + blk_src, 4, HALF),
+        name="src_join",
+    )
+    parts = over("col", parts, apart)
     src = call(
-        functools.partial(src_share_kernel, dim_src),
+        functools.partial(src_share_kernel, DIM),
         (parts,),
-        shape(n_col, blk_src, 4, HALF),
+        shape(near, blk_src, 4, HALF),
         name="src_share",
     )
-    src = over("col", src)
+    src = over("col", src, neighbours)
     f, g, si, ti = call(
-        functools.partial(end_kernel, (dim_src, dim_tgt)),
+        functools.partial(end_kernel, (DIM, dim_tgt)),
         (e, h, xsq, ysq, src, tgt),
         (shape(rs, HALF), shape(rt, HALF), shape(*x.shape), shape(*y.shape)),
         name="end",

time: 201 us -> 239 us (1.19)
  the two profiles are of different devices: /device:TPU:4 before, /device:TPU:6 now
where the time goes in v5:
time: 239 us; the launch traced here: 236 us
  blocking collectives  165 us (69%)
  Pallas kernels  58.8 us (25%)
  starting transfers between devices  5.78 us (2%)
  waiting for transfers between devices  4.22 us (2%)
    all_to_all x9, blocking collectives, over(): return lax.all_to_all(v, axis, 0, 0, axis_index_groups=groups)  165 us
    pallas_call x11, Pallas kernels, call(): pl.pallas_call(kernel, out_shape=outs, in_specs=[VMEM] * len(ins), out_sp...  58.8 us
    all_to_all x1, starting transfers between devices, over(): return lax.all_to_all(v, axis, 0, 0, axis_index_groups=groups)  5.78 us
  transfers between devices with their start and end apart: 1, of which 1 were waited for; matrix products, arithmetic and copies ran while one was open for 0% of the time, Pallas kernels for 1%

profile of v5, /device:TPU:6, one launch (start us, length us, event | category | flops | bytes accessed | tf_op | source)
XLA Modules:
  0.0 235.9 jit_solution(17971414515895395763)
XLA Ops:
  0.6 1.0 pad_maximum_fusion.xy_ref
  1.7 11.7 %start.1 = (bf16[1024,256]{1,0:T(8,128)(2,1)S(1)}, bf16[1536,256]{1,0:T(8,128)(2,1)S(1)}, bf16[256,1024]{1,0:T(8,128)(2,1)S(1)}, bf16[256,1536]{1,0:T(8,128)(2,1...) custom-call(f32[32,2560]{1,0:T(8,128)S(1)} %pad_maximum_fusion.xy_ref), custom_call_target="tpu_custom_call" | custom-call | tf_op jit(solution)/shard_map/start/pallas_call | solution.py:407
  13.3 27.7 %all_to_all.50.p = f32[16,1,8,128]{3,2,1,0:T(8,128)S(1)} all-to-all(f32[16,1,8,128]{3,2,1,0:T(8,128)S(1)} %get-tuple-element.29), channel_id=1, replica_groups=mesh['row'=32,'col'=16] {'col'}, dimensions={0} | all-to-all | bytes 131072 | tf_op jit(solution)/shard_map/all_to_all | solution.py:435
  41.1 11.7 %cols.2 = (f32[8,128]{1,0:T(8,128)S(1)}, f32[32,3,4,128]{3,2,1,0:T(4,128)S(1)}) custom-call(f32[16,1,8,128]{3,2,1,0:T(8,128)S(1)} %all_to_all.50.p, bf16[1024,256]{1,0:T(8,128)(2,1)S(1)} %get-tuple-element.30.c.col_ref, bf16[256,1536]{1,0:T(8,128)(2,1)S(1)} %get-tuple-element.31.r.row_ref.values_ref), custom_call_target="tpu_custom_call" | custom-call | tf_op jit(solution)/shard_map/cols/pallas_call | solution.py:407
  52.8 13.8 %all_to_all.51.parts_ref = f32[32,3,4,128]{3,2,1,0:T(4,128)S(1)} all-to-all(f32[32,3,4,128]{3,2,1,0:T(4,128)S(1)} %get-tuple-element.32), channel_id=1, replica_groups=mesh['row'=32,'col'=16] {'row'}, dimensions={0} | all-to-all | bytes 393216 | tf_op jit(solution)/shard_map/all_to_all | solution.py:435
  66.6 1.3 rows.2
  67.9 26.0 %all_to_all.52.parts_ref = f32[16,1,8,128]{3,2,1,0:T(8,128)S(1)} all-to-all(f32[16,1,8,128]{3,2,1,0:T(8,128)S(1)} %get-tuple-element.36), channel_id=1, replica_groups=mesh['row'=32,'col'=16] {'col'}, dimensions={0} | all-to-all | bytes 131072 | tf_op jit(solution)/shard_map/all_to_all | solution.py:435
  93.9 11.7 %cols.3 = (f32[8,128]{1,0:T(8,128)S(1)}, f32[32,3,4,128]{3,2,1,0:T(4,128)S(1)}) custom-call(f32[16,1,8,128]{3,2,1,0:T(8,128)S(1)} %all_to_all.52.parts_ref, bf16[1024,256]{1,0:T(8,128)(2,1)S(1)} %get-tuple-element.30.c.col_ref, bf16[256,1536]{1,0:T(8,128)(2,1)S(1)} %get-tuple-element.31.r.row_ref.values_ref, f32[12,128]{1,0:T(8,128)S(1)} %get-tuple-element.37.old_ref), custom_call_target="tpu_custom_call" | custom-call | tf_op jit(solution)/shard_map/cols/pallas_call | solution.py:407
  105.6 11.7 %all_to_all.53.parts_ref = f32[32,3,4,128]{3,2,1,0:T(4,128)S(1)} all-to-all(f32[32,3,4,128]{3,2,1,0:T(4,128)S(1)} %get-tuple-element.38), channel_id=1, replica_groups=mesh['row'=32,'col'=16] {'row'}, dimensions={0} | all-to-all | bytes 393216 | tf_op jit(solution)/shard_map/all_to_all | solution.py:435
  117.3 1.3 rows.3
  118.6 26.1 %all_to_all.54.parts_ref = f32[16,1,8,128]{3,2,1,0:T(8,128)S(1)} all-to-all(f32[16,1,8,128]{3,2,1,0:T(8,128)S(1)} %get-tuple-element.40), channel_id=1, replica_groups=mesh['row'=32,'col'=16] {'col'}, dimensions={0} | all-to-all | bytes 131072 | tf_op jit(solution)/shard_map/all_to_all | solution.py:435
  144.7 17.2 %tgt_part.1 = (f32[8,128]{1,0:T(8,128)S(1)}, f32[32,6,4,128]{3,2,1,0:T(4,128)S(1)}) custom-call(f32[16,1,8,128]{3,2,1,0:T(8,128)S(1)} %all_to_all.54.parts_ref, bf16[1024,256]{1,0:T(8,128)(2,1)S(1)} %get-tuple-element.30.c.col_ref, bf16[256,1536]{1,0:T(8,128)(2,1)S(1)} %get-tuple-element.31.r.row_ref.values_ref, ...), custom_call_target="tpu_custom_call" | custom-call | tf_op jit(solution)/shard_map/tgt_part/pallas_call | solution.py:407
  161.9 13.3 %all_to_all.55.parts_ref = f32[32,6,4,128]{3,2,1,0:T(4,128)S(1)} all-to-all(f32[32,6,4,128]{3,2,1,0:T(4,128)S(1)} %get-tuple-element.43), channel_id=1, replica_groups=mesh['row'=32,'col'=16] {'row'}, dimensions={0} | all-to-all | bytes 786432 | tf_op jit(solution)/shard_map/all_to_all | solution.py:435
  175.1 0.9 tgt_join.1
  176.0 5.8 %all-to-all-start.6 = ((f32[32,3,4,128]{3,2,1,0:T(4,128)}), f32[32,3,4,128]{3,2,1,0:T(4,128)S(1)}, u32[]{:S(2)}, u32[]{:S(2)}) async-start(f32[32,3,4,128]{3,2,1,0:T(4,128)} %get-tuple-element.47), calls=%async_computation.6 | async-start | bytes 393216 | tf_op jit(solution)/shard_map/all_to_all | solution.py:435
  181.8 2.2 src_part.1
  184.0 4.2 %all-to-all-done.6.tgt_ref = f32[32,3,4,128]{3,2,1,0:T(4,128)S(1)} async-done(((f32[32,3,4,128]{3,2,1,0:T(4,128)}), f32[32,3,4,128]{3,2,1,0:T(4,128)S(1)}, u32[]{:S(2)}, u32[]{:S(2)}) %all-to-all-start.6) | async-done | bytes 196640 | tf_op jit(solution)/shard_map/all_to_all | solution.py:435
  188.2 20.1 %all_to_all.56.parts_ref = f32[4,17,4,128]{3,2,1,0:T(4,128)S(1)} all-to-all(f32[4,17,4,128]{3,2,1,0:T(4,128)S(1)} %src_part.1), channel_id=1, replica_groups={{0,1,2,3},{4,5,6,7},{8,9,10,11},{12,13,14,15},{16,17,18,19},{20,21,22,2..., dimensions={0} | all-to-all | bytes 278528 | tf_op jit(solution)/shard_map/all_to_all | solution.py:435
  208.3 0.1 src_join.1
  208.4 18.2 %all_to_all.57.parts_ref = f32[4,17,4,128]{3,2,1,0:T(4,128)S(1)} all-to-all(f32[4,17,4,128]{3,2,1,0:T(4,128)S(1)} %src_join.1), channel_id=1, replica_groups={{0,4,8,12},{1,5,9,13},{2,6,10,14},{3,7,11,15},{16,20,24,28},{17,21,25,2..., dimensions={0} | all-to-all | bytes 278528 | tf_op jit(solution)/shard_map/all_to_all | solution.py:435
  226.6 0.1 src_share.1
  226.7 8.4 %all_to_all.58.src_ref = f32[4,16,4,128]{3,2,1,0:T(4,128)S(1)} all-to-all(f32[4,16,4,128]{3,2,1,0:T(4,128)S(1)} %src_share.1), channel_id=1, replica_groups={{0,1,2,3},{4,5,6,7},{8,9,10,11},{12,13,14,15},{16,17,18,19},{20,21,22,2..., dimensions={0} | all-to-all | bytes 262144 | tf_op jit(solution)/shard_map/all_to_all | solution.py:435
  235.1 0.8 end.1
Async XLA Ops:
  176.0 12.2 %all-to-all-start.6 = ((f32[32,3,4,128]{3,2,1,0:T(4,128)}), f32[32,3,4,128]{3,2,1,0:T(4,128)S(1)}, u32[]{:S(2)}, u32[]{:S(2)}) async-start(f32[32,3,4,128]{3,2,1,0:T(4,128)} %get-tuple-element.47), calls=%async_computation.6 | async-start | bytes 393216 | tf_op jit(solution)/shard_map/all_to_all | solution.py:435

commit v6 on v5

--- a/solution.py
+++ b/solution.py
@@ -298,19 +298,6 @@
     return log.shape[0] // 4
 
 
-def send_own_logs(out_ref, log, groups):
-    n, each = out_ref.shape[0], log.shape[0] // groups
-    blocks = -(-each // 4)
-    for group in range(groups):
-        rows = [log[c : c + 1] for c in range(group, log.shape[0], groups)]
-        rows = rows + [jnp.zeros_like(rows[0])] * (4 * blocks - each)
-        for b in range(blocks):
-            block = jnp.concatenate(rows[4 * b : 4 * b + 4], axis=0)
-            for k in range(group, n, groups):
-                out_ref[k, b] = block
-    return blocks
-
-
 def tgt_part_kernel(
     total, dims,
     parts_ref, col_ref, row_ref, values_ref, old_ref,
@@ -326,17 +313,35 @@
     )
 
 
-def src_part_kernel(
-    dims,
-    new_ref, col_ref, row_ref, values_ref, old_ref,
-    out_ref,
-    half_ref, shift_ref, moved_ref,
-):
+def src_part_kernel(near, new_ref, col_ref, row_ref, values_ref, old_ref, *refs):
+    outs, (half_ref, shift_ref, moved_ref, image_ref, log_ref) = refs[:near], refs[near:]
     half_ref[...] = column_half(as_row(new_ref[...]), 3, col_ref)
     shift_ref[...] = as_row(old_ref[...])
-    image(
-        dims, 1.0, send_own_logs, out_ref,
-        col_ref, half_ref, row_ref, values_ref, shift_ref, moved_ref, 0,
+    args = (col_ref, half_ref, row_ref, shift_ref)
+    mine = lax.rem(lax.axis_index("col"), near)
+    each = log_ref.shape[0] // near
+    base = -(-each // 4)
+
+    def finish(s):
+        log_ref[...] = jnp.log2(s) - as_dense(shift_ref[...])
+        part = moved_ref[16:48, :] + moved_ref[48:80, :] + moved_ref[80:112, :]
+        image_ref[...] = part / as_row(s)
+        for k, out_ref in enumerate(outs):
+            out_ref[:base] = jnp.zeros((base, 4, HALF), F32)
+            for c in range(each):
+                cell = near * c + (mine ^ k)
+                lanes = pl.ds(pl.multiple_of(HALF * cell, HALF), HALF)
+                out_ref[c // 4, c % 4 : c % 4 + 1, :] = log_ref[pl.ds(cell, 1), :]
+                for u in range(DIM // 4):
+                    out_ref[base + DIM // 4 * c + u] = image_ref[4 * u : 4 * u + 4, lanes]
+
+    guarded(
+        lambda: maps(*args, values_ref, moved_ref, 0),
+        lambda: slow_maps(*args, values_ref, moved_ref, 0),
+        finish,
+        moved_ref.at[0:1, :],
+        *args,
+        0,
     )
 
 
@@ -365,13 +370,16 @@
     share(parts_ref, out_ref, new_ref.shape[0] // 4, dims, logs_of)
 
 
-def src_join_kernel(dims, base, parts_ref, out_ref):
+def src_join_kernel(base, *refs):
+    ins, (out_ref, parts_ref) = refs[:-2], refs[-2:]
+    for k, ref in enumerate(ins):
+        parts_ref[k] = ref[...]
     out_ref[:, :base] = jnp.zeros((out_ref.shape[0], base, 4, HALF), F32)
-    for c in range((parts_ref.shape[1] - base) * 4 // dims):
+    for c in range((parts_ref.shape[1] - base) * 4 // DIM):
         rows = slice(c % 4, c % 4 + 1)
         log = joined(parts_ref[:, c // 4, rows, :])
         out_ref[:, c // 4, rows, :] = jnp.broadcast_to(log[None], (out_ref.shape[0], 1, HALF))
-    src_share_kernel(dims, parts_ref, out_ref.at[:, base:])
+    src_share_kernel(DIM, parts_ref, out_ref.at[:, base:])
 
 
 def src_share_kernel(dims, parts_ref, out_ref):
@@ -490,21 +498,28 @@
         name="tgt_join",
     )
     tgt = over("row", tgt)
+    block = (log_src + blk_src, 4, HALF)
     parts = call(
-        functools.partial(src_part_kernel, DIM),
+        functools.partial(src_part_kernel, near),
         (h, yt, xr, yr, e),
-        shape(near, log_src + blk_src, 4, HALF),
-        scratch(nt, ns, HALF),
+        tuple(shape(*block) for _ in range(near)),
+        scratch(nt, ns, HALF) + (pltpu.VMEM(x.shape, F32), pltpu.VMEM((rs, HALF), F32)),
         name="src_part",
     )
+    parts = parts[:1] + tuple(
+        lax.ppermute(
+            parts[k], "col", [(i, near * (i // near) + ((i % near) ^ k)) for i in range(n_col)]
+        )
+        for k in range(1, near)
+    )
+    parts = call(
+        functools.partial(src_join_kernel, log_src),
+        parts,
+        shape(n_col // near, *block),
+        (pltpu.VMEM((near, *block), F32),),
+        name="src_join",
+    )
     parts, tgt = lax.optimization_barrier((parts, tgt))
-    parts = over("col", parts, neighbours)
-    parts = call(
-        functools.partial(src_join_kernel, DIM, log_src),
-        (parts,),
-        shape(n_col // near, log_src + blk_src, 4, HALF),
-        name="src_join",
-    )
     parts = over("col", parts, apart)
     src = call(
         functools.partial(src_share_kernel, DIM),

time: 239 us -> 242 us (1.013)
  blocking collectives: 165 us -> 126 us
  Pallas kernels: 58.8 us -> 95.1 us
  starting transfers between devices: 5.78 us -> 15.9 us
    all_to_all x9 -> x8, blocking collectives: 165 us -> 126 us  [over(): return lax.all_to_all(v, axis, 0, 0, axis_index_groups=groups)]
    pallas_call x11, Pallas kernels: 58.8 us -> 95.1 us  [call(): pl.pallas_call(kernel, out_shape=outs, in_specs=[VMEM] * len(ins), out_sp...]
    ppermute x0 -> x3, starting transfers between devices: none -> 10.1 us  [local(): lax.ppermute(parts[k], 'col', [(i, near * (i // near) + (i % near ^ k)) f...]
    all_to_all x1, waiting for transfers between devices: 4.22 us -> 0.01 us  [over(): return lax.all_to_all(v, axis, 0, 0, axis_index_groups=groups)]
    ppermute x0 -> x3, waiting for transfers between devices: none -> 2.52 us  [local(): lax.ppermute(parts[k], 'col', [(i, near * (i // near) + (i % near ^ k)) f...]
  transfers between devices with their start and end apart: 1 -> 4, of which waited for: 1 -> 1; matrix products, arithmetic and copies ran while one was open for 0% -> 0% of each run, Pallas kernels for 1% -> 7%
where the time goes in v6:
time: 242 us; the launch traced here: 241 us
  blocking collectives  126 us (52%)
  Pallas kernels  95.1 us (39%)
  starting transfers between devices  15.9 us (7%)
  waiting for transfers between devices  2.53 us (1%)
    all_to_all x8, blocking collectives, over(): return lax.all_to_all(v, axis, 0, 0, axis_index_groups=groups)  126 us
    pallas_call x11, Pallas kernels, call(): pl.pallas_call(kernel, out_shape=outs, in_specs=[VMEM] * len(ins), out_sp...  95.1 us
    ppermute x3, starting transfers between devices, local(): lax.ppermute(parts[k], 'col', [(i, near * (i // near) + (i % near ^ k)) f...  10.1 us
    all_to_all x1, starting transfers between devices, over(): return lax.all_to_all(v, axis, 0, 0, axis_index_groups=groups)  5.78 us
  transfers between devices with their start and end apart: 4, of which 1 were waited for; matrix products, arithmetic and copies ran while one was open for 0% of the time, Pallas kernels for 7%

profile of v6, /device:TPU:6, one launch (start us, length us, event | category | flops | bytes accessed | tf_op | source)
XLA Modules:
  0.0 241.1 jit_solution(7851552165757879702)
XLA Ops:
  0.6 1.0 pad_maximum_fusion.xy_ref
  1.7 11.8 %start.1 = (bf16[1024,256]{1,0:T(8,128)(2,1)S(1)}, bf16[1536,256]{1,0:T(8,128)(2,1)S(1)}, bf16[256,1024]{1,0:T(8,128)(2,1)S(1)}, bf16[256,1536]{1,0:T(8,128)(2,1...) custom-call(f32[32,2560]{1,0:T(8,128)S(1)} %pad_maximum_fusion.xy_ref), custom_call_target="tpu_custom_call" | custom-call | tf_op jit(solution)/shard_map/start/pallas_call | solution.py:415
  13.5 27.7 %all_to_all.45.p = f32[16,1,8,128]{3,2,1,0:T(8,128)S(1)} all-to-all(f32[16,1,8,128]{3,2,1,0:T(8,128)S(1)} %get-tuple-element.33), channel_id=1, replica_groups=mesh['row'=32,'col'=16] {'col'}, dimensions={0} | all-to-all | bytes 131072 | tf_op jit(solution)/shard_map/all_to_all | solution.py:443
  41.2 11.8 %cols.2 = (f32[8,128]{1,0:T(8,128)S(1)}, f32[32,3,4,128]{3,2,1,0:T(4,128)S(1)}) custom-call(f32[16,1,8,128]{3,2,1,0:T(8,128)S(1)} %all_to_all.45.p, bf16[1024,256]{1,0:T(8,128)(2,1)S(1)} %get-tuple-element.34.c.col_ref, bf16[256,1536]{1,0:T(8,128)(2,1)S(1)} %get-tuple-element.35.r.row_ref.values_ref), custom_call_target="tpu_custom_call" | custom-call | tf_op jit(solution)/shard_map/cols/pallas_call | solution.py:415
  53.0 13.9 %all_to_all.46.parts_ref = f32[32,3,4,128]{3,2,1,0:T(4,128)S(1)} all-to-all(f32[32,3,4,128]{3,2,1,0:T(4,128)S(1)} %get-tuple-element.36), channel_id=1, replica_groups=mesh['row'=32,'col'=16] {'row'}, dimensions={0} | all-to-all | bytes 393216 | tf_op jit(solution)/shard_map/all_to_all | solution.py:443
  66.9 11.7 %rows.2 = (f32[12,128]{1,0:T(8,128)S(1)}, f32[16,1,8,128]{3,2,1,0:T(8,128)S(1)}) custom-call(f32[32,3,4,128]{3,2,1,0:T(4,128)S(1)} %all_to_all.46.parts_ref, bf16[1536,256]{1,0:T(8,128)(2,1)S(1)} %get-tuple-element.37.col_ref, bf16[256,1024]{1,0:T(8,128)(2,1)S(1)} %get-tuple-element.38.row_ref.values_ref, f32[8,128]{1,0:T(8,128)S(1)} %get-tuple-element.39.old_ref), custom_call_target="tpu_custom_call" | custom-call | tf_op jit(solution)/shard_map/rows/pallas_call | solution.py:415
  78.7 16.0 %all_to_all.47.parts_ref = f32[16,1,8,128]{3,2,1,0:T(8,128)S(1)} all-to-all(f32[16,1,8,128]{3,2,1,0:T(8,128)S(1)} %get-tuple-element.40), channel_id=1, replica_groups=mesh['row'=32,'col'=16] {'col'}, dimensions={0} | all-to-all | bytes 131072 | tf_op jit(solution)/shard_map/all_to_all | solution.py:443
  94.7 11.7 %cols.3 = (f32[8,128]{1,0:T(8,128)S(1)}, f32[32,3,4,128]{3,2,1,0:T(4,128)S(1)}) custom-call(f32[16,1,8,128]{3,2,1,0:T(8,128)S(1)} %all_to_all.47.parts_ref, bf16[1024,256]{1,0:T(8,128)(2,1)S(1)} %get-tuple-element.34.c.col_ref, bf16[256,1536]{1,0:T(8,128)(2,1)S(1)} %get-tuple-element.35.r.row_ref.values_ref, f32[12,128]{1,0:T(8,128)S(1)} %get-tuple-element.41.old_ref), custom_call_target="tpu_custom_call" | custom-call | tf_op jit(solution)/shard_map/cols/pallas_call | solution.py:415
  106.4 11.7 %all_to_all.48.parts_ref = f32[32,3,4,128]{3,2,1,0:T(4,128)S(1)} all-to-all(f32[32,3,4,128]{3,2,1,0:T(4,128)S(1)} %get-tuple-element.42), channel_id=1, replica_groups=mesh['row'=32,'col'=16] {'row'}, dimensions={0} | all-to-all | bytes 393216 | tf_op jit(solution)/shard_map/all_to_all | solution.py:443
  118.0 11.7 %rows.3 = (f32[12,128]{1,0:T(8,128)S(1)}, f32[16,1,8,128]{3,2,1,0:T(8,128)S(1)}) custom-call(f32[32,3,4,128]{3,2,1,0:T(4,128)S(1)} %all_to_all.48.parts_ref, bf16[1536,256]{1,0:T(8,128)(2,1)S(1)} %get-tuple-element.37.col_ref, bf16[256,1024]{1,0:T(8,128)(2,1)S(1)} %get-tuple-element.38.row_ref.values_ref, f32[8,128]{1,0:T(8,128)S(1)} %get-tuple-element.43.old_ref), custom_call_target="tpu_custom_call" | custom-call | tf_op jit(solution)/shard_map/rows/pallas_call | solution.py:415
  129.7 16.0 %all_to_all.49.parts_ref = f32[16,1,8,128]{3,2,1,0:T(8,128)S(1)} all-to-all(f32[16,1,8,128]{3,2,1,0:T(8,128)S(1)} %get-tuple-element.44), channel_id=1, replica_groups=mesh['row'=32,'col'=16] {'col'}, dimensions={0} | all-to-all | bytes 131072 | tf_op jit(solution)/shard_map/all_to_all | solution.py:443
  145.8 17.2 %tgt_part.1 = (f32[8,128]{1,0:T(8,128)S(1)}, f32[32,6,4,128]{3,2,1,0:T(4,128)S(1)}) custom-call(f32[16,1,8,128]{3,2,1,0:T(8,128)S(1)} %all_to_all.49.parts_ref, bf16[1024,256]{1,0:T(8,128)(2,1)S(1)} %get-tuple-element.34.c.col_ref, bf16[256,1536]{1,0:T(8,128)(2,1)S(1)} %get-tuple-element.35.r.row_ref.values_ref, ...), custom_call_target="tpu_custom_call" | custom-call | tf_op jit(solution)/shard_map/tgt_part/pallas_call | solution.py:415
  163.0 13.3 %all_to_all.50.parts_ref = f32[32,6,4,128]{3,2,1,0:T(4,128)S(1)} all-to-all(f32[32,6,4,128]{3,2,1,0:T(4,128)S(1)} %get-tuple-element.47), channel_id=1, replica_groups=mesh['row'=32,'col'=16] {'row'}, dimensions={0} | all-to-all | bytes 786432 | tf_op jit(solution)/shard_map/all_to_all | solution.py:443
  176.3 0.9 tgt_join.1
  177.2 5.8 %all-to-all-start.6 = ((f32[32,3,4,128]{3,2,1,0:T(4,128)}), f32[32,3,4,128]{3,2,1,0:T(4,128)S(1)}, u32[]{:S(2)}, u32[]{:S(2)}) async-start(f32[32,3,4,128]{3,2,1,0:T(4,128)} %get-tuple-element.55), calls=%async_computation.6 | async-start | bytes 393216 | tf_op jit(solution)/shard_map/all_to_all | solution.py:443
  183.0 17.3 %src_part.1 = (f32[17,4,128]{2,1,0:T(4,128)S(1)}, f32[17,4,128]{2,1,0:T(4,128)S(1)}, f32[17,4,128]{2,1,0:T(4,128)S(1)}, f32[17,4,128]{2,1,0:T(4,128)S(1)}) custom-call(f32[12,128]{1,0:T(8,128)S(1)} %get-tuple-element.48.new_ref.h_ref, bf16[1536,256]{1,0:T(8,128)(2,1)S(1)} %get-tuple-element.37.col_ref, ...), custom_call_target="tpu_custom_call" | custom-call | tf_op jit(solution)/shard_map/src_part/pallas_call | solution.py:415
  200.3 1.9 collective-permute-start
  202.2 3.1 %collective-permute-start.1 = (f32[17,4,128]{2,1,0:T(4,128)S(1)}, f32[17,4,128]{2,1,0:T(4,128)S(1)}, u32[]{:S(2)}, u32[]{:S(2)}) collective-permute-start(f32[17,4,128]{2,1,0:T(4,128)S(1)} %get-tuple-element.53), channel_id=1, source_target_pairs={{0,2},{1,3},{2,0},{3,1},{4,6},{5,7},{6,4},{7,5},{8,10},{9,11},{10,... | collective-permute-start | bytes 104456 | tf_op jit(solution)/shard_map/ppermute | solution.py:510
  205.3 5.1 %collective-permute-start.2 = (f32[17,4,128]{2,1,0:T(4,128)S(1)}, f32[17,4,128]{2,1,0:T(4,128)S(1)}, u32[]{:S(2)}, u32[]{:S(2)}) collective-permute-start(f32[17,4,128]{2,1,0:T(4,128)S(1)} %get-tuple-element.54), channel_id=1, source_target_pairs={{0,3},{1,2},{2,1},{3,0},{4,7},{5,6},{6,5},{7,4},{8,11},{9,10},{10,... | collective-permute-start | bytes 104456 | tf_op jit(solution)/shard_map/ppermute | solution.py:510
  210.5 0.0 collective-permute-done.refs_1_
  210.5 0.0 collective-permute-done.1.refs_2_
  210.5 2.5 %collective-permute-done.2.refs_3_ = f32[17,4,128]{2,1,0:T(4,128)S(1)} collective-permute-done((f32[17,4,128]{2,1,0:T(4,128)S(1)}, f32[17,4,128]{2,1,0:T(4,128)S(1)}, u32[]{:S(2)}, u32[]{:S(2)}) %collective-permute-start.2) | collective-permute-done | bytes 34848 | tf_op jit(solution)/shard_map/ppermute | solution.py:510
  213.0 0.1 src_join.1
  213.1 0.0 all-to-all-done.6.tgt_ref
  213.1 18.7 %all_to_all.51.parts_ref = f32[4,17,4,128]{3,2,1,0:T(4,128)S(1)} all-to-all(f32[4,17,4,128]{3,2,1,0:T(4,128)S(1)} %src_join.1), channel_id=1, replica_groups={{0,4,8,12},{1,5,9,13},{2,6,10,14},{3,7,11,15},{16,20,24,28},{17,21,25,2..., dimensions={0} | all-to-all | bytes 278528 | tf_op jit(solution)/shard_map/all_to_all | solution.py:443
  231.7 0.1 src_share.1
  231.8 8.6 %all_to_all.52.src_ref = f32[4,16,4,128]{3,2,1,0:T(4,128)S(1)} all-to-all(f32[4,16,4,128]{3,2,1,0:T(4,128)S(1)} %src_share.1), channel_id=1, replica_groups={{0,1,2,3},{4,5,6,7},{8,9,10,11},{12,13,14,15},{16,17,18,19},{20,21,22,2..., dimensions={0} | all-to-all | bytes 262144 | tf_op jit(solution)/shard_map/all_to_all | solution.py:443
  240.3 0.8 end.1
Async XLA Ops:
  177.2 35.8 %all-to-all-start.6 = ((f32[32,3,4,128]{3,2,1,0:T(4,128)}), f32[32,3,4,128]{3,2,1,0:T(4,128)S(1)}, u32[]{:S(2)}, u32[]{:S(2)}) async-start(f32[32,3,4,128]{3,2,1,0:T(4,128)} %get-tuple-element.55), calls=%async_computation.6 | async-start | bytes 393216 | tf_op jit(solution)/shard_map/all_to_all | solution.py:443
  200.3 10.1 %collective-permute-start = (f32[17,4,128]{2,1,0:T(4,128)S(1)}, f32[17,4,128]{2,1,0:T(4,128)S(1)}, u32[]{:S(2)}, u32[]{:S(2)}) collective-permute-start(f32[17,4,128]{2,1,0:T(4,128)S(1)} %get-tuple-element.52), channel_id=1, source_target_pairs={{0,1},{1,0},{2,3},{3,2},{4,5},{5,4},{6,7},{7,6},{8,9},{9,8},{10,11... | collective-permute-start | bytes 104456 | tf_op jit(solution)/shard_map/ppermute | solution.py:510
  202.2 8.2 %collective-permute-start.1 = (f32[17,4,128]{2,1,0:T(4,128)S(1)}, f32[17,4,128]{2,1,0:T(4,128)S(1)}, u32[]{:S(2)}, u32[]{:S(2)}) collective-permute-start(f32[17,4,128]{2,1,0:T(4,128)S(1)} %get-tuple-element.53), channel_id=1, source_target_pairs={{0,2},{1,3},{2,0},{3,1},{4,6},{5,7},{6,4},{7,5},{8,10},{9,11},{10,... | collective-permute-start | bytes 104456 | tf_op jit(solution)/shard_map/ppermute | solution.py:510
  205.3 7.7 %collective-permute-start.2 = (f32[17,4,128]{2,1,0:T(4,128)S(1)}, f32[17,4,128]{2,1,0:T(4,128)S(1)}, u32[]{:S(2)}, u32[]{:S(2)}) collective-permute-start(f32[17,4,128]{2,1,0:T(4,128)S(1)} %get-tuple-element.54), channel_id=1, source_target_pairs={{0,3},{1,2},{2,1},{3,0},{4,7},{5,6},{6,5},{7,4},{8,11},{9,10},{10,... | collective-permute-start | bytes 104456 | tf_op jit(solution)/shard_map/ppermute | solution.py:510

commit v7 on v6

--- a/solution.py
+++ b/solution.py
@@ -314,7 +314,8 @@
 
 
 def src_part_kernel(near, new_ref, col_ref, row_ref, values_ref, old_ref, *refs):
-    outs, (half_ref, shift_ref, moved_ref, image_ref, log_ref) = refs[:near], refs[near:]
+    out_refs, (half_ref, shift_ref, moved_ref, image_ref, log_ref) = refs[:-5], refs[-5:]
+    outs = [(k, out_refs[k % 2].at[k // 2]) for k in range(near)]
     half_ref[...] = column_half(as_row(new_ref[...]), 3, col_ref)
     shift_ref[...] = as_row(old_ref[...])
     args = (col_ref, half_ref, row_ref, shift_ref)
@@ -326,7 +327,7 @@
         log_ref[...] = jnp.log2(s) - as_dense(shift_ref[...])
         part = moved_ref[16:48, :] + moved_ref[48:80, :] + moved_ref[80:112, :]
         image_ref[...] = part / as_row(s)
-        for k, out_ref in enumerate(outs):
+        for k, out_ref in outs:
             out_ref[:base] = jnp.zeros((base, 4, HALF), F32)
             for c in range(each):
                 cell = near * c + (mine ^ k)
@@ -370,16 +371,18 @@
     share(parts_ref, out_ref, new_ref.shape[0] // 4, dims, logs_of)
 
 
-def src_join_kernel(base, *refs):
-    ins, (out_ref, parts_ref) = refs[:-2], refs[-2:]
-    for k, ref in enumerate(ins):
-        parts_ref[k] = ref[...]
-    out_ref[:, :base] = jnp.zeros((out_ref.shape[0], base, 4, HALF), F32)
-    for c in range((parts_ref.shape[1] - base) * 4 // DIM):
-        rows = slice(c % 4, c % 4 + 1)
-        log = joined(parts_ref[:, c // 4, rows, :])
-        out_ref[:, c // 4, rows, :] = jnp.broadcast_to(log[None], (out_ref.shape[0], 1, HALF))
-    src_share_kernel(DIM, parts_ref, out_ref.at[:, base:])
+def src_join_kernel(base, own, one_ref, other_ref, out_ref, parts_ref):
+    for k in range(out_ref.shape[0] if own is None else 1):
+        parts_ref[0] = one_ref[k if own is None else own]
+        parts_ref[1] = other_ref[k]
+        joined_ref = out_ref.at[k : k + 1] if own is None else out_ref
+        n = joined_ref.shape[0]
+        joined_ref[:, :base] = jnp.zeros((n, base, 4, HALF), F32)
+        for c in range((parts_ref.shape[1] - base) * 4 // DIM):
+            rows = slice(c % 4, c % 4 + 1)
+            log = joined(parts_ref[:, c // 4, rows, :])
+            joined_ref[:, c // 4, rows, :] = jnp.broadcast_to(log[None], (n, 1, HALF))
+        src_share_kernel(DIM, parts_ref, joined_ref.at[:, base:])
 
 
 def src_share_kernel(dims, parts_ref, out_ref):
@@ -389,22 +392,21 @@
     )
 
 
-def end_kernel(
-    dims_of, e_ref, h_ref, xsq_ref, ysq_ref, src_ref, tgt_ref, f_ref, g_ref, si_ref, ti_ref
-):
+def tgt_end_kernel(dims, e_ref, h_ref, xsq_ref, ysq_ref, tgt_ref, f_ref, g_ref, ti_ref):
     f_ref[...] = LN2 * e_ref[...] + xsq_ref[...]
     g_ref[...] = LN2 * h_ref[...] + ysq_ref[...]
-    for parts_ref, out_ref in ((src_ref, si_ref), (tgt_ref, ti_ref)):
-        n, blocks = parts_ref.shape[:2]
-        cells = out_ref.shape[1] // HALF
-        dims = dims_of[0] if out_ref is si_ref else dims_of[1]
-        groups = n * dims // DIM
-        for k in range(n):
-            top, at = dims * (k // groups), 0
-            for cell in range(k % groups, cells, groups):
-                for d in range(top, top + dims, 4):
-                    out_ref[d : d + 4, HALF * cell : HALF * (cell + 1)] = parts_ref[k, at]
-                    at += 1
+    end_kernel(dims, tgt_ref, ti_ref)
+
+
+def end_kernel(dims, parts_ref, out_ref):
+    n, cells = parts_ref.shape[0], out_ref.shape[1] // HALF
+    groups = n * dims // DIM
+    for k in range(n):
+        top, at = dims * (k // groups), 0
+        for cell in range(k % groups, cells, groups):
+            for d in range(top, top + dims, 4):
+                out_ref[d : d + 4, HALF * cell : HALF * (cell + 1)] = parts_ref[k, at]
+                at += 1
 
 
 def shape(*dims, dtype=F32):
@@ -499,27 +501,36 @@
     )
     tgt = over("row", tgt)
     block = (log_src + blk_src, 4, HALF)
-    parts = call(
+    pair = (pltpu.VMEM((2, *block), F32),)
+    keep, send = call(
         functools.partial(src_part_kernel, near),
         (h, yt, xr, yr, e),
-        tuple(shape(*block) for _ in range(near)),
+        (shape(2, *block), shape(2, *block)),
         scratch(nt, ns, HALF) + (pltpu.VMEM(x.shape, F32), pltpu.VMEM((rs, HALF), F32)),
         name="src_part",
     )
-    parts = parts[:1] + tuple(
-        lax.ppermute(
-            parts[k], "col", [(i, near * (i // near) + ((i % near) ^ k)) for i in range(n_col)]
-        )
-        for k in range(1, near)
-    )
     parts = call(
-        functools.partial(src_join_kernel, log_src),
-        parts,
+        functools.partial(src_join_kernel, log_src, None),
+        (keep, lax.ppermute(send, "col", [(i, i ^ 1) for i in range(n_col)])),
+        shape(2, *block),
+        pair,
+        name="src_join",
+    )
+    came = lax.ppermute(parts[1:], "col", [(i, i ^ 2) for i in range(n_col)])
+    f, g, ti = call(
+        functools.partial(tgt_end_kernel, dim_tgt),
+        (e, h, xsq, ysq, tgt),
+        (shape(rs, HALF), shape(rt, HALF), shape(*y.shape)),
+        name="tgt_end",
+    )
+    came, f, g, ti = lax.optimization_barrier((came, f, g, ti))
+    parts = call(
+        functools.partial(src_join_kernel, log_src, 0),
+        (parts, came),
         shape(n_col // near, *block),
-        (pltpu.VMEM((near, *block), F32),),
-        name="src_join",
-    )
-    parts, tgt = lax.optimization_barrier((parts, tgt))
+        pair,
+        name="src_join2",
+    )
     parts = over("col", parts, apart)
     src = call(
         functools.partial(src_share_kernel, DIM),
@@ -528,12 +539,7 @@
         name="src_share",
     )
     src = over("col", src, neighbours)
-    f, g, si, ti = call(
-        functools.partial(end_kernel, (DIM, dim_tgt)),
-        (e, h, xsq, ysq, src, tgt),
-        (shape(rs, HALF), shape(rt, HALF), shape(*x.shape), shape(*y.shape)),
-        name="end",
-    )
+    si = call(functools.partial(end_kernel, DIM), (src,), shape(*x.shape), name="src_end")
     return f.reshape(ns), g.reshape(nt), si, ti
 
 

time: 242 us -> 242 us (level)
  Pallas kernels: 95.1 us -> 59.9 us
  blocking collectives: 126 us -> 147 us
  starting transfers between devices: 15.9 us -> 27.5 us
  waiting for transfers between devices: 2.53 us -> 5.1 us
    pallas_call x11 -> x13, Pallas kernels: 95.1 us -> 59.9 us  [call(): pl.pallas_call(kernel, out_shape=outs, in_specs=[VMEM] * len(ins), out_sp...]
    all_to_all x8, blocking collectives: 126 us -> 147 us  [over(): return lax.all_to_all(v, axis, 0, 0, axis_index_groups=groups)]
    ppermute x3 -> x2, starting transfers between devices: 10.1 us -> 21.7 us  [the longest x1 18 us: local(): lax.ppermute(send, 'col', [(i, i ^ 1) for i in range(n_col)])]
    ppermute x3 -> x2, waiting for transfers between devices: 2.52 us -> 5.1 us  [the longest x1 2.81 us: local(): lax.ppermute(send, 'col', [(i, i ^ 1) for i in range(n_col)])]
  transfers between devices with their start and end apart: 4 -> 3, of which waited for: 1 -> 2; matrix products, arithmetic and copies ran while one was open for 0% -> 0% of each run, Pallas kernels for 7% -> 1%
where the time goes in v7:
time: 242 us; the launch traced here: 241 us
  blocking collectives  147 us (61%)
  Pallas kernels  59.9 us (25%)
  starting transfers between devices  27.5 us (11%)
  waiting for transfers between devices  5.1 us (2%)
    all_to_all x8, blocking collectives, over(): return lax.all_to_all(v, axis, 0, 0, axis_index_groups=groups)  147 us
    pallas_call x13, Pallas kernels, call(): pl.pallas_call(kernel, out_shape=outs, in_specs=[VMEM] * len(ins), out_sp...  59.9 us
    ppermute x1, starting transfers between devices, local(): lax.ppermute(send, 'col', [(i, i ^ 1) for i in range(n_col)])  18 us
    all_to_all x1, starting transfers between devices, over(): return lax.all_to_all(v, axis, 0, 0, axis_index_groups=groups)  5.78 us
  transfers between devices with their start and end apart: 3, of which 2 were waited for; matrix products, arithmetic and copies ran while one was open for 0% of the time, Pallas kernels for 1%

profile of v7, /device:TPU:6, one launch (start us, length us, event | category | flops | bytes accessed | tf_op | source)
XLA Modules:
  0.0 241.1 jit_solution(4790033162656994744)
XLA Ops:
  0.6 1.0 pad_maximum_fusion.xy_ref
  1.7 11.8 %start.1 = (bf16[1024,256]{1,0:T(8,128)(2,1)S(1)}, bf16[1536,256]{1,0:T(8,128)(2,1)S(1)}, bf16[256,1024]{1,0:T(8,128)(2,1)S(1)}, bf16[256,1536]{1,0:T(8,128)(2,1...) custom-call(f32[32,2560]{1,0:T(8,128)S(1)} %pad_maximum_fusion.xy_ref), custom_call_target="tpu_custom_call" | custom-call | tf_op jit(solution)/shard_map/start/pallas_call | solution.py:417
  13.4 27.7 %all_to_all.45.p = f32[16,1,8,128]{3,2,1,0:T(8,128)S(1)} all-to-all(f32[16,1,8,128]{3,2,1,0:T(8,128)S(1)} %get-tuple-element.32), channel_id=1, replica_groups=mesh['row'=32,'col'=16] {'col'}, dimensions={0} | all-to-all | bytes 131072 | tf_op jit(solution)/shard_map/all_to_all | solution.py:445
  41.2 11.8 %cols.2 = (f32[8,128]{1,0:T(8,128)S(1)}, f32[32,3,4,128]{3,2,1,0:T(4,128)S(1)}) custom-call(f32[16,1,8,128]{3,2,1,0:T(8,128)S(1)} %all_to_all.45.p, bf16[1024,256]{1,0:T(8,128)(2,1)S(1)} %get-tuple-element.33.c.col_ref, bf16[256,1536]{1,0:T(8,128)(2,1)S(1)} %get-tuple-element.34.r.row_ref.values_ref), custom_call_target="tpu_custom_call" | custom-call | tf_op jit(solution)/shard_map/cols/pallas_call | solution.py:417
  53.0 13.8 %all_to_all.46.parts_ref = f32[32,3,4,128]{3,2,1,0:T(4,128)S(1)} all-to-all(f32[32,3,4,128]{3,2,1,0:T(4,128)S(1)} %get-tuple-element.35), channel_id=1, replica_groups=mesh['row'=32,'col'=16] {'row'}, dimensions={0} | all-to-all | bytes 393216 | tf_op jit(solution)/shard_map/all_to_all | solution.py:445
  66.8 1.4 rows.2
  68.1 26.1 %all_to_all.47.parts_ref = f32[16,1,8,128]{3,2,1,0:T(8,128)S(1)} all-to-all(f32[16,1,8,128]{3,2,1,0:T(8,128)S(1)} %get-tuple-element.39), channel_id=1, replica_groups=mesh['row'=32,'col'=16] {'col'}, dimensions={0} | all-to-all | bytes 131072 | tf_op jit(solution)/shard_map/all_to_all | solution.py:445
  94.2 11.7 %cols.3 = (f32[8,128]{1,0:T(8,128)S(1)}, f32[32,3,4,128]{3,2,1,0:T(4,128)S(1)}) custom-call(f32[16,1,8,128]{3,2,1,0:T(8,128)S(1)} %all_to_all.47.parts_ref, bf16[1024,256]{1,0:T(8,128)(2,1)S(1)} %get-tuple-element.33.c.col_ref, bf16[256,1536]{1,0:T(8,128)(2,1)S(1)} %get-tuple-element.34.r.row_ref.values_ref, f32[12,128]{1,0:T(8,128)S(1)} %get-tuple-element.40.old_ref), custom_call_target="tpu_custom_call" | custom-call | tf_op jit(solution)/shard_map/cols/pallas_call | solution.py:417
  106.0 11.8 %all_to_all.48.parts_ref = f32[32,3,4,128]{3,2,1,0:T(4,128)S(1)} all-to-all(f32[32,3,4,128]{3,2,1,0:T(4,128)S(1)} %get-tuple-element.41), channel_id=1, replica_groups=mesh['row'=32,'col'=16] {'row'}, dimensions={0} | all-to-all | bytes 393216 | tf_op jit(solution)/shard_map/all_to_all | solution.py:445
  117.8 1.4 rows.3
  119.1 26.2 %all_to_all.49.parts_ref = f32[16,1,8,128]{3,2,1,0:T(8,128)S(1)} all-to-all(f32[16,1,8,128]{3,2,1,0:T(8,128)S(1)} %get-tuple-element.43), channel_id=1, replica_groups=mesh['row'=32,'col'=16] {'col'}, dimensions={0} | all-to-all | bytes 131072 | tf_op jit(solution)/shard_map/all_to_all | solution.py:445
  145.3 17.3 %tgt_part.1 = (f32[8,128]{1,0:T(8,128)S(1)}, f32[32,6,4,128]{3,2,1,0:T(4,128)S(1)}) custom-call(f32[16,1,8,128]{3,2,1,0:T(8,128)S(1)} %all_to_all.49.parts_ref, bf16[1024,256]{1,0:T(8,128)(2,1)S(1)} %get-tuple-element.33.c.col_ref, bf16[256,1536]{1,0:T(8,128)(2,1)S(1)} %get-tuple-element.34.r.row_ref.values_ref, ...), custom_call_target="tpu_custom_call" | custom-call | tf_op jit(solution)/shard_map/tgt_part/pallas_call | solution.py:417
  162.5 13.4 %all_to_all.50.parts_ref = f32[32,6,4,128]{3,2,1,0:T(4,128)S(1)} all-to-all(f32[32,6,4,128]{3,2,1,0:T(4,128)S(1)} %get-tuple-element.45), channel_id=1, replica_groups=mesh['row'=32,'col'=16] {'row'}, dimensions={0} | all-to-all | bytes 786432 | tf_op jit(solution)/shard_map/all_to_all | solution.py:445
  175.9 0.9 tgt_join.1
  176.8 5.8 %all-to-all-start.6 = ((f32[32,3,4,128]{3,2,1,0:T(4,128)}), f32[32,3,4,128]{3,2,1,0:T(4,128)S(1)}, u32[]{:S(2)}, u32[]{:S(2)}) async-start(f32[32,3,4,128]{3,2,1,0:T(4,128)} %get-tuple-element.52), calls=%async_computation.6 | async-start | bytes 393216 | tf_op jit(solution)/shard_map/all_to_all | solution.py:445
  182.6 2.2 src_part.1
  184.8 18.0 %collective-permute-start = (f32[2,17,4,128]{3,2,1,0:T(4,128)S(1)}, f32[2,17,4,128]{3,2,1,0:T(4,128)S(1)}, u32[]{:S(2)}, u32[]{:S(2)}) collective-permute-start(f32[2,17,4,128]{3,2,1,0:T(4,128)S(1)} %get-tuple-element.49), channel_id=1, source_target_pairs={{0,1},{1,0},{2,3},{3,2},{4,5},{5,4},{6,7},{7,6},{8,9},{9,8},{10,11... | collective-permute-start | bytes 208904 | tf_op jit(solution)/shard_map/ppermute | solution.py:514
  202.8 2.8 %collective-permute-done.other_ref = f32[2,17,4,128]{3,2,1,0:T(4,128)S(1)} collective-permute-done((f32[2,17,4,128]{3,2,1,0:T(4,128)S(1)}, f32[2,17,4,128]{3,2,1,0:T(4,128)S(1)}, u32[]{:S(2)}, u32[]{:S(2)}) %collective-permute-start) | collective-permute-done | bytes 69664 | tf_op jit(solution)/shard_map/ppermute | solution.py:514
  205.6 0.1 src_join.1.one_ref
  205.7 3.7 %collective-permute-start.1 = (f32[1,17,4,128]{3,2,1,0:T(4,128)S(1)}, f32[1,17,4,128]{3,2,1,0:T(4,128)S(1)}, u32[]{:S(2)}, u32[]{:S(2)}) collective-permute-start(f32[1,17,4,128]{3,2,1,0:T(4,128)S(1)} %slice.4), channel_id=1, source_target_pairs={{0,2},{1,3},{2,0},{3,1},{4,6},{5,7},{6,4},{7,5},{8,10},{9,11},{10,... | collective-permute-start | bytes 104456 | tf_op jit(solution)/shard_map/ppermute | solution.py:519
  209.4 0.0 all-to-all-done.6.tgt_ref
  209.4 0.7 tgt_end.1
  210.2 2.3 collective-permute-done.1.other_ref
  212.5 18.6 %all_to_all.51.parts_ref = f32[4,17,4,128]{3,2,1,0:T(4,128)S(1)} all-to-all(f32[4,17,4,128]{3,2,1,0:T(4,128)S(1)} %src_join2.1), channel_id=1, replica_groups={{0,4,8,12},{1,5,9,13},{2,6,10,14},{3,7,11,15},{16,20,24,28},{17,21,25,2..., dimensions={0} | all-to-all | bytes 278528 | tf_op jit(solution)/shard_map/all_to_all | solution.py:445
  231.1 0.1 src_share.1
  231.2 9.2 %all_to_all.52.parts_ref = f32[4,16,4,128]{3,2,1,0:T(4,128)S(1)} all-to-all(f32[4,16,4,128]{3,2,1,0:T(4,128)S(1)} %src_share.1), channel_id=1, replica_groups={{0,1,2,3},{4,5,6,7},{8,9,10,11},{12,13,14,15},{16,17,18,19},{20,21,22,2..., dimensions={0} | all-to-all | bytes 262144 | tf_op jit(solution)/shard_map/all_to_all | solution.py:445
  240.4 0.7 src_end.1
  (2 shorter events, 0.1 us)
Async XLA Ops:
  176.8 32.6 %all-to-all-start.6 = ((f32[32,3,4,128]{3,2,1,0:T(4,128)}), f32[32,3,4,128]{3,2,1,0:T(4,128)S(1)}, u32[]{:S(2)}, u32[]{:S(2)}) async-start(f32[32,3,4,128]{3,2,1,0:T(4,128)} %get-tuple-element.52), calls=%async_computation.6 | async-start | bytes 393216 | tf_op jit(solution)/shard_map/all_to_all | solution.py:445
  184.8 20.8 %collective-permute-start = (f32[2,17,4,128]{3,2,1,0:T(4,128)S(1)}, f32[2,17,4,128]{3,2,1,0:T(4,128)S(1)}, u32[]{:S(2)}, u32[]{:S(2)}) collective-permute-start(f32[2,17,4,128]{3,2,1,0:T(4,128)S(1)} %get-tuple-element.49), channel_id=1, source_target_pairs={{0,1},{1,0},{2,3},{3,2},{4,5},{5,4},{6,7},{7,6},{8,9},{9,8},{10,11... | collective-permute-start | bytes 208904 | tf_op jit(solution)/shard_map/ppermute | solution.py:514
  205.7 6.7 %collective-permute-start.1 = (f32[1,17,4,128]{3,2,1,0:T(4,128)S(1)}, f32[1,17,4,128]{3,2,1,0:T(4,128)S(1)}, u32[]{:S(2)}, u32[]{:S(2)}) collective-permute-start(f32[1,17,4,128]{3,2,1,0:T(4,128)S(1)} %slice.4), channel_id=1, source_target_pairs={{0,2},{1,3},{2,0},{3,1},{4,6},{5,7},{6,4},{7,5},{8,10},{9,11},{10,... | collective-permute-start | bytes 104456 | tf_op jit(solution)/shard_map/ppermute | solution.py:519

commit v8 on v7

--- a/solution.py
+++ b/solution.py
@@ -14,6 +14,7 @@
 DEPTH = 256
 HALF = 128
 DIM = 32
+NEAR = 4
 TILE = 256
 CHUNK = 256
 PROBE = 64
@@ -313,28 +314,39 @@
     )
 
 
-def src_part_kernel(near, new_ref, col_ref, row_ref, values_ref, old_ref, *refs):
-    out_refs, (half_ref, shift_ref, moved_ref, image_ref, log_ref) = refs[:-5], refs[-5:]
-    outs = [(k, out_refs[k % 2].at[k // 2]) for k in range(near)]
-    half_ref[...] = column_half(as_row(new_ref[...]), 3, col_ref)
-    shift_ref[...] = as_row(old_ref[...])
-    args = (col_ref, half_ref, row_ref, shift_ref)
-    mine = lax.rem(lax.axis_index("col"), near)
-    each = log_ref.shape[0] // near
-    base = -(-each // 4)
+def src_part_kernel(
+    flip, half_in, e_ref, row_ref, values_ref, col_ref, h_ref,
+    out_ref, half_ref,
+    rows_ref, shift_ref, moved_ref,
+):
+    if half_in is None:
+        half_ref[...] = column_half(as_row(h_ref[...]), 3, col_ref)
+    else:
+        half_ref = half_in
+    mine = lax.rem(lax.axis_index("col"), NEAR)
+    count = rows_ref.shape[1] // 2
+    cells = count // HALF
+    for k in range(2):
+        part = mine ^ (flip ^ 2 * k)
+        at = slice(count * k, count * (k + 1))
+        rows_ref[:, at] = row_ref[:, pl.ds(pl.multiple_of(count * part, count), count)]
+        shift_ref[:, at] = as_row(e_ref[pl.ds(cells * part, cells), :])
+    args = (col_ref, half_ref, rows_ref, shift_ref)
 
     def finish(s):
-        log_ref[...] = jnp.log2(s) - as_dense(shift_ref[...])
+        log = jnp.log2(s) - as_dense(shift_ref[...])
         part = moved_ref[16:48, :] + moved_ref[48:80, :] + moved_ref[80:112, :]
-        image_ref[...] = part / as_row(s)
-        for k, out_ref in outs:
-            out_ref[:base] = jnp.zeros((base, 4, HALF), F32)
-            for c in range(each):
-                cell = near * c + (mine ^ k)
-                lanes = pl.ds(pl.multiple_of(HALF * cell, HALF), HALF)
-                out_ref[c // 4, c % 4 : c % 4 + 1, :] = log_ref[pl.ds(cell, 1), :]
+        part = part / as_row(s)
+        for k in range(2):
+            out_ref[k, 0] = jnp.concatenate(
+                [log[cells * k : cells * (k + 1)], jnp.zeros((4 - cells, HALF), F32)], axis=0
+            )
+            for c in range(cells):
+                cell = cells * k + c
                 for u in range(DIM // 4):
-                    out_ref[base + DIM // 4 * c + u] = image_ref[4 * u : 4 * u + 4, lanes]
+                    out_ref[k, 1 + DIM // 4 * c + u] = part[
+                        4 * u : 4 * u + 4, HALF * cell : HALF * (cell + 1)
+                    ]
 
     guarded(
         lambda: maps(*args, values_ref, moved_ref, 0),
@@ -344,6 +356,14 @@
         *args,
         0,
     )
+
+
+def src_send_kernel(h_ref, col_ref, row_ref, values_ref, e_ref, out_ref, half_ref, *scratch):
+    src_part_kernel(1, None, e_ref, row_ref, values_ref, col_ref, h_ref, out_ref, half_ref, *scratch)
+
+
+def src_keep_kernel(half_ref, col_ref, row_ref, values_ref, e_ref, out_ref, *scratch):
+    src_part_kernel(0, half_ref, e_ref, row_ref, values_ref, col_ref, None, out_ref, None, *scratch)
 
 
 def share(parts_ref, out_ref, base, dims, logs_of):
@@ -403,7 +423,11 @@
     groups = n * dims // DIM
     for k in range(n):
         top, at = dims * (k // groups), 0
-        for cell in range(k % groups, cells, groups):
+        if dims == DIM:
+            span = range(k * cells // n, (k + 1) * cells // n)
+        else:
+            span = range(k % groups, cells, groups)
+        for cell in span:
             for d in range(top, top + dims, 4):
                 out_ref[d : d + 4, HALF * cell : HALF * (cell + 1)] = parts_ref[k, at]
                 at += 1
@@ -413,7 +437,7 @@
     return jax.ShapeDtypeStruct(dims, dtype)
 
 
-def call(kernel, ins, outs, scratch=(), name=None):
+def call(kernel, ins, outs, scratch=(), name=None, cost=None):
     return pl.pallas_call(
         kernel,
         out_shape=outs,
@@ -422,6 +446,7 @@
         scratch_shapes=list(scratch),
         compiler_params=pltpu.CompilerParams(vmem_limit_bytes=32 * 2**20),
         name=name,
+        cost_estimate=cost,
     )(*ins)
 
 
@@ -433,7 +458,7 @@
     dim_tgt = DIM // min(n_row, 8)
     grp_tgt = n_row * dim_tgt // DIM
     blk_tgt = nt * DIM // n_row // 512
-    near = min(n_col, 4)
+    near = NEAR
     neighbours = [[near * k + j for j in range(near)] for k in range(n_col // near)]
     apart = [[near * k + j for k in range(n_col // near)] for j in range(near)]
     blk_src, log_src = ns * DIM // near // 512, -(-rs // near // 4)
@@ -502,16 +527,28 @@
     tgt = over("row", tgt)
     block = (log_src + blk_src, 4, HALF)
     pair = (pltpu.VMEM((2, *block), F32),)
-    keep, send = call(
-        functools.partial(src_part_kernel, near),
+    half = shape(2, *block)
+    src_scratch = (
+        pltpu.VMEM((DEPTH, ns // 2), BF),
+        pltpu.VMEM((1, ns // 2), F32),
+        pltpu.VMEM((HALF, ns // 2), F32),
+    )
+    work = pl.CostEstimate(flops=2 * 2**29, bytes_accessed=2**21, transcendentals=2**20)
+    send, half_h = call(
+        src_send_kernel,
         (h, yt, xr, yr, e),
-        (shape(2, *block), shape(2, *block)),
-        scratch(nt, ns, HALF) + (pltpu.VMEM(x.shape, F32), pltpu.VMEM((rs, HALF), F32)),
-        name="src_part",
+        (half, shape(nt, HALF, dtype=BF)),
+        src_scratch,
+        name="src_send",
+        cost=work,
+    )
+    send = lax.ppermute(send, "col", [(i, i ^ 1) for i in range(n_col)])
+    keep = call(
+        src_keep_kernel, (half_h, yt, xr, yr, e), half, src_scratch, name="src_keep", cost=work
     )
     parts = call(
         functools.partial(src_join_kernel, log_src, None),
-        (keep, lax.ppermute(send, "col", [(i, i ^ 1) for i in range(n_col)])),
+        (keep, send),
         shape(2, *block),
         pair,
         name="src_join",

time: 242 us -> 238 us (0.983)
  Pallas kernels: 59.9 us -> 88.4 us
  blocking collectives: 147 us -> 127 us
  starting transfers between devices: 27.5 us -> 15.7 us
    pallas_call x13 -> x14, Pallas kernels: 59.9 us -> 88.4 us  [call(): pl.pallas_call(kernel, out_shape=outs, in_specs=[VMEM] * len(ins), out_sp...]
    all_to_all x8, blocking collectives: 147 us -> 127 us  [over(): return lax.all_to_all(v, axis, 0, 0, axis_index_groups=groups)]
    ppermute x1, starting transfers between devices: 18 us -> 1.92 us  [local(): send = lax.ppermute(send, 'col', [(i, i ^ 1) for i in range(n_col)])]
    ppermute x1, starting transfers between devices: 3.7 us -> 8.02 us  [local(): came = lax.ppermute(parts[1:], 'col', [(i, i ^ 2) for i in range(n_col)])]
  transfers between devices with their start and end apart: 3 -> 3, of which waited for: 2 -> 2; matrix products, arithmetic and copies ran while one was open for 0% -> 0% of each run, Pallas kernels for 1% -> 5%
where the time goes in v8:
time: 238 us; the launch traced here: 237 us
  blocking collectives  127 us (53%)
  Pallas kernels  88.4 us (37%)
  starting transfers between devices  15.7 us (7%)
  waiting for transfers between devices  4.11 us (2%)
    all_to_all x8, blocking collectives, over(): return lax.all_to_all(v, axis, 0, 0, axis_index_groups=groups)  127 us
    pallas_call x14, Pallas kernels, call(): pl.pallas_call(kernel, out_shape=outs, in_specs=[VMEM] * len(ins), out_sp...  88.4 us
    ppermute x1, starting transfers between devices, local(): came = lax.ppermute(parts[1:], 'col', [(i, i ^ 2) for i in range(n_col)])  8.02 us
    all_to_all x1, starting transfers between devices, over(): return lax.all_to_all(v, axis, 0, 0, axis_index_groups=groups)  5.78 us
  transfers between devices with their start and end apart: 3, of which 2 were waited for; matrix products, arithmetic and copies ran while one was open for 0% of the time, Pallas kernels for 5%

profile of v8, /device:TPU:6, one launch (start us, length us, event | category | flops | bytes accessed | tf_op | source)
XLA Modules:
  0.0 236.9 jit_solution(6488166851436791684)
XLA Ops:
  0.6 1.0 pad_maximum_fusion.xy_ref
  1.7 11.8 %start.1 = (bf16[1024,256]{1,0:T(8,128)(2,1)S(1)}, bf16[1536,256]{1,0:T(8,128)(2,1)S(1)}, bf16[256,1024]{1,0:T(8,128)(2,1)S(1)}, bf16[256,1536]{1,0:T(8,128)(2,1...) custom-call(f32[32,2560]{1,0:T(8,128)S(1)} %pad_maximum_fusion.xy_ref), custom_call_target="tpu_custom_call" | custom-call | tf_op jit(solution)/shard_map/start/pallas_call | solution.py:441
  13.4 27.7 %all_to_all.45.p = f32[16,1,8,128]{3,2,1,0:T(8,128)S(1)} all-to-all(f32[16,1,8,128]{3,2,1,0:T(8,128)S(1)} %get-tuple-element.32), channel_id=1, replica_groups=mesh['row'=32,'col'=16] {'col'}, dimensions={0} | all-to-all | bytes 131072 | tf_op jit(solution)/shard_map/all_to_all | solution.py:470
  41.2 11.8 %cols.2 = (f32[8,128]{1,0:T(8,128)S(1)}, f32[32,3,4,128]{3,2,1,0:T(4,128)S(1)}) custom-call(f32[16,1,8,128]{3,2,1,0:T(8,128)S(1)} %all_to_all.45.p, bf16[1024,256]{1,0:T(8,128)(2,1)S(1)} %get-tuple-element.33.c.col_ref, bf16[256,1536]{1,0:T(8,128)(2,1)S(1)} %get-tuple-element.34.r.row_ref.values_ref), custom_call_target="tpu_custom_call" | custom-call | tf_op jit(solution)/shard_map/cols/pallas_call | solution.py:441
  53.0 13.8 %all_to_all.46.parts_ref = f32[32,3,4,128]{3,2,1,0:T(4,128)S(1)} all-to-all(f32[32,3,4,128]{3,2,1,0:T(4,128)S(1)} %get-tuple-element.35), channel_id=1, replica_groups=mesh['row'=32,'col'=16] {'row'}, dimensions={0} | all-to-all | bytes 393216 | tf_op jit(solution)/shard_map/all_to_all | solution.py:470
  66.8 11.6 %rows.2 = (f32[12,128]{1,0:T(8,128)S(1)}, f32[16,1,8,128]{3,2,1,0:T(8,128)S(1)}) custom-call(f32[32,3,4,128]{3,2,1,0:T(4,128)S(1)} %all_to_all.46.parts_ref, bf16[1536,256]{1,0:T(8,128)(2,1)S(1)} %get-tuple-element.36.col_ref, bf16[256,1024]{1,0:T(8,128)(2,1)S(1)} %get-tuple-element.37.row_ref.values_ref, f32[8,128]{1,0:T(8,128)S(1)} %get-tuple-element.38.old_ref), custom_call_target="tpu_custom_call" | custom-call | tf_op jit(solution)/shard_map/rows/pallas_call | solution.py:441
  78.4 15.8 %all_to_all.47.parts_ref = f32[16,1,8,128]{3,2,1,0:T(8,128)S(1)} all-to-all(f32[16,1,8,128]{3,2,1,0:T(8,128)S(1)} %get-tuple-element.39), channel_id=1, replica_groups=mesh['row'=32,'col'=16] {'col'}, dimensions={0} | all-to-all | bytes 131072 | tf_op jit(solution)/shard_map/all_to_all | solution.py:470
  94.2 11.7 %cols.3 = (f32[8,128]{1,0:T(8,128)S(1)}, f32[32,3,4,128]{3,2,1,0:T(4,128)S(1)}) custom-call(f32[16,1,8,128]{3,2,1,0:T(8,128)S(1)} %all_to_all.47.parts_ref, bf16[1024,256]{1,0:T(8,128)(2,1)S(1)} %get-tuple-element.33.c.col_ref, bf16[256,1536]{1,0:T(8,128)(2,1)S(1)} %get-tuple-element.34.r.row_ref.values_ref, f32[12,128]{1,0:T(8,128)S(1)} %get-tuple-element.40.old_ref), custom_call_target="tpu_custom_call" | custom-call | tf_op jit(solution)/shard_map/cols/pallas_call | solution.py:441
  106.0 11.8 %all_to_all.48.parts_ref = f32[32,3,4,128]{3,2,1,0:T(4,128)S(1)} all-to-all(f32[32,3,4,128]{3,2,1,0:T(4,128)S(1)} %get-tuple-element.41), channel_id=1, replica_groups=mesh['row'=32,'col'=16] {'row'}, dimensions={0} | all-to-all | bytes 393216 | tf_op jit(solution)/shard_map/all_to_all | solution.py:470
  117.8 11.6 %rows.3 = (f32[12,128]{1,0:T(8,128)S(1)}, f32[16,1,8,128]{3,2,1,0:T(8,128)S(1)}) custom-call(f32[32,3,4,128]{3,2,1,0:T(4,128)S(1)} %all_to_all.48.parts_ref, bf16[1536,256]{1,0:T(8,128)(2,1)S(1)} %get-tuple-element.36.col_ref, bf16[256,1024]{1,0:T(8,128)(2,1)S(1)} %get-tuple-element.37.row_ref.values_ref, f32[8,128]{1,0:T(8,128)S(1)} %get-tuple-element.42.old_ref), custom_call_target="tpu_custom_call" | custom-call | tf_op jit(solution)/shard_map/rows/pallas_call | solution.py:441
  129.4 16.0 %all_to_all.49.parts_ref = f32[16,1,8,128]{3,2,1,0:T(8,128)S(1)} all-to-all(f32[16,1,8,128]{3,2,1,0:T(8,128)S(1)} %get-tuple-element.43), channel_id=1, replica_groups=mesh['row'=32,'col'=16] {'col'}, dimensions={0} | all-to-all | bytes 131072 | tf_op jit(solution)/shard_map/all_to_all | solution.py:470
  145.4 17.3 %tgt_part.1 = (f32[8,128]{1,0:T(8,128)S(1)}, f32[32,6,4,128]{3,2,1,0:T(4,128)S(1)}) custom-call(f32[16,1,8,128]{3,2,1,0:T(8,128)S(1)} %all_to_all.49.parts_ref, bf16[1024,256]{1,0:T(8,128)(2,1)S(1)} %get-tuple-element.33.c.col_ref, bf16[256,1536]{1,0:T(8,128)(2,1)S(1)} %get-tuple-element.34.r.row_ref.values_ref, ...), custom_call_target="tpu_custom_call" | custom-call | tf_op jit(solution)/shard_map/tgt_part/pallas_call | solution.py:441
  162.6 13.3 %all_to_all.50.parts_ref = f32[32,6,4,128]{3,2,1,0:T(4,128)S(1)} all-to-all(f32[32,6,4,128]{3,2,1,0:T(4,128)S(1)} %get-tuple-element.45), channel_id=1, replica_groups=mesh['row'=32,'col'=16] {'row'}, dimensions={0} | all-to-all | bytes 786432 | tf_op jit(solution)/shard_map/all_to_all | solution.py:470
  175.9 0.9 tgt_join.1
  176.8 5.8 %all-to-all-start.6 = ((f32[32,3,4,128]{3,2,1,0:T(4,128)}), f32[32,3,4,128]{3,2,1,0:T(4,128)S(1)}, u32[]{:S(2)}, u32[]{:S(2)}) async-start(f32[32,3,4,128]{3,2,1,0:T(4,128)} %get-tuple-element.52), calls=%async_computation.6 | async-start | bytes 393216 | tf_op jit(solution)/shard_map/all_to_all | solution.py:470
  182.6 8.8 %src_send.1 = (f32[2,17,4,128]{3,2,1,0:T(4,128)S(1)}, bf16[1536,128]{1,0:T(8,128)(2,1)S(1)}) custom-call(f32[12,128]{1,0:T(8,128)S(1)} %get-tuple-element.46.h_ref, bf16[1536,256]{1,0:T(8,128)(2,1)S(1)} %get-tuple-element.36.col_ref, bf16[256,1024]{1,0:T(8,128)(2,1)S(1)} %get-tuple-element.37.row_ref.values_ref, ...), custom_call_target="tpu_custom_call" | custom-call | flops 1073741824 | bytes 2097152 | tf_op jit(solution)/shard_map/src_send/pallas_call | solution.py:441
  191.4 1.9 collective-permute-start
  193.3 1.3 src_keep.1.one_ref
  194.6 3.0 %collective-permute-done.other_ref = f32[2,17,4,128]{3,2,1,0:T(4,128)S(1)} collective-permute-done((f32[2,17,4,128]{3,2,1,0:T(4,128)S(1)}, f32[2,17,4,128]{3,2,1,0:T(4,128)S(1)}, u32[]{:S(2)}, u32[]{:S(2)}) %collective-permute-start) | collective-permute-done | bytes 69664 | tf_op jit(solution)/shard_map/ppermute | solution.py:545
  197.6 0.1 src_join.1.one_ref
  197.7 8.0 %collective-permute-start.1 = (f32[1,17,4,128]{3,2,1,0:T(4,128)S(1)}, f32[1,17,4,128]{3,2,1,0:T(4,128)S(1)}, u32[]{:S(2)}, u32[]{:S(2)}) collective-permute-start(f32[1,17,4,128]{3,2,1,0:T(4,128)S(1)} %slice.4), channel_id=1, source_target_pairs={{0,2},{1,3},{2,0},{3,1},{4,6},{5,7},{6,4},{7,5},{8,10},{9,11},{10,... | collective-permute-start | bytes 104456 | tf_op jit(solution)/shard_map/ppermute | solution.py:556
  205.7 0.0 all-to-all-done.6.tgt_ref
  205.7 0.7 tgt_end.1
  206.4 1.2 collective-permute-done.1.other_ref
  207.6 19.0 %all_to_all.51.parts_ref = f32[4,17,4,128]{3,2,1,0:T(4,128)S(1)} all-to-all(f32[4,17,4,128]{3,2,1,0:T(4,128)S(1)} %src_join2.1), channel_id=1, replica_groups={{0,4,8,12},{1,5,9,13},{2,6,10,14},{3,7,11,15},{16,20,24,28},{17,21,25,2..., dimensions={0} | all-to-all | bytes 278528 | tf_op jit(solution)/shard_map/all_to_all | solution.py:470
  226.7 0.1 src_share.1
  226.7 9.5 %all_to_all.52.parts_ref = f32[4,16,4,128]{3,2,1,0:T(4,128)S(1)} all-to-all(f32[4,16,4,128]{3,2,1,0:T(4,128)S(1)} %src_share.1), channel_id=1, replica_groups={{0,1,2,3},{4,5,6,7},{8,9,10,11},{12,13,14,15},{16,17,18,19},{20,21,22,2..., dimensions={0} | all-to-all | bytes 262144 | tf_op jit(solution)/shard_map/all_to_all | solution.py:470
  236.2 0.7 src_end.1
  (2 shorter events, 0.1 us)
Async XLA Ops:
  176.8 28.9 %all-to-all-start.6 = ((f32[32,3,4,128]{3,2,1,0:T(4,128)}), f32[32,3,4,128]{3,2,1,0:T(4,128)S(1)}, u32[]{:S(2)}, u32[]{:S(2)}) async-start(f32[32,3,4,128]{3,2,1,0:T(4,128)} %get-tuple-element.52), calls=%async_computation.6 | async-start | bytes 393216 | tf_op jit(solution)/shard_map/all_to_all | solution.py:470
  191.4 6.2 %collective-permute-start = (f32[2,17,4,128]{3,2,1,0:T(4,128)S(1)}, f32[2,17,4,128]{3,2,1,0:T(4,128)S(1)}, u32[]{:S(2)}, u32[]{:S(2)}) collective-permute-start(f32[2,17,4,128]{3,2,1,0:T(4,128)S(1)} %get-tuple-element.49), channel_id=1, source_target_pairs={{0,1},{1,0},{2,3},{3,2},{4,5},{5,4},{6,7},{7,6},{8,9},{9,8},{10,11... | collective-permute-start | bytes 208904 | tf_op jit(solution)/shard_map/ppermute | solution.py:545
  197.7 9.9 %collective-permute-start.1 = (f32[1,17,4,128]{3,2,1,0:T(4,128)S(1)}, f32[1,17,4,128]{3,2,1,0:T(4,128)S(1)}, u32[]{:S(2)}, u32[]{:S(2)}) collective-permute-start(f32[1,17,4,128]{3,2,1,0:T(4,128)S(1)} %slice.4), channel_id=1, source_target_pairs={{0,2},{1,3},{2,0},{3,1},{4,6},{5,7},{6,4},{7,5},{8,10},{9,11},{10,... | collective-permute-start | bytes 104456 | tf_op jit(solution)/shard_map/ppermute | solution.py:556

commit v9 on v8

--- a/solution.py
+++ b/solution.py
@@ -21,6 +21,7 @@
 LOW, HIGH = 2.0**-90, 2.0**100
 BF, F32 = jnp.bfloat16, jnp.float32
 VMEM = pl.BlockSpec(memory_space=pltpu.VMEM)
+HBM = pl.BlockSpec(memory_space=pltpu.HBM)
 
 
 def rounded(v):
@@ -314,15 +315,9 @@
     )
 
 
-def src_part_kernel(
-    flip, half_in, e_ref, row_ref, values_ref, col_ref, h_ref,
-    out_ref, half_ref,
-    rows_ref, shift_ref, moved_ref,
+def src_part(
+    flip, half_ref, col_ref, row_ref, values_ref, e_ref, out_ref, rows_ref, shift_ref, moved_ref
 ):
-    if half_in is None:
-        half_ref[...] = column_half(as_row(h_ref[...]), 3, col_ref)
-    else:
-        half_ref = half_in
     mine = lax.rem(lax.axis_index("col"), NEAR)
     count = rows_ref.shape[1] // 2
     cells = count // HALF
@@ -358,12 +353,23 @@
     )
 
 
-def src_send_kernel(h_ref, col_ref, row_ref, values_ref, e_ref, out_ref, half_ref, *scratch):
-    src_part_kernel(1, None, e_ref, row_ref, values_ref, col_ref, h_ref, out_ref, half_ref, *scratch)
+def src_send_kernel(
+    total, dims, groups,
+    parts_ref, col_ref, row_ref, values_ref, e_ref,
+    new_ref, half_ref, out_ref, tgt_out,
+    tgt_ref, sem, *scratch,
+):
+    tgt_share(dims, groups, parts_ref, tgt_ref)
+    copy = pltpu.make_async_copy(tgt_ref, tgt_out, sem)
+    copy.start()
+    joined_rows(total, parts_ref.at[:, : new_ref.shape[0] // 4], new_ref)
+    half_ref[...] = column_half(as_row(new_ref[...]), 3, col_ref)
+    src_part(1, half_ref, col_ref, row_ref, values_ref, e_ref, out_ref, *scratch)
+    copy.wait()
 
 
 def src_keep_kernel(half_ref, col_ref, row_ref, values_ref, e_ref, out_ref, *scratch):
-    src_part_kernel(0, half_ref, e_ref, row_ref, values_ref, col_ref, None, out_ref, None, *scratch)
+    src_part(0, half_ref, col_ref, row_ref, values_ref, e_ref, out_ref, *scratch)
 
 
 def share(parts_ref, out_ref, base, dims, logs_of):
@@ -379,16 +385,15 @@
             out_ref[:, at] = jnp.broadcast_to(part[None], (n, 4, HALF))
 
 
-def tgt_join_kernel(total, dims, groups, parts_ref, new_ref, out_ref):
-    logs_ref = parts_ref.at[:, : new_ref.shape[0] // 4]
-    joined_rows(total, logs_ref, new_ref)
+def tgt_share(dims, groups, parts_ref, out_ref):
+    base = parts_ref.shape[1] - out_ref.shape[1]
     group = lax.rem(lax.axis_index("row"), groups)
 
     def logs_of(c):
         cell = groups * c + group
-        return logs_ref[:, cell // 4, pl.ds(lax.rem(cell, 4), 1), :]
-
-    share(parts_ref, out_ref, new_ref.shape[0] // 4, dims, logs_of)
+        return parts_ref[:, cell // 4, pl.ds(lax.rem(cell, 4), 1), :]
+
+    share(parts_ref, out_ref, base, dims, logs_of)
 
 
 def src_join_kernel(base, own, one_ref, other_ref, out_ref, parts_ref):
@@ -437,12 +442,12 @@
     return jax.ShapeDtypeStruct(dims, dtype)
 
 
-def call(kernel, ins, outs, scratch=(), name=None, cost=None):
+def call(kernel, ins, outs, scratch=(), name=None, cost=None, out_specs=None):
     return pl.pallas_call(
         kernel,
         out_shape=outs,
         in_specs=[VMEM] * len(ins),
-        out_specs=jax.tree.map(lambda _: VMEM, outs),
+        out_specs=out_specs or jax.tree.map(lambda _: VMEM, outs),
         scratch_shapes=list(scratch),
         compiler_params=pltpu.CompilerParams(vmem_limit_bytes=32 * 2**20),
         name=name,
@@ -518,13 +523,6 @@
         name="tgt_part",
     )
     parts = over("row", parts)
-    h, tgt = call(
-        functools.partial(tgt_join_kernel, all_src, dim_tgt, grp_tgt),
-        (parts,),
-        (shape(rt, HALF), shape(n_row, blk_tgt, 4, HALF)),
-        name="tgt_join",
-    )
-    tgt = over("row", tgt)
     block = (log_src + blk_src, 4, HALF)
     pair = (pltpu.VMEM((2, *block), F32),)
     half = shape(2, *block)
@@ -534,14 +532,16 @@
         pltpu.VMEM((HALF, ns // 2), F32),
     )
     work = pl.CostEstimate(flops=2 * 2**29, bytes_accessed=2**21, transcendentals=2**20)
-    send, half_h = call(
-        src_send_kernel,
-        (h, yt, xr, yr, e),
-        (half, shape(nt, HALF, dtype=BF)),
-        src_scratch,
+    h, half_h, send, tgt = call(
+        functools.partial(src_send_kernel, all_src, dim_tgt, grp_tgt),
+        (parts, yt, xr, yr, e),
+        (shape(rt, HALF), shape(nt, HALF, dtype=BF), half, shape(n_row, blk_tgt, 4, HALF)),
+        (pltpu.VMEM((n_row, blk_tgt, 4, HALF), F32), pltpu.SemaphoreType.DMA) + src_scratch,
         name="src_send",
         cost=work,
-    )
+        out_specs=(VMEM, VMEM, VMEM, HBM),
+    )
+    tgt = over("row", tgt)
     send = lax.ppermute(send, "col", [(i, i ^ 1) for i in range(n_col)])
     keep = call(
         src_keep_kernel, (half_h, yt, xr, yr, e), half, src_scratch, name="src_keep", cost=work

time: 238 us -> 237 us (level)
    all_to_all x1, starting transfers between devices: 5.78 us -> 12.5 us  [over(): return lax.all_to_all(v, axis, 0, 0, axis_index_groups=groups)]
    ppermute x1, starting transfers between devices: 8.02 us -> 2.47 us  [local(): came = lax.ppermute(parts[1:], 'col', [(i, i ^ 2) for i in range(n_col)])]
    ppermute x1, waiting for transfers between devices: 1.16 us -> 4.29 us  [local(): came = lax.ppermute(parts[1:], 'col', [(i, i ^ 2) for i in range(n_col)])]
    ppermute x1, waiting for transfers between devices: 2.95 us -> 0.01 us  [local(): send = lax.ppermute(send, 'col', [(i, i ^ 1) for i in range(n_col)])]
    pallas_call x14 -> x13, Pallas kernels: 88.4 us -> 87.5 us  [call(): pl.pallas_call(kernel, out_shape=outs, in_specs=[VMEM] * len(ins), out_sp...]
  transfers between devices with their start and end apart: 3 -> 3, of which waited for: 2 -> 1; matrix products, arithmetic and copies ran while one was open for 0% -> 0% of each run, Pallas kernels for 5% -> 4%
where the time goes in v9:
time: 237 us; the launch traced here: 236 us
  blocking collectives  125 us (53%)
  Pallas kernels  87.5 us (37%)
  starting transfers between devices  18 us (8%)
  waiting for transfers between devices  4.3 us (2%)
    all_to_all x8, blocking collectives, over(): return lax.all_to_all(v, axis, 0, 0, axis_index_groups=groups)  125 us
    pallas_call x13, Pallas kernels, call(): pl.pallas_call(kernel, out_shape=outs, in_specs=[VMEM] * len(ins), out_sp...  87.5 us
    all_to_all x1, starting transfers between devices, over(): return lax.all_to_all(v, axis, 0, 0, axis_index_groups=groups)  12.5 us
  transfers between devices with their start and end apart: 3, of which 1 were waited for; matrix products, arithmetic and copies ran while one was open for 0% of the time, Pallas kernels for 4%

profile of v9, /device:TPU:6, one launch (start us, length us, event | category | flops | bytes accessed | tf_op | source)
XLA Modules:
  0.0 236.2 jit_solution(3709986860438368467)
XLA Ops:
  0.6 1.0 pad_maximum_fusion.xy_ref
  1.7 11.7 %start.1 = (bf16[1024,256]{1,0:T(8,128)(2,1)S(1)}, bf16[1536,256]{1,0:T(8,128)(2,1)S(1)}, bf16[256,1024]{1,0:T(8,128)(2,1)S(1)}, bf16[256,1536]{1,0:T(8,128)(2,1...) custom-call(f32[32,2560]{1,0:T(8,128)S(1)} %pad_maximum_fusion.xy_ref), custom_call_target="tpu_custom_call" | custom-call | tf_op jit(solution)/shard_map/start/pallas_call | solution.py:446
  13.3 27.7 %all_to_all.45.p = f32[16,1,8,128]{3,2,1,0:T(8,128)S(1)} all-to-all(f32[16,1,8,128]{3,2,1,0:T(8,128)S(1)} %get-tuple-element.32), channel_id=1, replica_groups=mesh['row'=32,'col'=16] {'col'}, dimensions={0} | all-to-all | bytes 131072 | tf_op jit(solution)/shard_map/all_to_all | solution.py:475
  41.0 11.7 %cols.2 = (f32[8,128]{1,0:T(8,128)S(1)}, f32[32,3,4,128]{3,2,1,0:T(4,128)S(1)}) custom-call(f32[16,1,8,128]{3,2,1,0:T(8,128)S(1)} %all_to_all.45.p, bf16[1024,256]{1,0:T(8,128)(2,1)S(1)} %get-tuple-element.33.c.col_ref, bf16[256,1536]{1,0:T(8,128)(2,1)S(1)} %get-tuple-element.34.r.row_ref.values_ref), custom_call_target="tpu_custom_call" | custom-call | tf_op jit(solution)/shard_map/cols/pallas_call | solution.py:446
  52.8 13.9 %all_to_all.46.parts_ref = f32[32,3,4,128]{3,2,1,0:T(4,128)S(1)} all-to-all(f32[32,3,4,128]{3,2,1,0:T(4,128)S(1)} %get-tuple-element.35), channel_id=1, replica_groups=mesh['row'=32,'col'=16] {'row'}, dimensions={0} | all-to-all | bytes 393216 | tf_op jit(solution)/shard_map/all_to_all | solution.py:475
  66.7 11.4 %rows.2 = (f32[12,128]{1,0:T(8,128)S(1)}, f32[16,1,8,128]{3,2,1,0:T(8,128)S(1)}) custom-call(f32[32,3,4,128]{3,2,1,0:T(4,128)S(1)} %all_to_all.46.parts_ref, bf16[1536,256]{1,0:T(8,128)(2,1)S(1)} %get-tuple-element.36.col_ref, bf16[256,1024]{1,0:T(8,128)(2,1)S(1)} %get-tuple-element.37.row_ref.values_ref, f32[8,128]{1,0:T(8,128)S(1)} %get-tuple-element.38.old_ref), custom_call_target="tpu_custom_call" | custom-call | tf_op jit(solution)/shard_map/rows/pallas_call | solution.py:446
  78.1 15.6 %all_to_all.47.parts_ref = f32[16,1,8,128]{3,2,1,0:T(8,128)S(1)} all-to-all(f32[16,1,8,128]{3,2,1,0:T(8,128)S(1)} %get-tuple-element.39), channel_id=1, replica_groups=mesh['row'=32,'col'=16] {'col'}, dimensions={0} | all-to-all | bytes 131072 | tf_op jit(solution)/shard_map/all_to_all | solution.py:475
  93.7 11.7 %cols.3 = (f32[8,128]{1,0:T(8,128)S(1)}, f32[32,3,4,128]{3,2,1,0:T(4,128)S(1)}) custom-call(f32[16,1,8,128]{3,2,1,0:T(8,128)S(1)} %all_to_all.47.parts_ref, bf16[1024,256]{1,0:T(8,128)(2,1)S(1)} %get-tuple-element.33.c.col_ref, bf16[256,1536]{1,0:T(8,128)(2,1)S(1)} %get-tuple-element.34.r.row_ref.values_ref, f32[12,128]{1,0:T(8,128)S(1)} %get-tuple-element.40.old_ref), custom_call_target="tpu_custom_call" | custom-call | tf_op jit(solution)/shard_map/cols/pallas_call | solution.py:446
  105.4 12.0 %all_to_all.48.parts_ref = f32[32,3,4,128]{3,2,1,0:T(4,128)S(1)} all-to-all(f32[32,3,4,128]{3,2,1,0:T(4,128)S(1)} %get-tuple-element.41), channel_id=1, replica_groups=mesh['row'=32,'col'=16] {'row'}, dimensions={0} | all-to-all | bytes 393216 | tf_op jit(solution)/shard_map/all_to_all | solution.py:475
  117.3 11.4 %rows.3 = (f32[12,128]{1,0:T(8,128)S(1)}, f32[16,1,8,128]{3,2,1,0:T(8,128)S(1)}) custom-call(f32[32,3,4,128]{3,2,1,0:T(4,128)S(1)} %all_to_all.48.parts_ref, bf16[1536,256]{1,0:T(8,128)(2,1)S(1)} %get-tuple-element.36.col_ref, bf16[256,1024]{1,0:T(8,128)(2,1)S(1)} %get-tuple-element.37.row_ref.values_ref, f32[8,128]{1,0:T(8,128)S(1)} %get-tuple-element.42.old_ref), custom_call_target="tpu_custom_call" | custom-call | tf_op jit(solution)/shard_map/rows/pallas_call | solution.py:446
  128.7 15.7 %all_to_all.49.parts_ref = f32[16,1,8,128]{3,2,1,0:T(8,128)S(1)} all-to-all(f32[16,1,8,128]{3,2,1,0:T(8,128)S(1)} %get-tuple-element.43), channel_id=1, replica_groups=mesh['row'=32,'col'=16] {'col'}, dimensions={0} | all-to-all | bytes 131072 | tf_op jit(solution)/shard_map/all_to_all | solution.py:475
  144.4 17.2 %tgt_part.1 = (f32[8,128]{1,0:T(8,128)S(1)}, f32[32,6,4,128]{3,2,1,0:T(4,128)S(1)}) custom-call(f32[16,1,8,128]{3,2,1,0:T(8,128)S(1)} %all_to_all.49.parts_ref, bf16[1024,256]{1,0:T(8,128)(2,1)S(1)} %get-tuple-element.33.c.col_ref, bf16[256,1536]{1,0:T(8,128)(2,1)S(1)} %get-tuple-element.34.r.row_ref.values_ref, ...), custom_call_target="tpu_custom_call" | custom-call | tf_op jit(solution)/shard_map/tgt_part/pallas_call | solution.py:446
  161.6 13.5 %all_to_all.50.parts_ref = f32[32,6,4,128]{3,2,1,0:T(4,128)S(1)} all-to-all(f32[32,6,4,128]{3,2,1,0:T(4,128)S(1)} %get-tuple-element.45), channel_id=1, replica_groups=mesh['row'=32,'col'=16] {'row'}, dimensions={0} | all-to-all | bytes 786432 | tf_op jit(solution)/shard_map/all_to_all | solution.py:475
  175.1 2.2 src_send.1
  177.3 12.5 %all-to-all-start.6 = ((f32[32,3,4,128]{3,2,1,0:T(4,128)}), f32[32,3,4,128]{3,2,1,0:T(4,128)S(1)}, u32[]{:S(2)}, u32[]{:S(2)}) async-start(f32[32,3,4,128]{3,2,1,0:T(4,128)} %get-tuple-element.52), calls=%async_computation.6 | async-start | bytes 393216 | tf_op jit(solution)/shard_map/all_to_all | solution.py:475
  189.8 3.0 %collective-permute-start = (f32[2,17,4,128]{3,2,1,0:T(4,128)S(1)}, f32[2,17,4,128]{3,2,1,0:T(4,128)S(1)}, u32[]{:S(2)}, u32[]{:S(2)}) collective-permute-start(f32[2,17,4,128]{3,2,1,0:T(4,128)S(1)} %get-tuple-element.48), channel_id=1, source_target_pairs={{0,1},{1,0},{2,3},{3,2},{4,5},{5,4},{6,7},{7,6},{8,9},{9,8},{10,11... | collective-permute-start | bytes 208904 | tf_op jit(solution)/shard_map/ppermute | solution.py:545
  192.8 8.7 %src_keep.1.one_ref = f32[2,17,4,128]{3,2,1,0:T(4,128)S(1)} custom-call(bf16[1536,128]{1,0:T(8,128)(2,1)S(1)} %get-tuple-element.47.half_ref, bf16[1536,256]{1,0:T(8,128)(2,1)S(1)} %get-tuple-element.36.col_ref, bf16[256,1024]{1,0:T(8,128)(2,1)S(1)} %get-tuple-element.37.row_ref.values_ref, bf16[256,1536]{1,0:T(8,128)(2,1)S(1)} %get-tuple-element.34.r.row_ref.values_ref, ...), custom_call_target="tpu_custom_call" | custom-call | flops 1073741824 | bytes 2097152 | tf_op jit(solution)/shard_map/src_keep/pallas_call | solution.py:446
  201.6 0.0 collective-permute-done.other_ref
  201.6 0.1 src_join.1.one_ref
  201.7 2.5 %collective-permute-start.1 = (f32[1,17,4,128]{3,2,1,0:T(4,128)S(1)}, f32[1,17,4,128]{3,2,1,0:T(4,128)S(1)}, u32[]{:S(2)}, u32[]{:S(2)}) collective-permute-start(f32[1,17,4,128]{3,2,1,0:T(4,128)S(1)} %slice.4), channel_id=1, source_target_pairs={{0,2},{1,3},{2,0},{3,1},{4,6},{5,7},{6,4},{7,5},{8,10},{9,11},{10,... | collective-permute-start | bytes 104456 | tf_op jit(solution)/shard_map/ppermute | solution.py:556
  204.1 0.0 all-to-all-done.6.tgt_ref
  204.1 0.7 tgt_end.1
  204.9 4.3 %collective-permute-done.1.other_ref = f32[1,17,4,128]{3,2,1,0:T(4,128)S(1)} collective-permute-done((f32[1,17,4,128]{3,2,1,0:T(4,128)S(1)}, f32[1,17,4,128]{3,2,1,0:T(4,128)S(1)}, u32[]{:S(2)}, u32[]{:S(2)}) %collective-permute-start.1) | collective-permute-done | bytes 34848 | tf_op jit(solution)/shard_map/ppermute | solution.py:556
  209.2 17.4 %all_to_all.51.parts_ref = f32[4,17,4,128]{3,2,1,0:T(4,128)S(1)} all-to-all(f32[4,17,4,128]{3,2,1,0:T(4,128)S(1)} %src_join2.1), channel_id=1, replica_groups={{0,4,8,12},{1,5,9,13},{2,6,10,14},{3,7,11,15},{16,20,24,28},{17,21,25,2..., dimensions={0} | all-to-all | bytes 278528 | tf_op jit(solution)/shard_map/all_to_all | solution.py:475
  226.6 0.1 src_share.1
  226.7 8.8 %all_to_all.52.parts_ref = f32[4,16,4,128]{3,2,1,0:T(4,128)S(1)} all-to-all(f32[4,16,4,128]{3,2,1,0:T(4,128)S(1)} %src_share.1), channel_id=1, replica_groups={{0,1,2,3},{4,5,6,7},{8,9,10,11},{12,13,14,15},{16,17,18,19},{20,21,22,2..., dimensions={0} | all-to-all | bytes 262144 | tf_op jit(solution)/shard_map/all_to_all | solution.py:475
  235.5 0.7 src_end.1
  (2 shorter events, 0.1 us)
Async XLA Ops:
  177.3 26.8 %all-to-all-start.6 = ((f32[32,3,4,128]{3,2,1,0:T(4,128)}), f32[32,3,4,128]{3,2,1,0:T(4,128)S(1)}, u32[]{:S(2)}, u32[]{:S(2)}) async-start(f32[32,3,4,128]{3,2,1,0:T(4,128)} %get-tuple-element.52), calls=%async_computation.6 | async-start | bytes 393216 | tf_op jit(solution)/shard_map/all_to_all | solution.py:475
  189.8 11.7 %collective-permute-start = (f32[2,17,4,128]{3,2,1,0:T(4,128)S(1)}, f32[2,17,4,128]{3,2,1,0:T(4,128)S(1)}, u32[]{:S(2)}, u32[]{:S(2)}) collective-permute-start(f32[2,17,4,128]{3,2,1,0:T(4,128)S(1)} %get-tuple-element.48), channel_id=1, source_target_pairs={{0,1},{1,0},{2,3},{3,2},{4,5},{5,4},{6,7},{7,6},{8,9},{9,8},{10,11... | collective-permute-start | bytes 208904 | tf_op jit(solution)/shard_map/ppermute | solution.py:545
  201.7 7.5 %collective-permute-start.1 = (f32[1,17,4,128]{3,2,1,0:T(4,128)S(1)}, f32[1,17,4,128]{3,2,1,0:T(4,128)S(1)}, u32[]{:S(2)}, u32[]{:S(2)}) collective-permute-start(f32[1,17,4,128]{3,2,1,0:T(4,128)S(1)} %slice.4), channel_id=1, source_target_pairs={{0,2},{1,3},{2,0},{3,1},{4,6},{5,7},{6,4},{7,5},{8,10},{9,11},{10,... | collective-permute-start | bytes 104456 | tf_op jit(solution)/shard_map/ppermute | solution.py:556

commit v10 on v9

--- a/solution.py
+++ b/solution.py
@@ -378,10 +378,10 @@
     for c in range(blocks // each):
         logs = logs_of(c)
         weights = jnp.exp2(logs - jnp.max(logs, axis=0)[None])
-        weights = weights / jnp.sum(weights, axis=0)[None]
+        whole = 1.0 / jnp.sum(weights, axis=0)
         for u in range(each):
             at = c * each + u
-            part = jnp.sum(parts_ref[:, base + at] * weights, axis=0)
+            part = jnp.sum(parts_ref[:, base + at] * weights, axis=0) * whole
             out_ref[:, at] = jnp.broadcast_to(part[None], (n, 4, HALF))
 
 

time: 237 us -> 237 us (level)
  Pallas kernels: 87.5 us -> 59.9 us
  blocking collectives: 125 us -> 147 us
  starting transfers between devices: 18 us -> 23.6 us
    pallas_call x13, Pallas kernels: 87.5 us -> 59.9 us  [call(): pl.pallas_call(kernel, out_shape=outs, in_specs=[VMEM] * len(ins), out_sp...]
    all_to_all x8, blocking collectives: 125 us -> 147 us  [over(): return lax.all_to_all(v, axis, 0, 0, axis_index_groups=groups)]
    ppermute x1, starting transfers between devices: 2.47 us -> 8.22 us  [local(): came = lax.ppermute(parts[1:], 'col', [(i, i ^ 2) for i in range(n_col)])]
    ppermute x1, waiting for transfers between devices: 4.29 us -> 1.16 us  [local(): came = lax.ppermute(parts[1:], 'col', [(i, i ^ 2) for i in range(n_col)])]
  transfers between devices with their start and end apart: 3 -> 3, of which waited for: 1 -> 2; matrix products, arithmetic and copies ran while one was open for 0% -> 0% of each run, Pallas kernels for 4% -> 1%
where the time goes in v10:
time: 237 us; the launch traced here: 236 us
  blocking collectives  147 us (62%)
  Pallas kernels  59.9 us (25%)
  starting transfers between devices  23.6 us (10%)
  waiting for transfers between devices  2.94 us (1%)
    all_to_all x8, blocking collectives, over(): return lax.all_to_all(v, axis, 0, 0, axis_index_groups=groups)  147 us
    pallas_call x13, Pallas kernels, call(): pl.pallas_call(kernel, out_shape=outs, in_specs=[VMEM] * len(ins), out_sp...  59.9 us
    all_to_all x1, starting transfers between devices, over(): return lax.all_to_all(v, axis, 0, 0, axis_index_groups=groups)  12.2 us
    ppermute x1, starting transfers between devices, local(): came = lax.ppermute(parts[1:], 'col', [(i, i ^ 2) for i in range(n_col)])  8.22 us
  transfers between devices with their start and end apart: 3, of which 2 were waited for; matrix products, arithmetic and copies ran while one was open for 0% of the time, Pallas kernels for 1%

profile of v10, /device:TPU:6, one launch (start us, length us, event | category | flops | bytes accessed | tf_op | source)
XLA Modules:
  0.0 235.7 jit_solution(14872151755973721197)
XLA Ops:
  0.6 1.0 pad_maximum_fusion.xy_ref
  1.7 11.7 %start.1 = (bf16[1024,256]{1,0:T(8,128)(2,1)S(1)}, bf16[1536,256]{1,0:T(8,128)(2,1)S(1)}, bf16[256,1024]{1,0:T(8,128)(2,1)S(1)}, bf16[256,1536]{1,0:T(8,128)(2,1...) custom-call(f32[32,2560]{1,0:T(8,128)S(1)} %pad_maximum_fusion.xy_ref), custom_call_target="tpu_custom_call" | custom-call | tf_op jit(solution)/shard_map/start/pallas_call | solution.py:446
  13.3 27.7 %all_to_all.45.p = f32[16,1,8,128]{3,2,1,0:T(8,128)S(1)} all-to-all(f32[16,1,8,128]{3,2,1,0:T(8,128)S(1)} %get-tuple-element.32), channel_id=1, replica_groups=mesh['row'=32,'col'=16] {'col'}, dimensions={0} | all-to-all | bytes 131072 | tf_op jit(solution)/shard_map/all_to_all | solution.py:475
  41.0 11.7 %cols.2 = (f32[8,128]{1,0:T(8,128)S(1)}, f32[32,3,4,128]{3,2,1,0:T(4,128)S(1)}) custom-call(f32[16,1,8,128]{3,2,1,0:T(8,128)S(1)} %all_to_all.45.p, bf16[1024,256]{1,0:T(8,128)(2,1)S(1)} %get-tuple-element.33.c.col_ref, bf16[256,1536]{1,0:T(8,128)(2,1)S(1)} %get-tuple-element.34.r.row_ref.values_ref), custom_call_target="tpu_custom_call" | custom-call | tf_op jit(solution)/shard_map/cols/pallas_call | solution.py:446
  52.8 13.9 %all_to_all.46.parts_ref = f32[32,3,4,128]{3,2,1,0:T(4,128)S(1)} all-to-all(f32[32,3,4,128]{3,2,1,0:T(4,128)S(1)} %get-tuple-element.35), channel_id=1, replica_groups=mesh['row'=32,'col'=16] {'row'}, dimensions={0} | all-to-all | bytes 393216 | tf_op jit(solution)/shard_map/all_to_all | solution.py:475
  66.7 1.3 rows.2
  68.0 26.0 %all_to_all.47.parts_ref = f32[16,1,8,128]{3,2,1,0:T(8,128)S(1)} all-to-all(f32[16,1,8,128]{3,2,1,0:T(8,128)S(1)} %get-tuple-element.39), channel_id=1, replica_groups=mesh['row'=32,'col'=16] {'col'}, dimensions={0} | all-to-all | bytes 131072 | tf_op jit(solution)/shard_map/all_to_all | solution.py:475
  93.9 11.7 %cols.3 = (f32[8,128]{1,0:T(8,128)S(1)}, f32[32,3,4,128]{3,2,1,0:T(4,128)S(1)}) custom-call(f32[16,1,8,128]{3,2,1,0:T(8,128)S(1)} %all_to_all.47.parts_ref, bf16[1024,256]{1,0:T(8,128)(2,1)S(1)} %get-tuple-element.33.c.col_ref, bf16[256,1536]{1,0:T(8,128)(2,1)S(1)} %get-tuple-element.34.r.row_ref.values_ref, f32[12,128]{1,0:T(8,128)S(1)} %get-tuple-element.40.old_ref), custom_call_target="tpu_custom_call" | custom-call | tf_op jit(solution)/shard_map/cols/pallas_call | solution.py:446
  105.6 11.7 %all_to_all.48.parts_ref = f32[32,3,4,128]{3,2,1,0:T(4,128)S(1)} all-to-all(f32[32,3,4,128]{3,2,1,0:T(4,128)S(1)} %get-tuple-element.41), channel_id=1, replica_groups=mesh['row'=32,'col'=16] {'row'}, dimensions={0} | all-to-all | bytes 393216 | tf_op jit(solution)/shard_map/all_to_all | solution.py:475
  117.3 1.3 rows.3
  118.6 26.0 %all_to_all.49.parts_ref = f32[16,1,8,128]{3,2,1,0:T(8,128)S(1)} all-to-all(f32[16,1,8,128]{3,2,1,0:T(8,128)S(1)} %get-tuple-element.43), channel_id=1, replica_groups=mesh['row'=32,'col'=16] {'col'}, dimensions={0} | all-to-all | bytes 131072 | tf_op jit(solution)/shard_map/all_to_all | solution.py:475
  144.6 17.2 %tgt_part.1 = (f32[8,128]{1,0:T(8,128)S(1)}, f32[32,6,4,128]{3,2,1,0:T(4,128)S(1)}) custom-call(f32[16,1,8,128]{3,2,1,0:T(8,128)S(1)} %all_to_all.49.parts_ref, bf16[1024,256]{1,0:T(8,128)(2,1)S(1)} %get-tuple-element.33.c.col_ref, bf16[256,1536]{1,0:T(8,128)(2,1)S(1)} %get-tuple-element.34.r.row_ref.values_ref, ...), custom_call_target="tpu_custom_call" | custom-call | tf_op jit(solution)/shard_map/tgt_part/pallas_call | solution.py:446
  161.8 13.3 %all_to_all.50.parts_ref = f32[32,6,4,128]{3,2,1,0:T(4,128)S(1)} all-to-all(f32[32,6,4,128]{3,2,1,0:T(4,128)S(1)} %get-tuple-element.45), channel_id=1, replica_groups=mesh['row'=32,'col'=16] {'row'}, dimensions={0} | all-to-all | bytes 786432 | tf_op jit(solution)/shard_map/all_to_all | solution.py:475
  175.2 2.2 src_send.1
  177.3 12.2 %all-to-all-start.6 = ((f32[32,3,4,128]{3,2,1,0:T(4,128)}), f32[32,3,4,128]{3,2,1,0:T(4,128)S(1)}, u32[]{:S(2)}, u32[]{:S(2)}) async-start(f32[32,3,4,128]{3,2,1,0:T(4,128)} %get-tuple-element.52), calls=%async_computation.6 | async-start | bytes 393216 | tf_op jit(solution)/shard_map/all_to_all | solution.py:475
  189.6 3.1 %collective-permute-start = (f32[2,17,4,128]{3,2,1,0:T(4,128)S(1)}, f32[2,17,4,128]{3,2,1,0:T(4,128)S(1)}, u32[]{:S(2)}, u32[]{:S(2)}) collective-permute-start(f32[2,17,4,128]{3,2,1,0:T(4,128)S(1)} %get-tuple-element.48), channel_id=1, source_target_pairs={{0,1},{1,0},{2,3},{3,2},{4,5},{5,4},{6,7},{7,6},{8,9},{9,8},{10,11... | collective-permute-start | bytes 208904 | tf_op jit(solution)/shard_map/ppermute | solution.py:545
  192.7 1.3 src_keep.1.one_ref
  194.0 1.8 collective-permute-done.other_ref
  195.8 0.1 src_join.1.one_ref
  195.9 8.2 %collective-permute-start.1 = (f32[1,17,4,128]{3,2,1,0:T(4,128)S(1)}, f32[1,17,4,128]{3,2,1,0:T(4,128)S(1)}, u32[]{:S(2)}, u32[]{:S(2)}) collective-permute-start(f32[1,17,4,128]{3,2,1,0:T(4,128)S(1)} %slice.4), channel_id=1, source_target_pairs={{0,2},{1,3},{2,0},{3,1},{4,6},{5,7},{6,4},{7,5},{8,10},{9,11},{10,... | collective-permute-start | bytes 104456 | tf_op jit(solution)/shard_map/ppermute | solution.py:556
  204.1 0.0 all-to-all-done.6.tgt_ref
  204.1 0.7 tgt_end.1
  204.8 1.2 collective-permute-done.1.other_ref
  206.0 20.6 %all_to_all.51.parts_ref = f32[4,17,4,128]{3,2,1,0:T(4,128)S(1)} all-to-all(f32[4,17,4,128]{3,2,1,0:T(4,128)S(1)} %src_join2.1), channel_id=1, replica_groups={{0,4,8,12},{1,5,9,13},{2,6,10,14},{3,7,11,15},{16,20,24,28},{17,21,25,2..., dimensions={0} | all-to-all | bytes 278528 | tf_op jit(solution)/shard_map/all_to_all | solution.py:475
  226.7 8.3 %all_to_all.52.parts_ref = f32[4,16,4,128]{3,2,1,0:T(4,128)S(1)} all-to-all(f32[4,16,4,128]{3,2,1,0:T(4,128)S(1)} %src_share.1), channel_id=1, replica_groups={{0,1,2,3},{4,5,6,7},{8,9,10,11},{12,13,14,15},{16,17,18,19},{20,21,22,2..., dimensions={0} | all-to-all | bytes 262144 | tf_op jit(solution)/shard_map/all_to_all | solution.py:475
  235.0 0.7 src_end.1
  (3 shorter events, 0.1 us)
Async XLA Ops:
  177.3 26.8 %all-to-all-start.6 = ((f32[32,3,4,128]{3,2,1,0:T(4,128)}), f32[32,3,4,128]{3,2,1,0:T(4,128)S(1)}, u32[]{:S(2)}, u32[]{:S(2)}) async-start(f32[32,3,4,128]{3,2,1,0:T(4,128)} %get-tuple-element.52), calls=%async_computation.6 | async-start | bytes 393216 | tf_op jit(solution)/shard_map/all_to_all | solution.py:475
  189.6 6.2 %collective-permute-start = (f32[2,17,4,128]{3,2,1,0:T(4,128)S(1)}, f32[2,17,4,128]{3,2,1,0:T(4,128)S(1)}, u32[]{:S(2)}, u32[]{:S(2)}) collective-permute-start(f32[2,17,4,128]{3,2,1,0:T(4,128)S(1)} %get-tuple-element.48), channel_id=1, source_target_pairs={{0,1},{1,0},{2,3},{3,2},{4,5},{5,4},{6,7},{7,6},{8,9},{9,8},{10,11... | collective-permute-start | bytes 208904 | tf_op jit(solution)/shard_map/ppermute | solution.py:545
  195.9 10.1 %collective-permute-start.1 = (f32[1,17,4,128]{3,2,1,0:T(4,128)S(1)}, f32[1,17,4,128]{3,2,1,0:T(4,128)S(1)}, u32[]{:S(2)}, u32[]{:S(2)}) collective-permute-start(f32[1,17,4,128]{3,2,1,0:T(4,128)S(1)} %slice.4), channel_id=1, source_target_pairs={{0,2},{1,3},{2,0},{3,1},{4,6},{5,7},{6,4},{7,5},{8,10},{9,11},{10,... | collective-permute-start | bytes 104456 | tf_op jit(solution)/shard_map/ppermute | solution.py:556

commit v11 on v10

--- a/solution.py
+++ b/solution.py
@@ -245,7 +245,7 @@
     )
 
 
-def maps(col_ref, half_ref, row_ref, shift_ref, values_ref, moved_ref, first):
+def maps(col_ref, half_ref, row_ref, shift_ref, values_ref, moved_ref, first, beside=None):
     count, n = col_ref.shape[0], row_ref.shape[1]
     for t in range(n // TILE):
         cols = slice(t * TILE, (t + 1) * TILE)
@@ -255,6 +255,8 @@
             values = values_ref[HALF:, c * CHUNK : (c + 1) * CHUNK]
             total += weighted(scores(col_ref, half_ref, c * CHUNK, rhs), values)
         moved_ref[:, cols] = total
+        if beside and t == 0:
+            beside()
 
 
 def slow_maps(col_ref, half_ref, row_ref, shift_ref, values_ref, moved_ref, first):
@@ -316,7 +318,8 @@
 
 
 def src_part(
-    flip, half_ref, col_ref, row_ref, values_ref, e_ref, out_ref, rows_ref, shift_ref, moved_ref
+    flip, half_ref, col_ref, row_ref, values_ref, e_ref, out_ref, rows_ref, shift_ref, moved_ref,
+    beside=None,
 ):
     mine = lax.rem(lax.axis_index("col"), NEAR)
     count = rows_ref.shape[1] // 2
@@ -344,7 +347,7 @@
                     ]
 
     guarded(
-        lambda: maps(*args, values_ref, moved_ref, 0),
+        lambda: maps(*args, values_ref, moved_ref, 0, beside),
         lambda: slow_maps(*args, values_ref, moved_ref, 0),
         finish,
         moved_ref.at[0:1, :],
@@ -359,12 +362,11 @@
     new_ref, half_ref, out_ref, tgt_out,
     tgt_ref, sem, *scratch,
 ):
-    tgt_share(dims, groups, parts_ref, tgt_ref)
     copy = pltpu.make_async_copy(tgt_ref, tgt_out, sem)
-    copy.start()
     joined_rows(total, parts_ref.at[:, : new_ref.shape[0] // 4], new_ref)
     half_ref[...] = column_half(as_row(new_ref[...]), 3, col_ref)
-    src_part(1, half_ref, col_ref, row_ref, values_ref, e_ref, out_ref, *scratch)
+    tgt_share(dims, groups, parts_ref, tgt_ref)
+    src_part(1, half_ref, col_ref, row_ref, values_ref, e_ref, out_ref, *scratch, copy.start)
     copy.wait()
 
 

time: 237 us -> 237 us (level); the launches traced: 236 us -> 233 us
  Pallas kernels: 59.9 us -> 87.5 us
  blocking collectives: 147 us -> 123 us
  starting transfers between devices: 23.6 us -> 17.3 us
    pallas_call x13, Pallas kernels: 59.9 us -> 87.5 us  [call(): pl.pallas_call(kernel, out_shape=outs, in_specs=[VMEM] * len(ins), out_sp...]
    all_to_all x8, blocking collectives: 147 us -> 123 us  [over(): return lax.all_to_all(v, axis, 0, 0, axis_index_groups=groups)]
    ppermute x1, starting transfers between devices: 8.22 us -> 1.92 us  [local(): came = lax.ppermute(parts[1:], 'col', [(i, i ^ 2) for i in range(n_col)])]
    ppermute x1, waiting for transfers between devices: 1.16 us -> 4.06 us  [local(): came = lax.ppermute(parts[1:], 'col', [(i, i ^ 2) for i in range(n_col)])]
  transfers between devices with their start and end apart: 3 -> 3, of which waited for: 2 -> 1; matrix products, arithmetic and copies ran while one was open for 0% -> 0% of each run, Pallas kernels for 1% -> 4%
where the time goes in v11:
time: 237 us; the launch traced here: 233 us
  blocking collectives  123 us (52%)
  Pallas kernels  87.5 us (37%)
  starting transfers between devices  17.3 us (7%)
  waiting for transfers between devices  4.07 us (2%)
    all_to_all x8, blocking collectives, over(): return lax.all_to_all(v, axis, 0, 0, axis_index_groups=groups)  123 us
    pallas_call x13, Pallas kernels, call(): pl.pallas_call(kernel, out_shape=outs, in_specs=[VMEM] * len(ins), out_sp...  87.5 us
    all_to_all x1, starting transfers between devices, over(): return lax.all_to_all(v, axis, 0, 0, axis_index_groups=groups)  12.5 us
  transfers between devices with their start and end apart: 3, of which 1 were waited for; matrix products, arithmetic and copies ran while one was open for 0% of the time, Pallas kernels for 4%

profile of v11, /device:TPU:6, one launch (start us, length us, event | category | flops | bytes accessed | tf_op | source)
XLA Modules:
  0.0 233.3 jit_solution(14872151755973721197)
XLA Ops:
  0.6 1.0 pad_maximum_fusion.xy_ref
  1.7 11.7 %start.1 = (bf16[1024,256]{1,0:T(8,128)(2,1)S(1)}, bf16[1536,256]{1,0:T(8,128)(2,1)S(1)}, bf16[256,1024]{1,0:T(8,128)(2,1)S(1)}, bf16[256,1536]{1,0:T(8,128)(2,1...) custom-call(f32[32,2560]{1,0:T(8,128)S(1)} %pad_maximum_fusion.xy_ref), custom_call_target="tpu_custom_call" | custom-call | tf_op jit(solution)/shard_map/start/pallas_call | solution.py:448
  13.3 27.8 %all_to_all.45.p = f32[16,1,8,128]{3,2,1,0:T(8,128)S(1)} all-to-all(f32[16,1,8,128]{3,2,1,0:T(8,128)S(1)} %get-tuple-element.32), channel_id=1, replica_groups=mesh['row'=32,'col'=16] {'col'}, dimensions={0} | all-to-all | bytes 131072 | tf_op jit(solution)/shard_map/all_to_all | solution.py:477
  41.2 11.7 %cols.2 = (f32[8,128]{1,0:T(8,128)S(1)}, f32[32,3,4,128]{3,2,1,0:T(4,128)S(1)}) custom-call(f32[16,1,8,128]{3,2,1,0:T(8,128)S(1)} %all_to_all.45.p, bf16[1024,256]{1,0:T(8,128)(2,1)S(1)} %get-tuple-element.33.c.col_ref, bf16[256,1536]{1,0:T(8,128)(2,1)S(1)} %get-tuple-element.34.r.row_ref.values_ref), custom_call_target="tpu_custom_call" | custom-call | tf_op jit(solution)/shard_map/cols/pallas_call | solution.py:448
  52.9 13.7 %all_to_all.46.parts_ref = f32[32,3,4,128]{3,2,1,0:T(4,128)S(1)} all-to-all(f32[32,3,4,128]{3,2,1,0:T(4,128)S(1)} %get-tuple-element.35), channel_id=1, replica_groups=mesh['row'=32,'col'=16] {'row'}, dimensions={0} | all-to-all | bytes 393216 | tf_op jit(solution)/shard_map/all_to_all | solution.py:477
  66.7 11.4 %rows.2 = (f32[12,128]{1,0:T(8,128)S(1)}, f32[16,1,8,128]{3,2,1,0:T(8,128)S(1)}) custom-call(f32[32,3,4,128]{3,2,1,0:T(4,128)S(1)} %all_to_all.46.parts_ref, bf16[1536,256]{1,0:T(8,128)(2,1)S(1)} %get-tuple-element.36.col_ref, bf16[256,1024]{1,0:T(8,128)(2,1)S(1)} %get-tuple-element.37.row_ref.values_ref, f32[8,128]{1,0:T(8,128)S(1)} %get-tuple-element.38.old_ref), custom_call_target="tpu_custom_call" | custom-call | tf_op jit(solution)/shard_map/rows/pallas_call | solution.py:448
  78.1 16.0 %all_to_all.47.parts_ref = f32[16,1,8,128]{3,2,1,0:T(8,128)S(1)} all-to-all(f32[16,1,8,128]{3,2,1,0:T(8,128)S(1)} %get-tuple-element.39), channel_id=1, replica_groups=mesh['row'=32,'col'=16] {'col'}, dimensions={0} | all-to-all | bytes 131072 | tf_op jit(solution)/shard_map/all_to_all | solution.py:477
  94.0 11.7 %cols.3 = (f32[8,128]{1,0:T(8,128)S(1)}, f32[32,3,4,128]{3,2,1,0:T(4,128)S(1)}) custom-call(f32[16,1,8,128]{3,2,1,0:T(8,128)S(1)} %all_to_all.47.parts_ref, bf16[1024,256]{1,0:T(8,128)(2,1)S(1)} %get-tuple-element.33.c.col_ref, bf16[256,1536]{1,0:T(8,128)(2,1)S(1)} %get-tuple-element.34.r.row_ref.values_ref, f32[12,128]{1,0:T(8,128)S(1)} %get-tuple-element.40.old_ref), custom_call_target="tpu_custom_call" | custom-call | tf_op jit(solution)/shard_map/cols/pallas_call | solution.py:448
  105.7 11.5 %all_to_all.48.parts_ref = f32[32,3,4,128]{3,2,1,0:T(4,128)S(1)} all-to-all(f32[32,3,4,128]{3,2,1,0:T(4,128)S(1)} %get-tuple-element.41), channel_id=1, replica_groups=mesh['row'=32,'col'=16] {'row'}, dimensions={0} | all-to-all | bytes 393216 | tf_op jit(solution)/shard_map/all_to_all | solution.py:477
  117.2 11.4 %rows.3 = (f32[12,128]{1,0:T(8,128)S(1)}, f32[16,1,8,128]{3,2,1,0:T(8,128)S(1)}) custom-call(f32[32,3,4,128]{3,2,1,0:T(4,128)S(1)} %all_to_all.48.parts_ref, bf16[1536,256]{1,0:T(8,128)(2,1)S(1)} %get-tuple-element.36.col_ref, bf16[256,1024]{1,0:T(8,128)(2,1)S(1)} %get-tuple-element.37.row_ref.values_ref, f32[8,128]{1,0:T(8,128)S(1)} %get-tuple-element.42.old_ref), custom_call_target="tpu_custom_call" | custom-call | tf_op jit(solution)/shard_map/rows/pallas_call | solution.py:448
  128.6 15.9 %all_to_all.49.parts_ref = f32[16,1,8,128]{3,2,1,0:T(8,128)S(1)} all-to-all(f32[16,1,8,128]{3,2,1,0:T(8,128)S(1)} %get-tuple-element.43), channel_id=1, replica_groups=mesh['row'=32,'col'=16] {'col'}, dimensions={0} | all-to-all | bytes 131072 | tf_op jit(solution)/shard_map/all_to_all | solution.py:477
  144.6 17.2 %tgt_part.1 = (f32[8,128]{1,0:T(8,128)S(1)}, f32[32,6,4,128]{3,2,1,0:T(4,128)S(1)}) custom-call(f32[16,1,8,128]{3,2,1,0:T(8,128)S(1)} %all_to_all.49.parts_ref, bf16[1024,256]{1,0:T(8,128)(2,1)S(1)} %get-tuple-element.33.c.col_ref, bf16[256,1536]{1,0:T(8,128)(2,1)S(1)} %get-tuple-element.34.r.row_ref.values_ref, ...), custom_call_target="tpu_custom_call" | custom-call | tf_op jit(solution)/shard_map/tgt_part/pallas_call | solution.py:448
  161.8 13.3 %all_to_all.50.parts_ref = f32[32,6,4,128]{3,2,1,0:T(4,128)S(1)} all-to-all(f32[32,6,4,128]{3,2,1,0:T(4,128)S(1)} %get-tuple-element.45), channel_id=1, replica_groups=mesh['row'=32,'col'=16] {'row'}, dimensions={0} | all-to-all | bytes 786432 | tf_op jit(solution)/shard_map/all_to_all | solution.py:477
  175.0 2.2 src_send.1
  177.2 12.5 %all-to-all-start.6 = ((f32[32,3,4,128]{3,2,1,0:T(4,128)}), f32[32,3,4,128]{3,2,1,0:T(4,128)S(1)}, u32[]{:S(2)}, u32[]{:S(2)}) async-start(f32[32,3,4,128]{3,2,1,0:T(4,128)} %get-tuple-element.52), calls=%async_computation.6 | async-start | bytes 393216 | tf_op jit(solution)/shard_map/all_to_all | solution.py:477
  189.7 2.9 %collective-permute-start = (f32[2,17,4,128]{3,2,1,0:T(4,128)S(1)}, f32[2,17,4,128]{3,2,1,0:T(4,128)S(1)}, u32[]{:S(2)}, u32[]{:S(2)}) collective-permute-start(f32[2,17,4,128]{3,2,1,0:T(4,128)S(1)} %get-tuple-element.48), channel_id=1, source_target_pairs={{0,1},{1,0},{2,3},{3,2},{4,5},{5,4},{6,7},{7,6},{8,9},{9,8},{10,11... | collective-permute-start | bytes 208904 | tf_op jit(solution)/shard_map/ppermute | solution.py:547
  192.6 8.7 %src_keep.1.one_ref = f32[2,17,4,128]{3,2,1,0:T(4,128)S(1)} custom-call(bf16[1536,128]{1,0:T(8,128)(2,1)S(1)} %get-tuple-element.47.half_ref, bf16[1536,256]{1,0:T(8,128)(2,1)S(1)} %get-tuple-element.36.col_ref, bf16[256,1024]{1,0:T(8,128)(2,1)S(1)} %get-tuple-element.37.row_ref.values_ref, bf16[256,1536]{1,0:T(8,128)(2,1)S(1)} %get-tuple-element.34.r.row_ref.values_ref, ...), custom_call_target="tpu_custom_call" | custom-call | flops 1073741824 | bytes 2097152 | tf_op jit(solution)/shard_map/src_keep/pallas_call | solution.py:448
  201.4 0.0 collective-permute-done.other_ref
  201.4 0.1 src_join.1.one_ref
  201.5 1.9 collective-permute-start.1
  203.4 0.0 all-to-all-done.6.tgt_ref
  203.4 0.7 tgt_end.1
  204.1 4.1 %collective-permute-done.1.other_ref = f32[1,17,4,128]{3,2,1,0:T(4,128)S(1)} collective-permute-done((f32[1,17,4,128]{3,2,1,0:T(4,128)S(1)}, f32[1,17,4,128]{3,2,1,0:T(4,128)S(1)}, u32[]{:S(2)}, u32[]{:S(2)}) %collective-permute-start.1) | collective-permute-done | bytes 34848 | tf_op jit(solution)/shard_map/ppermute | solution.py:558
  208.2 16.0 %all_to_all.51.parts_ref = f32[4,17,4,128]{3,2,1,0:T(4,128)S(1)} all-to-all(f32[4,17,4,128]{3,2,1,0:T(4,128)S(1)} %src_join2.1), channel_id=1, replica_groups={{0,4,8,12},{1,5,9,13},{2,6,10,14},{3,7,11,15},{16,20,24,28},{17,21,25,2..., dimensions={0} | all-to-all | bytes 278528 | tf_op jit(solution)/shard_map/all_to_all | solution.py:477
  224.3 8.3 %all_to_all.52.parts_ref = f32[4,16,4,128]{3,2,1,0:T(4,128)S(1)} all-to-all(f32[4,16,4,128]{3,2,1,0:T(4,128)S(1)} %src_share.1), channel_id=1, replica_groups={{0,1,2,3},{4,5,6,7},{8,9,10,11},{12,13,14,15},{16,17,18,19},{20,21,22,2..., dimensions={0} | all-to-all | bytes 262144 | tf_op jit(solution)/shard_map/all_to_all | solution.py:477
  232.6 0.7 src_end.1
  (3 shorter events, 0.1 us)
Async XLA Ops:
  177.2 26.1 %all-to-all-start.6 = ((f32[32,3,4,128]{3,2,1,0:T(4,128)}), f32[32,3,4,128]{3,2,1,0:T(4,128)S(1)}, u32[]{:S(2)}, u32[]{:S(2)}) async-start(f32[32,3,4,128]{3,2,1,0:T(4,128)} %get-tuple-element.52), calls=%async_computation.6 | async-start | bytes 393216 | tf_op jit(solution)/shard_map/all_to_all | solution.py:477
  189.7 11.6 %collective-permute-start = (f32[2,17,4,128]{3,2,1,0:T(4,128)S(1)}, f32[2,17,4,128]{3,2,1,0:T(4,128)S(1)}, u32[]{:S(2)}, u32[]{:S(2)}) collective-permute-start(f32[2,17,4,128]{3,2,1,0:T(4,128)S(1)} %get-tuple-element.48), channel_id=1, source_target_pairs={{0,1},{1,0},{2,3},{3,2},{4,5},{5,4},{6,7},{7,6},{8,9},{9,8},{10,11... | collective-permute-start | bytes 208904 | tf_op jit(solution)/shard_map/ppermute | solution.py:547
  201.5 6.7 %collective-permute-start.1 = (f32[1,17,4,128]{3,2,1,0:T(4,128)S(1)}, f32[1,17,4,128]{3,2,1,0:T(4,128)S(1)}, u32[]{:S(2)}, u32[]{:S(2)}) collective-permute-start(f32[1,17,4,128]{3,2,1,0:T(4,128)S(1)} %slice.4), channel_id=1, source_target_pairs={{0,2},{1,3},{2,0},{3,1},{4,6},{5,7},{6,4},{7,5},{8,10},{9,11},{10,... | collective-permute-start | bytes 104456 | tf_op jit(solution)/shard_map/ppermute | solution.py:558
